TPU v7x, 32 devices: a whole 2x2x4 slice. The times are simulated.
32 devices in a mesh: box: 4 (over z), dir: 8 (over y, x, core).
Axes of the slice: x: 2, y: 2, z: 4, core: 2. Of those that a mesh axis runs over, the one named last changes fastest.
Arguments:
- leaf_out: bfloat16 [2, 2048, 1024], P(None, ('box', 'dir')), may hold values from -6 to 6
- interp_mid: bfloat16 [1024, 4096], replicated, may hold values from -0.1875 to 0.1875
- shift_mid: float32 [8, 4096], replicated, may hold values from -3.140625 to 3.140625
- trans_mid: float32 [2, 316, 4096], P(None, None, 'dir'), may hold values from -0.5 to 0.5
- list_mid: int32 [256, 64], replicated, may hold values from 0 to 255
- offset_mid: int32 [256, 64], replicated, may hold values from 0 to 315
- interp_top: bfloat16 [8, 512, 2048], P('dir'), may hold values from -0.25 to 0.25
- shift_top: float32 [8, 8, 2048], P(None, 'dir'), may hold values from -3.140625 to 3.140625
- trans_top: float32 [2, 316, 8, 2048], P(None, None, 'dir', 'box'), may hold values from -0.5 to 0.5
- list_top: int32 [32, 64], replicated, may hold values from 0 to 31
- offset_top: int32 [32, 64], replicated, may hold values from 0 to 315
Outputs:
- leaf_in: float32 [2, 2048, 1024], P(None, ('box', 'dir'))
Inputs may be any that keep to these rules, and one draw needn't show every extreme that they name: `list_mid`: middle box indices. `offset_mid`: offset indices. `list_top`: top box indices. `offset_top`: offset indices.
All inputs are finite; a program needn't handle non-finite values.
Results may differ from a plain program's by a relative error of at most 0.014.
Values may be sent and summed in bfloat16 or wider, within the bound.
No kernel may reach another device: no remote copies, remote signals or barrier semaphores. Data moves between devices by JAX's collectives and lax.ppermute only.
A program may use at most 64 MiB of HBM per device.

v0:
```python
import math

import jax
import jax.numpy as jnp
from jax import lax
from jax.sharding import PartitionSpec as P


def complex_translate(patterns, sources, offsets, operators):
    row_count = sources.shape[0]
    list_width = sources.shape[1]
    block_rows = math.gcd(row_count, 32)
    source_count = patterns.shape[1]
    offset_count = operators.shape[1]
    width = patterns.shape[2]
    source_blocks = sources.reshape(row_count // block_rows, block_rows * list_width)
    offset_blocks = offsets.reshape(row_count // block_rows, block_rows * list_width)

    def one_block(indices):
        source_hot = (indices[0][:, None] == lax.iota(jnp.int32, source_count)[None, :]).astype(
            jnp.bfloat16
        )
        offset_hot = (indices[1][:, None] == lax.iota(jnp.int32, offset_count)[None, :]).astype(
            jnp.float32
        )
        picked = jnp.einsum("rn,cnk->crk", source_hot, patterns, preferred_element_type=jnp.float32)
        factors = jnp.einsum("ro,cok->crk", offset_hot, operators, precision=lax.Precision.HIGHEST)
        picked = picked.reshape(2, block_rows, list_width, width)
        factors = factors.reshape(2, block_rows, list_width, width)
        real_part = jnp.sum(picked[0] * factors[0] - picked[1] * factors[1], axis=1)
        imag_part = jnp.sum(picked[0] * factors[1] + picked[1] * factors[0], axis=1)
        return jnp.stack([real_part, imag_part])

    blocks = lax.map(one_block, (source_blocks, offset_blocks))
    return jnp.transpose(blocks, (1, 0, 2, 3)).reshape(2, row_count, width)


def interpolate_shift(leaves_part, matrix, cos_table, sin_table):
    row_count = leaves_part.shape[1]
    real_part = jnp.dot(leaves_part[0], matrix, preferred_element_type=jnp.float32)
    imag_part = jnp.dot(leaves_part[1], matrix, preferred_element_type=jnp.float32)
    octant = lax.iota(jnp.int32, row_count) % 8
    selector = (octant[:, None] == lax.iota(jnp.int32, 8)[None, :]).astype(jnp.float32)
    cos_rows = jnp.dot(selector, cos_table, precision=lax.Precision.HIGHEST)
    sin_rows = jnp.dot(selector, sin_table, precision=lax.Precision.HIGHEST)
    return jnp.stack(
        [real_part * cos_rows - imag_part * sin_rows, real_part * sin_rows + imag_part * cos_rows]
    )


def sum_children(values):
    return jnp.sum(values.reshape(2, values.shape[1] // 8, 8, values.shape[2]), axis=2)


def child_shift(parents, cos_table, sin_table):
    real_part = parents[0].astype(jnp.float32)[:, None, :]
    imag_part = parents[1].astype(jnp.float32)[:, None, :]
    new_real = real_part * cos_table[None] + imag_part * sin_table[None]
    new_imag = imag_part * cos_table[None] - real_part * sin_table[None]
    return jnp.stack([new_real, new_imag]).reshape(2, -1, cos_table.shape[1]).astype(jnp.bfloat16)


def adjoint_apply(children, matrix):
    dims = (((1,), (1,)), ((), ()))
    real_part = lax.dot_general(children[0], matrix, dims, preferred_element_type=jnp.float32)
    imag_part = lax.dot_general(children[1], matrix, dims, preferred_element_type=jnp.float32)
    return jnp.stack([real_part, imag_part])


def on_device(
    leaf_out,
    interp_mid,
    shift_mid,
    trans_mid,
    list_mid,
    offset_mid,
    interp_top,
    shift_top,
    trans_top,
    list_top,
    offset_top,
):
    box_index = lax.axis_index("box")
    sector = trans_mid.shape[2]
    top_width = trans_top.shape[3]
    cos_mid = jnp.cos(shift_mid)
    sin_mid = jnp.sin(shift_mid)
    shifted = interpolate_shift(leaf_out, interp_mid, cos_mid, sin_mid)
    own_parents = sum_children(shifted).astype(jnp.bfloat16)
    mid_pattern = lax.all_to_all(own_parents, "dir", split_axis=2, concat_axis=1, tiled=True)
    mid_group = mid_pattern.shape[1]
    mid_all = lax.all_gather(mid_pattern, "box", axis=1, tiled=True)
    own_list = lax.dynamic_slice_in_dim(list_mid, box_index * mid_group, mid_group, 0)
    own_offsets = lax.dynamic_slice_in_dim(offset_mid, box_index * mid_group, mid_group, 0)
    mid_far = complex_translate(mid_all, own_list, own_offsets, trans_mid)
    table_top = interp_top[0]
    cos_top = jnp.cos(shift_top[:, 0, :])
    sin_top = jnp.sin(shift_top[:, 0, :])
    scale_top = sector / table_top.shape[1]
    columns_top = lax.dynamic_slice_in_dim(table_top, box_index * top_width, top_width, 1)
    cos_owned = lax.dynamic_slice_in_dim(cos_top, box_index * top_width, top_width, 1)
    sin_owned = lax.dynamic_slice_in_dim(sin_top, box_index * top_width, top_width, 1)
    top_pattern = sum_children(
        interpolate_shift(mid_all, columns_top, cos_owned, sin_owned)
    ).astype(jnp.bfloat16)
    top_in = complex_translate(top_pattern, list_top, offset_top, trans_top[:, :, 0, :]).astype(
        jnp.bfloat16
    )
    children = child_shift(top_in, cos_owned, sin_owned)
    partial_terms = adjoint_apply(children, columns_top)
    down_top = lax.psum_scatter(
        partial_terms.astype(jnp.bfloat16), "box", scatter_dimension=1, tiled=True
    ).astype(jnp.float32)
    mid_in = (mid_far + scale_top * down_top).astype(jnp.bfloat16)
    parents = lax.all_to_all(mid_in, "dir", split_axis=1, concat_axis=2, tiled=True)
    leaf_children = child_shift(parents, cos_mid, sin_mid)
    scale_leaf = interp_mid.shape[0] / interp_mid.shape[1]
    return scale_leaf * adjoint_apply(leaf_children, interp_mid)


def solution(mesh):
    return jax.shard_map(
        on_device,
        mesh=mesh,
        in_specs=(
            P(None, ("box", "dir"), None),
            P(),
            P(),
            P(None, None, "dir"),
            P(),
            P(),
            P("dir", None, None),
            P(None, "dir", None),
            P(None, None, "dir", "box"),
            P(),
            P(),
        ),
        out_specs=P(None, ("box", "dir"), None),
        check_vma=False,
    )
```

profile of v0, /device:TPU:0, one launch (start us, length us, event | category | flops | bytes accessed | tf_op | source)
XLA Modules:
  0.0 179.8 jit_solution(16214106124689342426)
XLA Ops:
  6.5 5.2 %fusion.51 = f32[64,4096]{1,0:T(8,128)S(1)} fusion(bf16[1024,4096]{1,0:T(8,128)(2,1)} %param.14, bf16[2,64,1024]{2,1,0:T(8,128)(2,1)} %param.13), kind=kOutput, calls=%fused_computation.77 | convolution fusion | flops 536870912 | bytes 9568256 | tf_op jit(solution)/shard_map/dot_general | solution.py:41
  16.7 3.8 %copy.44 = bf16[2,8,4096]{1,0,2:T(2,128)(2,1)} copy(bf16[2,8,4096]{2,1,0:T(8,128)(2,1)S(1)} %maximum_reduce_fusion) | data formatting | bytes 262144 | tf_op jit(solution)/shard_map/convert_element_type | solution.py:89
  20.5 4.0 %reshape.342 = bf16[8,2,4096]{2,1,0:T(2,128)(2,1)} reshape(bf16[4096,2,8]{2,1,0:T(2,128)(2,1)} %bitcast.156) | data formatting | bytes 262144
  24.5 5.2 %all-to-all-start = ((bf16[8,2,4096]{2,1,0:T(2,128)(2,1)}), bf16[8,2,4096]{2,1,0:T(2,128)(2,1)}, u32[]{:S(2)}, u32[]{:S(2)}) async-start(bf16[8,2,4096]{2,1,0:T(2,128)(2,1)} %reshape.342), calls=%async_computation | async-start | bytes 262144 | tf_op jit(solution)/shard_map/all_to_all | solution.py:90
  37.1 10.2 %convolution_bitcast_fusion.2 = f32[2,2048,512]{1,2,0:T(8,128)} fusion(f32[2,316,1,512]{3,2,1,0:T(1,128)} %param.21, s32[2048]{0:T(1024)} %eq.126), kind=kOutput, calls=%fused_computation.14 | convolution fusion | flops 7953047552 | bytes 9691136 | tf_op jit(solution)/shard_map/while/body/eval_jaxpr/ro,cok->crk/dot_general | solution.py:27
  49.2 4.2 %reshape.343 = bf16[4096,2,8]{2,1,0:T(2,128)(2,1)} reshape(bf16[8,2,4096]{2,1,0:T(2,128)(2,1)} %all-to-all-done) | data formatting | bytes 262144
  53.4 5.6 %copy.45 = bf16[2,8,8,512]{3,2,1,0:T(8,128)(2,1)} copy(bf16[2,8,8,512]{2,0,3,1:T(2,128)(2,1)} %bitcast.157) | data formatting | bytes 262144 | tf_op jit(solution)/shard_map/all_to_all | solution.py:90
  59.0 16.8 %all_gather.3 = bf16[2,256,512]{2,1,0:T(8,128)(2,1)S(1)} all-gather(bf16[2,64,512]{2,1,0:T(8,128)(2,1)} %bitcast.166), channel_id=1, replica_groups=mesh['box'=4,'dir'=8] {'box'}, dimensions={1}, use_global_device_ids=true | all-gather | bytes 655360 | tf_op jit(solution)/shard_map/all_gather | solution.py:92
  81.0 4.1 %multiply_subtract_fusion.1 = (f32[1,2048,512]{1,2,0:T(8,128)}, f32[1,2048,512]{1,2,0:T(8,128)}) fusion(f32[2,2048,512]{1,2,0:T(8,128)S(1)} %bitcast.153, f32[2,2048,512]{1,2,0:T(8,128)S(1)} %convolution_bitcast_fusion.3), kind=kLoop, calls=%fused_computation.17 | loop fusion | flops 6291456 | bytes 25165824 | tf_op jit(solution)/shard_map/while/body/eval_jaxpr/sub | solution.py:30
  85.1 5.4 %copy.51 = f32[1,2048,512]{2,1,0:T(8,128)} copy(f32[1,2048,512]{1,2,0:T(8,128)} %get-tuple-element.103) | data formatting | bytes 8388608 | tf_op jit(solution)/shard_map/while/body/eval_jaxpr/add | solution.py:31
  90.5 3.4 %reduce_sum.59 = bf16[32,512]{1,0:T(8,128)(2,1)} reduce(f32[32,64,512]{2,1,0:T(8,128)} %bitcast.154, f32[]{:T(128)} %constant.63.clone.1), dimensions={1}, to_apply=%region_7.8 | reduce | flops 1032192 | bytes 4227076 | tf_op jit(solution)/shard_map/while/body/eval_jaxpr/reduce_sum | solution.py:31
  95.2 5.4 %copy.50 = f32[1,2048,512]{2,1,0:T(8,128)} copy(f32[1,2048,512]{1,2,0:T(8,128)} %get-tuple-element.102) | data formatting | bytes 8388608 | tf_op jit(solution)/shard_map/while/body/eval_jaxpr/sub | solution.py:30
  100.6 3.4 %reduce_sum.58 = bf16[32,512]{1,0:T(8,128)(2,1)} reduce(f32[32,64,512]{2,1,0:T(8,128)} %bitcast.155, f32[]{:T(128)} %constant.63.clone.1), dimensions={1}, to_apply=%region_6.7 | reduce | flops 1032192 | bytes 4227076 | tf_op jit(solution)/shard_map/while/body/eval_jaxpr/reduce_sum | solution.py:30
  108.1 40.1 %while.2 = (s32[]{:T(128)}, f32[2,2,32,512]{3,2,1,0:T(8,128)}, s32[2,2048]{1,0:T(2,128)S(1)}, bf16[2,256,512]{2,1,0:T(8,128)(2,1)}, s32[2,2048]{1,0:T(2,128)}, /...) while((s32[]{:T(128)}, f32[2,2,32,512]{3,2,1,0:T(8,128)}, s32[2,2048]{1,0:T(2,128)S(1)}, ...), condition=%wide.region_4.5_spmd, body=%wide.region_1.4_spmd.sunk | while | flops 9035702272 | bytes 56787136 | solution.py:34
  109.1 7.2 %convolution_bitcast_fusion.8 = f32[2,2048,512]{2,1,0:T(8,128)S(1)} fusion(f32[2,316,512]{2,1,0:T(8,128)S(1)} %get-tuple-element.184, s32[2048]{0:T(1024)S(1)} %bitcast.165), kind=kOutput, calls=%fused_computation.clone.1 | convolution fusion | flops 7953047552 | bytes 9691136 | tf_op jit(solution)/shard_map/while/body/eval_jaxpr/ro,cok->crk/dot_general | solution.py:27
  117.6 4.3 %multiply_subtract_fusion.3 = (f32[1,2048,512]{2,1,0:T(8,128)}, f32[1,2048,512]{2,1,0:T(8,128)}) fusion(f32[2,2048,512]{2,1,0:T(8,128)S(1)} %convolution_bitcast_fusion.8, f32[2,2048,512]{2,1,0:T(8,128)S(1)} %convolution_bitcast_fusion.9), kind=kLoop, calls=%fused_computation.3.clone.1 | loop fusion | flops 6291456 | bytes 25165824 | tf_op jit(solution)/shard_map/while/body/eval_jaxpr/sub | solution.py:30
  121.9 2.9 %reduce_sum.64 = f32[32,512]{1,0:T(8,128)S(1)} reduce(f32[32,64,512]{2,1,0:T(8,128)} %bitcast.151, f32[]{:T(128)} %constant.63.clone.1..sunk), dimensions={1}, to_apply=%region_3.3 | reduce | flops 1032192 | bytes 4259844 | tf_op jit(solution)/shard_map/while/body/eval_jaxpr/reduce_sum | solution.py:31
  124.7 2.8 %reduce_sum.65 = f32[32,512]{1,0:T(8,128)S(1)} reduce(f32[32,64,512]{2,1,0:T(8,128)} %bitcast.150, f32[]{:T(128)} %constant.63.clone.1..sunk), dimensions={1}, to_apply=%region_2.2 | reduce | flops 1032192 | bytes 4259844 | tf_op jit(solution)/shard_map/while/body/eval_jaxpr/reduce_sum | solution.py:30
  129.0 7.2 %convolution_bitcast_fusion.8 = f32[2,2048,512]{2,1,0:T(8,128)S(1)} fusion(f32[2,316,512]{2,1,0:T(8,128)S(1)} %get-tuple-element.184, s32[2048]{0:T(1024)S(1)} %bitcast.165), kind=kOutput, calls=%fused_computation.clone.1 | convolution fusion | flops 7953047552 | bytes 9691136 | tf_op jit(solution)/shard_map/while/body/eval_jaxpr/ro,cok->crk/dot_general | solution.py:27
  137.5 4.3 %multiply_subtract_fusion.3 = (f32[1,2048,512]{2,1,0:T(8,128)}, f32[1,2048,512]{2,1,0:T(8,128)}) fusion(f32[2,2048,512]{2,1,0:T(8,128)S(1)} %convolution_bitcast_fusion.8, f32[2,2048,512]{2,1,0:T(8,128)S(1)} %convolution_bitcast_fusion.9), kind=kLoop, calls=%fused_computation.3.clone.1 | loop fusion | flops 6291456 | bytes 25165824 | tf_op jit(solution)/shard_map/while/body/eval_jaxpr/sub | solution.py:30
  141.8 2.8 %reduce_sum.64 = f32[32,512]{1,0:T(8,128)S(1)} reduce(f32[32,64,512]{2,1,0:T(8,128)} %bitcast.151, f32[]{:T(128)} %constant.63.clone.1..sunk), dimensions={1}, to_apply=%region_3.3 | reduce | flops 1032192 | bytes 4259844 | tf_op jit(solution)/shard_map/while/body/eval_jaxpr/reduce_sum | solution.py:31
  150.3 9.2 %all_to_all.33 = bf16[2,64,512]{2,0,1:T(2,128)(2,1)S(1)} all-to-all(bf16[2,64,512]{2,0,1:T(2,128)(2,1)S(1)} %copy.52), channel_id=1, replica_groups=mesh['box'=4,'dir'=8] {'dir'}, dimensions={1} | all-to-all | bytes 262144 | tf_op jit(solution)/shard_map/all_to_all | solution.py:115
  159.8 6.3 %convolution_bitcast_fusion.4 = f32[1,64,1024]{2,1,0:T(8,128)S(1)} fusion(bf16[1024,4096]{1,0:T(8,128)(2,1)} %param.14, f32[8,4096]{1,0:T(8,128)} %copy-done.5, f32[8,4096]{1,0:T(8,128)S(1)} %bitcast.160, f32[8,4096]{1,0:T(8,128)S(1)} %get-tuple-element.110, f32[8,4096]{1,0:T(8,128)S(1)} %bitcast.162), kind=kOutput, calls=%fused_computation.28 | convolution fusion | flops 537919488 | bytes 9175040 | tf_op jit(solution)/shard_map/dot_general | solution.py:66
  166.1 6.0 %convolution_bitcast_fusion.5 = f32[1,64,1024]{2,1,0:T(8,128)S(1)} fusion(bf16[1024,4096]{1,0:T(8,128)(2,1)} %param.14, f32[8,4096]{1,0:T(8,128)S(1)} %copy-done.6, f32[8,4096]{1,0:T(8,128)S(1)} %bitcast.161, f32[8,4096]{1,0:T(8,128)S(1)} %get-tuple-element.110, f32[8,4096]{1,0:T(8,128)S(1)} %bitcast.163), kind=kOutput, calls=%fused_computation.29 | convolution fusion | flops 537919488 | bytes 9175040 | tf_op jit(solution)/shard_map/dot_general | solution.py:65
  (91 shorter events, 36.1 us)
Async XLA Ops:
  6.5 69.3 %copy-start = (bf16[1,512,2048]{2,1,0:T(8,128)(2,1)S(1)}, bf16[1,512,2048]{2,1,0:T(8,128)(2,1)}, u32[]{:S(2)}) copy-start(bf16[1,512,2048]{2,1,0:T(8,128)(2,1)} %param.19) | copy-start | bytes 6291460
  6.5 6.0 %copy-start.2 = (bf16[1024,4096]{1,0:T(8,128)(2,1)S(1)}, bf16[1024,4096]{1,0:T(8,128)(2,1)}, u32[]{:S(2)}) copy-start(bf16[1024,4096]{1,0:T(8,128)(2,1)} %param.14) | copy-start | bytes 25165828
  6.5 6.0 %copy-start.7 = (bf16[2,64,1024]{2,1,0:T(8,128)(2,1)S(1)}, bf16[2,64,1024]{2,1,0:T(8,128)(2,1)}, u32[]{:S(2)}) copy-start(bf16[2,64,1024]{2,1,0:T(8,128)(2,1)} %param.13) | copy-start | bytes 786436
  12.5 1.6 copy-start.11
  14.6 2.1 %copy-start.5 = (f32[8,4096]{1,0:T(8,128)}, f32[8,4096]{1,0:T(8,128)S(1)}, u32[]{:S(2)}) copy-start(f32[8,4096]{1,0:T(8,128)S(1)} %get-tuple-element.111) | copy-start | bytes 393220
  16.1 14.4 %copy-start.13 = (s32[256,64]{0,1:T(8,128)S(1)}, s32[256,64]{0,1:T(8,128)}, u32[]{:S(2)}) copy-start(s32[256,64]{0,1:T(8,128)} %param.18) | copy-start | bytes 196612
  16.1 14.4 %copy-start.14 = (s32[256,64]{0,1:T(8,128)S(1)}, s32[256,64]{0,1:T(8,128)}, u32[]{:S(2)}) copy-start(s32[256,64]{0,1:T(8,128)} %param.17) | copy-start | bytes 196612
  24.5 24.6 %all-to-all-start = ((bf16[8,2,4096]{2,1,0:T(2,128)(2,1)}), bf16[8,2,4096]{2,1,0:T(2,128)(2,1)}, u32[]{:S(2)}, u32[]{:S(2)}) async-start(bf16[8,2,4096]{2,1,0:T(2,128)(2,1)} %reshape.342), calls=%async_computation | async-start | bytes 262144 | tf_op jit(solution)/shard_map/all_to_all | solution.py:90
  29.7 119.5 %reduce-scatter.2.cloned.1.call-start = ((), (), s32[]{:S(2)}) async-start(), calls=%async_computation.3 | async-start | bytes 655360 | tf_op jit(solution)/shard_map/reduce_scatter | solution.py:111
  37.1 11.5 %copy-start.10 = (f32[8,1,512]{2,1,0:T(1,128)}, f32[8,1,512]{2,1,0:T(1,128)S(1)}, u32[]{:S(2)}) copy-start(f32[8,1,512]{2,1,0:T(1,128)S(1)} %get-tuple-element.112) | copy-start | bytes 49156
  37.1 10.2 %copy-start.15 = (s32[256]{0:T(256)S(1)}, s32[256]{0:T(256)}, u32[]{:S(2)}) copy-start(s32[256]{0:T(256)} %and_select_fusion) | copy-start | bytes 3076
  59.0 19.8 %copy-start.12 = (s32[2048]{0:T(1024)S(1)}, s32[2048]{0:T(1024)}, u32[]{:S(2)}) copy-start(s32[2048]{0:T(1024)} %eq.122) | copy-start | bytes 24580
  59.0 21.1 %slice-start = ((s8[8388608]{0:T(1024)(128)(4,1)}), s8[4194304]{0:T(1024)(128)(4,1)S(1)}, s32[]{:S(2)}) async-start(s8[8388608]{0:T(1024)(128)(4,1)} %bitcast.152), calls=%async_computation.4 | async-start | bytes 8388608
  75.8 0.8 copy-start.3
  78.8 2.2 %slice-start.1 = ((s8[8388608]{0:T(1024)(128)(4,1)}), s8[4194304]{0:T(1024)(128)(4,1)S(1)}, s32[]{:S(2)}) async-start(s8[8388608]{0:T(1024)(128)(4,1)} %bitcast.152), calls=%async_computation.5 | async-start | bytes 8388608
  109.0 7.2 %copy-start.4 = (bf16[2,256,512]{2,1,0:T(8,128)(2,1)S(1)}, bf16[2,256,512]{2,1,0:T(8,128)(2,1)}, u32[]{:S(2)}) copy-start(bf16[2,256,512]{2,1,0:T(8,128)(2,1)} %get-tuple-element.182) | copy-start | bytes 1572868 | tf_op jit(solution)/shard_map/while
  121.9 5.7 %copy-start.8 = (f32[2,2,32,512]{3,2,1,0:T(8,128)S(1)}, f32[2,2,32,512]{3,2,1,0:T(8,128)}, u32[]{:S(2)}) copy-start(f32[2,2,32,512]{3,2,1,0:T(8,128)} %get-tuple-element.172) | copy-start | bytes 786436 | tf_op jit(solution)/shard_map/while
  127.6 0.7 copy-start.9
  129.0 7.2 %copy-start.4 = (bf16[2,256,512]{2,1,0:T(8,128)(2,1)S(1)}, bf16[2,256,512]{2,1,0:T(8,128)(2,1)}, u32[]{:S(2)}) copy-start(bf16[2,256,512]{2,1,0:T(8,128)(2,1)} %get-tuple-element.182) | copy-start | bytes 1572868 | tf_op jit(solution)/shard_map/while
  141.8 5.6 %copy-start.8 = (f32[2,2,32,512]{3,2,1,0:T(8,128)S(1)}, f32[2,2,32,512]{3,2,1,0:T(8,128)}, u32[]{:S(2)}) copy-start(f32[2,2,32,512]{3,2,1,0:T(8,128)} %get-tuple-element.172) | copy-start | bytes 786436 | tf_op jit(solution)/shard_map/while
  147.5 0.7 copy-start.9
  159.8 6.3 %copy-start.6 = (f32[8,4096]{1,0:T(8,128)S(1)}, f32[8,4096]{1,0:T(8,128)}, u32[]{:S(2)}) copy-start(f32[8,4096]{1,0:T(8,128)} %copy-done.5) | copy-start | bytes 393220
  159.8 13.2 %copy-start.1 = (bf16[1,512,2048]{2,1,0:T(8,128)(2,1)S(1)}, bf16[1,512,2048]{2,1,0:T(8,128)(2,1)}, u32[]{:S(2)}) copy-start(bf16[1,512,2048]{2,1,0:T(8,128)(2,1)} %param.19) | copy-start | bytes 6291460
Sparse Core Ops, SparseCore 0:
  108.2 23.2 reduce-scatter.1
where the time goes:
time: 181 us; the launch traced here: 180 us
  matrix products  54.9 us (30%)
  local copies, waits for them, and re-layouts  42.5 us (23%)
  other arithmetic  37 us (20%)
  blocking collectives  26 us (14%)
  between operations  13.7 us (8%)
  starting transfers between devices  5.4 us (3%)
    dot_general x3, matrix products, one_block(): jnp.einsum('ro,cok->crk', offset_hot, operators, precision=lax.Precision....  24.6 us
    all_gather x1, blocking collectives, on_device(): mid_all = lax.all_gather(mid_pattern, 'box', axis=1, tiled=True)  16.8 us
    sub x3, other arithmetic, one_block(): real_part = jnp.sum(picked[0] * factors[0] - picked[1] * factors[1], axis=1)  12.6 us
    unnamed x35, local copies, waits for them, and re-layouts  11.3 us
    all_to_all x1, blocking collectives, on_device(): lax.all_to_all(mid_in, 'dir', split_axis=1, concat_axis=2, tiled=True)  9.21 us
    reduce_sum x3, other arithmetic, one_block(): imag_part = jnp.sum(picked[0] * factors[1] + picked[1] * factors[0], axis=1)  9.09 us
    reduce_sum x3, other arithmetic, one_block(): real_part = jnp.sum(picked[0] * factors[0] - picked[1] * factors[1], axis=1)  9 us
    dot_general x2, matrix products, adjoint_apply(): lax.dot_general(children[1], matrix, dims, preferred_element_type=jnp.flo...  7.44 us
  transfers between devices with their start and end apart: 2, of which 0 were waited for; matrix products, arithmetic and copies ran while one was open for 33% of the time, Pallas kernels for 0%

commit v1 on v0

v1 whole, which is shorter than its diff:
```python
import functools

import jax
import jax.numpy as jnp
from jax import lax
from jax.experimental import pallas as pl
from jax.experimental.pallas import tpu as pltpu
from jax.sharding import PartitionSpec as P

SINE = (1.0, -0.16666647791862488, 0.00833289884030819, -0.0001980085507966578, 2.5904087124217767e-06)
COSINE = (1.0, -0.5, 0.04166663438081741, -0.0013888360699638724, 2.476012559782248e-05, -2.6050881274386484e-07)
LANES = 128
ROWS = 8
VMEM_BYTES = 48 * 1024 * 1024


def powers(square, factors):
    total = jnp.full_like(square, factors[-1])
    for factor in factors[-2::-1]:
        total = total * square + factor
    return total


def phase(angle):
    half = angle * 0.5
    square = half * half
    sine = half * powers(square, SINE)
    cosine = powers(square, COSINE)
    return 1.0 - 2.0 * sine * sine, 2.0 * sine * cosine


def leaf_up(leaf_ref, table_ref, shift_ref, out_ref):
    octants, width = shift_ref.shape
    values = jnp.dot(leaf_ref[...], table_ref[...], preferred_element_type=jnp.float32)
    leaves = values.shape[0] // 2
    real = values[:leaves].reshape(leaves // octants, octants, width)
    imag = values[leaves:].reshape(leaves // octants, octants, width)
    cos, sin = phase(shift_ref[...])
    new_real = jnp.sum(real * cos[None] - imag * sin[None], axis=1)
    new_imag = jnp.sum(real * sin[None] + imag * cos[None], axis=1)
    block = jnp.concatenate([new_real, new_imag], axis=0).astype(out_ref.dtype)
    for copy in range(out_ref.shape[0]):
        out_ref[copy, 0] = block


def spread_rows(block, plain_ref, swapped_ref, first, part):
    pieces = block.shape[1] // LANES
    height = 2 * pieces
    for piece in range(pieces):
        lanes = block[:, piece * LANES : (piece + 1) * LANES]
        plain_ref[pl.ds(first * height + 2 * piece + part, ROWS, stride=height), :] = lanes
        swapped_ref[pl.ds(first * height + 2 * piece + 1 - part, ROWS, stride=height), :] = lanes


def translate(source_ref, offset_ref, trans_ref, plain_ref, swapped_ref, same_ref, cross_ref, row_count, height):
    list_width = source_ref.shape[0] // row_count

    def one_row(row, carry):
        same = [jnp.zeros((height, LANES), jnp.float32) for _ in range(2)]
        cross = [jnp.zeros((height, LANES), jnp.float32) for _ in range(2)]
        for entry in range(list_width):
            at = row * list_width + entry
            offset = pl.ds(pl.multiple_of(offset_ref[at], height), height)
            source = pl.ds(pl.multiple_of(source_ref[at], height), height)
            factor = trans_ref[offset, :]
            same[entry % 2] += factor * plain_ref[source, :]
            cross[entry % 2] += factor * swapped_ref[source, :]
        place = pl.ds(pl.multiple_of(row * height, height), height)
        same_ref[place, :] = same[0] + same[1]
        cross_ref[place, :] = cross[0] + cross[1]
        return carry

    lax.fori_loop(0, row_count, one_row, 0)


def gather_rows(same_ref, cross_ref, first, height):
    real, imag = [], []
    for piece in range(height // 2):
        even = pl.ds(first * height + 2 * piece, ROWS, stride=height)
        odd = pl.ds(first * height + 2 * piece + 1, ROWS, stride=height)
        real.append(same_ref[even, :] - same_ref[odd, :])
        imag.append(cross_ref[even, :] + cross_ref[odd, :])
    return jnp.concatenate(real, axis=1), jnp.concatenate(imag, axis=1)


def mid_translate(source_ref, offset_ref, mid_ref, trans_ref, out_ref, plain_ref, swapped_ref, same_ref, cross_ref):
    blocks, _, width = mid_ref.shape
    height = 2 * width // LANES
    for block in range(blocks):
        rows = mid_ref[block].astype(jnp.float32)
        spread_rows(rows[:ROWS], plain_ref, swapped_ref, block * ROWS, 0)
        spread_rows(rows[ROWS:], plain_ref, swapped_ref, block * ROWS, 1)
    row_count = out_ref.shape[1]
    translate(source_ref, offset_ref, trans_ref, plain_ref, swapped_ref, same_ref, cross_ref, row_count, height)
    for first in range(0, row_count, ROWS):
        real, imag = gather_rows(same_ref, cross_ref, first, height)
        out_ref[0, first : first + ROWS] = real
        out_ref[1, first : first + ROWS] = imag


def top_level(box_ref, source_ref, offset_ref, mid_ref, table_ref, shift_ref, trans_ref, out_ref, plain_ref, swapped_ref, same_ref, cross_ref):
    blocks, double, _ = mid_ref.shape
    octants, width = shift_ref.shape
    height = 2 * width // LANES
    cos, sin = phase(shift_ref[...])
    for first in range(0, blocks, ROWS):
        group = mid_ref[first : first + ROWS].reshape(ROWS * double, mid_ref.shape[2])
        values = jnp.dot(group, table_ref[0], preferred_element_type=jnp.float32)
        values = values.reshape(ROWS, double, width)
        real, imag = values[:, :octants], values[:, octants:]
        new_real = jnp.sum(real * cos[None] - imag * sin[None], axis=1)
        new_imag = jnp.sum(real * sin[None] + imag * cos[None], axis=1)
        new_real = new_real.astype(jnp.bfloat16).astype(jnp.float32)
        new_imag = new_imag.astype(jnp.bfloat16).astype(jnp.float32)
        spread_rows(new_real, plain_ref, swapped_ref, first, 0)
        spread_rows(new_imag, plain_ref, swapped_ref, first, 1)
    translate(source_ref, offset_ref, trans_ref, plain_ref, swapped_ref, same_ref, cross_ref, blocks, height)
    groups, own, _ = out_ref.shape
    own = own // 2
    for group in range(groups):
        real, imag = [], []
        for first in range(0, own, ROWS):
            new_real, new_imag = gather_rows(same_ref, cross_ref, group * own + first, height)
            real.append(new_real)
            imag.append(new_imag)
        out_ref[group] = jnp.concatenate(real + imag, axis=0).astype(out_ref.dtype)


def children_of(parents, cos, sin):
    half = parents.shape[0] // 2
    octants, width = cos.shape
    parents = parents.astype(jnp.float32)
    real, imag = parents[:half, None, :], parents[half:, None, :]
    new_real = (real * cos[None] + imag * sin[None]).reshape(half * octants, width)
    new_imag = (imag * cos[None] - real * sin[None]).reshape(half * octants, width)
    return jnp.concatenate([new_real, new_imag], axis=0).astype(jnp.bfloat16)


ADJOINT = (((1,), (1,)), ((), ()))


def top_down(scale, top_ref, table_ref, shift_ref, far_ref, out_ref):
    slices, double, width = top_ref.shape
    total = None
    for part in range(slices):
        columns = slice(part * width, (part + 1) * width)
        cos, sin = phase(shift_ref[:, columns])
        children = children_of(top_ref[part], cos, sin)
        term = lax.dot_general(children, table_ref[0, :, columns], ADJOINT, preferred_element_type=jnp.float32)
        total = term if total is None else total + term
    half = total.shape[0] // 2
    real = far_ref[0] + scale * total[:half]
    imag = far_ref[1] + scale * total[half:]
    owners, rows, _ = out_ref.shape
    rows = rows // 2
    for owner in range(owners):
        place = slice(owner * rows, (owner + 1) * rows)
        out_ref[owner] = jnp.concatenate([real[place], imag[place]], axis=0).astype(out_ref.dtype)


def leaf_down(scale, mid_ref, table_ref, shift_ref, out_ref):
    step = pl.program_id(0)
    cos, sin = phase(shift_ref[...])
    children = children_of(mid_ref[0], cos, sin)
    term = lax.dot_general(children, table_ref[...], ADJOINT, preferred_element_type=jnp.float32) * scale

    @pl.when(step == 0)
    def _():
        out_ref[...] = term

    @pl.when(step > 0)
    def _():
        out_ref[...] += term


def params():
    return pltpu.CompilerParams(vmem_limit_bytes=VMEM_BYTES)


def rows_of(trans):
    _, offsets, width = trans.shape
    pieces = width // LANES
    rows = jnp.transpose(trans.reshape(2, offsets, pieces, LANES), (1, 2, 0, 3))
    return rows.reshape(offsets * pieces * 2, LANES)


def on_device(
    leaf_out,
    interp_mid,
    shift_mid,
    trans_mid,
    list_mid,
    offset_mid,
    interp_top,
    shift_top,
    trans_top,
    list_top,
    offset_top,
):
    boxes = lax.axis_size("box")
    dirs = lax.axis_size("dir")
    box_index = lax.axis_index("box")
    octants = shift_mid.shape[0]
    leaves = leaf_out.shape[1]
    leaf_width, mid_width = interp_mid.shape
    own_mids = leaves // octants
    sector = trans_mid.shape[2]
    top_sector = interp_top.shape[2]
    top_width = trans_top.shape[3]
    devices = boxes * dirs
    mids = list_mid.shape[0]
    group_mids = mids // boxes
    tops = list_top.shape[0]
    group_tops = tops // boxes
    vmem = pl.BlockSpec(memory_space=pltpu.VMEM)
    smem = pl.BlockSpec(memory_space=pltpu.SMEM)

    outgoing = pl.pallas_call(
        leaf_up,
        grid=(dirs,),
        in_specs=[
            pl.BlockSpec((2 * leaves, leaf_width), lambda s: (0, 0)),
            pl.BlockSpec((leaf_width, sector), lambda s: (0, s)),
            pl.BlockSpec((octants, sector), lambda s: (0, s)),
        ],
        out_specs=pl.BlockSpec((boxes, 1, 2 * own_mids, sector), lambda s: (0, s, 0, 0)),
        out_shape=jax.ShapeDtypeStruct((boxes, dirs, 2 * own_mids, sector), jnp.bfloat16),
        compiler_params=params(),
        name="leaf_up",
    )(leaf_out.reshape(2 * leaves, leaf_width), interp_mid, shift_mid)
    outgoing = outgoing.reshape(devices, 2 * own_mids, sector)
    mid_all = lax.all_to_all(outgoing, ("box", "dir"), split_axis=0, concat_axis=0, tiled=True)

    top_height = 2 * top_width // LANES
    box_scalar = box_index.astype(jnp.int32).reshape(1)
    top_in = pl.pallas_call(
        top_level,
        grid_spec=pltpu.PrefetchScalarGridSpec(
            num_scalar_prefetch=3,
            grid=(1,),
            in_specs=[
                pl.BlockSpec(mid_all.shape, lambda i, box, *_: (0, 0, 0)),
                pl.BlockSpec((1, sector, top_width), lambda i, box, *_: (0, 0, box[0])),
                pl.BlockSpec((octants, top_width), lambda i, box, *_: (0, box[0])),
                pl.BlockSpec((trans_top.shape[1] * top_height, LANES), lambda i, box, *_: (0, 0)),
            ],
            out_specs=pl.BlockSpec((boxes, 2 * group_tops, top_width), lambda i, box, *_: (0, 0, 0)),
            scratch_shapes=[pltpu.VMEM((tops * top_height, LANES), jnp.float32)] * 4,
        ),
        out_shape=jax.ShapeDtypeStruct((boxes, 2 * group_tops, top_width), jnp.bfloat16),
        compiler_params=params(),
        name="top_level",
    )(
        box_scalar,
        (list_top * top_height).reshape(-1),
        (offset_top * top_height).reshape(-1),
        mid_all,
        interp_top,
        shift_top.reshape(octants, top_sector),
        rows_of(trans_top.reshape(2, -1, top_width)),
    )
    top_back = lax.all_to_all(top_in, "box", split_axis=0, concat_axis=0, tiled=True)

    mid_height = 2 * sector // LANES
    own_list = lax.dynamic_slice_in_dim(list_mid, box_index * group_mids, group_mids, 0)
    own_offsets = lax.dynamic_slice_in_dim(offset_mid, box_index * group_mids, group_mids, 0)
    mid_far = pl.pallas_call(
        mid_translate,
        in_specs=[smem, smem, vmem, vmem],
        out_specs=vmem,
        out_shape=jax.ShapeDtypeStruct((2, group_mids, sector), jnp.float32),
        scratch_shapes=[pltpu.VMEM((mids * mid_height, LANES), jnp.float32)] * 2
        + [pltpu.VMEM((group_mids * mid_height, LANES), jnp.float32)] * 2,
        compiler_params=params(),
        name="mid_translate",
    )(
        (own_list * mid_height).reshape(-1),
        (own_offsets * mid_height).reshape(-1),
        mid_all,
        rows_of(trans_mid),
    )

    incoming = pl.pallas_call(
        functools.partial(top_down, sector / top_sector),
        in_specs=[vmem] * 4,
        out_specs=vmem,
        out_shape=jax.ShapeDtypeStruct((dirs, 2 * own_mids, sector), jnp.bfloat16),
        compiler_params=params(),
        name="top_down",
    )(top_back, interp_top, shift_top.reshape(octants, top_sector), mid_far)
    mid_back = lax.all_to_all(incoming, "dir", split_axis=0, concat_axis=0, tiled=True)

    leaf_in = pl.pallas_call(
        functools.partial(leaf_down, leaf_width / mid_width),
        grid=(dirs,),
        in_specs=[
            pl.BlockSpec((1, 2 * own_mids, sector), lambda s: (s, 0, 0)),
            pl.BlockSpec((leaf_width, sector), lambda s: (0, s)),
            pl.BlockSpec((octants, sector), lambda s: (0, s)),
        ],
        out_specs=pl.BlockSpec((2 * leaves, leaf_width), lambda s: (0, 0)),
        out_shape=jax.ShapeDtypeStruct((2 * leaves, leaf_width), jnp.float32),
        compiler_params=params(),
        name="leaf_down",
    )(mid_back, interp_mid, shift_mid)
    return leaf_in.reshape(2, leaves, leaf_width)


def solution(mesh):
    return jax.shard_map(
        on_device,
        mesh=mesh,
        in_specs=(
            P(None, ("box", "dir"), None),
            P(),
            P(),
            P(None, None, "dir"),
            P(),
            P(),
            P("dir", None, None),
            P(None, "dir", None),
            P(None, None, "dir", "box"),
            P(),
            P(),
        ),
        out_specs=P(None, ("box", "dir"), None),
        check_vma=False,
    )
```

time: 181 us -> 76.8 us (0.42)
  matrix products: 54.9 us -> 0 us
  Pallas kernels: 0 us -> 36.9 us
  local copies, waits for them, and re-layouts: 42.5 us -> 5.8 us
  other arithmetic: 37 us -> 0.85 us
  blocking collectives: 26 us -> 8.45 us
  between operations: 13.7 us -> 0.12 us
  waiting for transfers between devices: 0.04 us -> 13.2 us
  starting transfers between devices: 5.4 us -> 10.7 us
    dot_general x18 -> x0, matrix products: 54.9 us -> none  [the longest x3 24.6 us: one_block(): jnp.einsum('ro,cok->crk', offset_hot, operators, precision=lax.Precision....]
    pallas_call x0 -> x5, Pallas kernels: none -> 36.9 us  [the longest x1 11.3 us: on_device(): pl.pallas_call(mid_translate, in_specs=[smem, smem, vmem, vmem], out_spec...]
    reduce_sum x8 -> x0, other arithmetic: 18.9 us -> none  [the longest x3 9.09 us: one_block(): imag_part = jnp.sum(picked[0] * factors[1] + picked[1] * factors[0], axis=1)]
    all_gather x1 -> x0, blocking collectives: 16.8 us -> none  [on_device(): mid_all = lax.all_gather(mid_pattern, 'box', axis=1, tiled=True)]
    all_to_all x1 -> x2, waiting for transfers between devices: 0.01 us -> 13.2 us  [the longest x1 13.2 us: on_device(): lax.all_to_all(outgoing, ('box', 'dir'), split_axis=0, concat_axis=0, til...]
    sub x3 -> x0, other arithmetic: 12.6 us -> none  [one_block(): real_part = jnp.sum(picked[0] * factors[0] - picked[1] * factors[1], axis=1)]
    unnamed x35 -> x19, local copies, waits for them, and re-layouts: 11.3 us -> 3.23 us
    all_to_all x2 -> x0, local copies, waits for them, and re-layouts: 5.68 us -> none  [the longest x1 5.6 us: on_device(): lax.all_to_all(own_parents, 'dir', split_axis=2, concat_axis=1, tiled=True)]
  transfers between devices with their start and end apart: 2 -> 2, of which waited for: 0 -> 1; matrix products, arithmetic and copies ran while one was open for 33% -> 5% of each run, Pallas kernels for 0% -> 15%
where the time goes in v1:
time: 76.8 us; the launch traced here: 76 us
  Pallas kernels  36.9 us (48%)
  waiting for transfers between devices  13.2 us (17%)
  starting transfers between devices  10.7 us (14%)
  blocking collectives  8.45 us (11%)
  local copies, waits for them, and re-layouts  5.8 us (8%)
  other arithmetic  0.85 us (1%)
    all_to_all x1, waiting for transfers between devices, on_device(): lax.all_to_all(outgoing, ('box', 'dir'), split_axis=0, concat_axis=0, til...  13.2 us
    pallas_call x1, Pallas kernels, on_device(): pl.pallas_call(mid_translate, in_specs=[smem, smem, vmem, vmem], out_spec...  11.3 us
    pallas_call x1, Pallas kernels, on_device(): pl.pallas_call(functools.partial(leaf_down, leaf_width / mid_width), grid...  8.58 us
    all_to_all x1, blocking collectives, on_device(): lax.all_to_all(incoming, 'dir', split_axis=0, concat_axis=0, tiled=True)  8.45 us
    pallas_call x1, Pallas kernels, on_device(): pl.pallas_call(top_level, grid_spec=pltpu.PrefetchScalarGridSpec(num_scal...  8.09 us
    pallas_call x1, Pallas kernels, on_device(): pl.pallas_call(leaf_up, grid=(dirs,), in_specs=[pl.BlockSpec((2 * leaves,...  8.05 us
    all_to_all x1, starting transfers between devices, on_device(): lax.all_to_all(outgoing, ('box', 'dir'), split_axis=0, concat_axis=0, til...  7.43 us
    all_to_all x1, starting transfers between devices, on_device(): lax.all_to_all(top_in, 'box', split_axis=0, concat_axis=0, tiled=True)  3.28 us
  transfers between devices with their start and end apart: 2, of which 1 were waited for; matrix products, arithmetic and copies ran while one was open for 5% of the time, Pallas kernels for 15%

profile of v1, /device:TPU:0, one launch (start us, length us, event | category | flops | bytes accessed | tf_op | source)
XLA Modules:
  0.0 76.0 jit_solution(12697805202758228604)
XLA Ops:
  0.0 0.9 %copy-done.2 = f32[8,4096]{1,0:T(8,128)S(1)} copy-done((f32[8,4096]{1,0:T(8,128)S(1)}, f32[8,4096]{1,0:T(8,128)}, u32[]{:S(2)}) %copy-start.2) | copy-done | bytes 131096
  0.9 0.9 %copy-done.4 = bf16[2,64,1024]{2,1,0:T(8,128)(2,1)S(1)} copy-done((bf16[2,64,1024]{2,1,0:T(8,128)(2,1)S(1)}, bf16[2,64,1024]{2,1,0:T(8,128)(2,1)}, u32[]{:S(2)}) %copy-start.4) | copy-done | bytes 262168
  1.9 8.0 %leaf_up.1 = bf16[4,8,16,512]{3,2,1,0:T(8,128)(2,1)} custom-call(bf16[128,1024]{1,0:T(8,128)(2,1)S(1)} %bitcast.20, bf16[1024,4096]{1,0:T(8,128)(2,1)} %table_ref.7, f32[8,4096]{1,0:T(8,128)S(1)} %copy-done.2), custom_call_target="tpu_custom_call" | custom-call | tf_op jit(solution)/shard_map/leaf_up/pallas_call | solution.py:218
  9.9 7.4 %all-to-all-start = ((bf16[32,16,512]{2,1,0:T(8,128)(2,1)}), bf16[32,16,512]{2,1,0:T(8,128)(2,1)}, u32[]{:S(2)}, u32[]{:S(2)}) async-start(bf16[32,16,512]{2,1,0:T(8,128)(2,1)} %bitcast.2), calls=%async_computation | async-start | bytes 1048576 | tf_op jit(solution)/shard_map/all_to_all | solution.py:232
  17.4 0.0 copy-done.6
  17.4 0.1 reshape.38.source_ref
  17.5 0.1 reshape.39.offset_ref
  17.6 0.0 copy-start
  17.6 2.1 %copy.14 = f32[2,316,4,128]{3,0,2,1:T(2,128)S(1)} copy(f32[2,316,4,128]{3,2,1,0:T(4,128)} %bitcast.21) | data formatting | bytes 2588672 | tf_op jit(solution)/shard_map/reshape;reshape | solution.py:183
  19.7 13.2 %all-to-all-done.mid_ref = bf16[32,16,512]{2,1,0:T(8,128)(2,1)} async-done(((bf16[32,16,512]{2,1,0:T(8,128)(2,1)}), bf16[32,16,512]{2,1,0:T(8,128)(2,1)}, u32[]{:S(2)}, u32[]{:S(2)}) %all-to-all-start) | async-done | bytes 524320 | tf_op jit(solution)/shard_map/all_to_all | solution.py:232
  32.9 8.1 %top_level.1 = bf16[4,16,512]{2,1,0:T(8,128)(2,1)} custom-call(s32[1]{0:T(128)} %bitcast.box_ref, s32[2048]{0:T(1024)S(1)} %reshape.38.source_ref, s32[2048]{0:T(1024)S(1)} %reshape.39.offset_ref, bf16[32,16,512]{2,1,0:T(8,128)(2,1)} %all-to-all-done.mid_ref, bf16[1,512,2048]{2,1,0:T(8,128)(2,1)S(1)} %copy-done, f32[8,2048]{1,0:T(8,128)S(1)} %bitcast.18, ...), custom_call_target="tpu_custom_call" | custom-call | tf_op jit(solution)/shard_map/top_level/pallas_call | solution.py:236
  41.0 3.3 %all-to-all-start.1 = ((bf16[4,16,512]{2,1,0:T(8,128)(2,1)}), bf16[4,16,512]{2,1,0:T(8,128)(2,1)S(1)}, u32[]{:S(2)}, u32[]{:S(2)}) async-start(bf16[4,16,512]{2,1,0:T(8,128)(2,1)} %top_level.1), calls=%async_computation.1 | async-start | bytes 131072 | tf_op jit(solution)/shard_map/all_to_all | solution.py:262
  44.3 0.8 %dynamic-slice_multiply_fusion = (s32[64,64]{0,1:T(8,128)S(1)}, s32[64,64]{0,1:T(8,128)S(1)}) fusion(s32[256,64]{0,1:T(8,128)S(1)} %copy-done.8, s32[]{:T(128)S(6)} %select_n.4, s32[256,64]{0,1:T(8,128)} %param.15), kind=kLoop, calls=%fused_computation.1 | loop fusion | flops 8192 | bytes 65540 | tf_op jit(solution)/shard_map/mul | solution.py:278
  45.1 0.1 copy.15
  45.2 0.1 reshape.44.source_ref
  45.3 0.1 copy.16
  45.3 0.1 reshape.45.offset_ref
  45.4 1.3 %copy-done.1 = f32[2,316,512]{2,0,1:T(2,128)S(1)} copy-done((f32[2,316,512]{2,0,1:T(2,128)S(1)}, f32[2,316,512]{2,0,1:T(2,128)}, u32[]{:S(2)}) %copy-start.1) | copy-done | bytes 1294360
  46.8 11.3 %mid_translate.1.far_ref = f32[2,64,512]{2,1,0:T(8,128)S(1)} custom-call(s32[4096]{0:T(1024)S(1)} %reshape.44.source_ref, s32[4096]{0:T(1024)S(1)} %reshape.45.offset_ref, bf16[32,16,512]{2,1,0:T(8,128)(2,1)} %all-to-all-done.mid_ref, f32[2528,128]{1,0:T(8,128)S(1)} %bitcast.17), custom_call_target="tpu_custom_call" | custom-call | tf_op jit(solution)/shard_map/mid_translate/pallas_call | solution.py:267
  58.1 0.0 copy-start.3
  58.1 0.0 all-to-all-done.1.top_ref
  58.1 0.8 %top_down.1 = bf16[8,16,512]{2,1,0:T(8,128)(2,1)S(1)} custom-call(bf16[4,16,512]{2,1,0:T(8,128)(2,1)S(1)} %all-to-all-done.1.top_ref, bf16[1,512,2048]{2,1,0:T(8,128)(2,1)S(1)} %copy-done, f32[8,2048]{1,0:T(8,128)S(1)} %bitcast.19, f32[2,64,512]{2,1,0:T(8,128)S(1)} %mid_translate.1.far_ref), custom_call_target="tpu_custom_call" | custom-call | tf_op jit(solution)/shard_map/top_down/pallas_call | solution.py:283
  59.0 8.5 %all_to_all.15.mid_ref = bf16[8,16,512]{2,1,0:T(8,128)(2,1)S(1)} all-to-all(bf16[8,16,512]{2,1,0:T(8,128)(2,1)S(1)} %top_down.1), channel_id=1, replica_groups=mesh['box'=4,'dir'=8] {'dir'}, dimensions={0} | all-to-all | bytes 262144 | tf_op jit(solution)/shard_map/all_to_all | solution.py:291
  67.4 8.6 %leaf_down.1 = f32[128,1024]{1,0:T(8,128)} custom-call(bf16[8,16,512]{2,1,0:T(8,128)(2,1)S(1)} %all_to_all.15.mid_ref, bf16[1024,4096]{1,0:T(8,128)(2,1)} %table_ref.7, f32[8,4096]{1,0:T(8,128)S(1)} %copy-done.3), custom_call_target="tpu_custom_call" | custom-call | tf_op jit(solution)/shard_map/leaf_down/pallas_call | solution.py:293
  (15 shorter events, 0.1 us)
Async XLA Ops:
  0.0 0.9 %copy-start.2 = (f32[8,4096]{1,0:T(8,128)S(1)}, f32[8,4096]{1,0:T(8,128)}, u32[]{:S(2)}) copy-start(f32[8,4096]{1,0:T(8,128)} %shift_ref.3) | copy-start | bytes 393220
  0.9 0.9 %copy-start.4 = (bf16[2,64,1024]{2,1,0:T(8,128)(2,1)S(1)}, bf16[2,64,1024]{2,1,0:T(8,128)(2,1)}, u32[]{:S(2)}) copy-start(bf16[2,64,1024]{2,1,0:T(8,128)(2,1)} %param.11) | copy-start | bytes 786436
  1.9 15.5 %copy-start.6 = (s32[32,64]{1,0:T(8,128)S(1)}, s32[32,64]{1,0:T(8,128)}, u32[]{:S(2)}) copy-start(s32[32,64]{1,0:T(8,128)} %param.20) | copy-start | bytes 24580
  1.9 15.6 %copy-start.7 = (s32[32,64]{1,0:T(8,128)S(1)}, s32[32,64]{1,0:T(8,128)}, u32[]{:S(2)}) copy-start(s32[32,64]{1,0:T(8,128)} %param.21) | copy-start | bytes 24580
  1.9 15.7 %copy-start.5 = (f32[8,1,2048]{2,1,0:T(1,128)S(1)}, f32[8,1,2048]{2,1,0:T(1,128)}, u32[]{:S(2)}) copy-start(f32[8,1,2048]{2,1,0:T(1,128)} %param.18) | copy-start | bytes 196612
  9.9 23.0 %all-to-all-start = ((bf16[32,16,512]{2,1,0:T(8,128)(2,1)}), bf16[32,16,512]{2,1,0:T(8,128)(2,1)}, u32[]{:S(2)}, u32[]{:S(2)}) async-start(bf16[32,16,512]{2,1,0:T(8,128)(2,1)} %bitcast.2), calls=%async_computation | async-start | bytes 1048576 | tf_op jit(solution)/shard_map/all_to_all | solution.py:232
  17.6 15.3 %copy-start = (bf16[1,512,2048]{2,1,0:T(8,128)(2,1)S(1)}, bf16[1,512,2048]{2,1,0:T(8,128)(2,1)}, u32[]{:S(2)}) copy-start(bf16[1,512,2048]{2,1,0:T(8,128)(2,1)} %table_ref.6) | copy-start | bytes 6291460
  32.9 11.4 %copy-start.8 = (s32[256,64]{0,1:T(8,128)S(1)}, s32[256,64]{0,1:T(8,128)}, u32[]{:S(2)}) copy-start(s32[256,64]{0,1:T(8,128)} %param.16) | copy-start | bytes 196612
  41.0 17.1 %all-to-all-start.1 = ((bf16[4,16,512]{2,1,0:T(8,128)(2,1)}), bf16[4,16,512]{2,1,0:T(8,128)(2,1)S(1)}, u32[]{:S(2)}, u32[]{:S(2)}) async-start(bf16[4,16,512]{2,1,0:T(8,128)(2,1)} %top_level.1), calls=%async_computation.1 | async-start | bytes 131072 | tf_op jit(solution)/shard_map/all_to_all | solution.py:262
  45.4 1.3 %copy-start.1 = (f32[2,316,512]{2,0,1:T(2,128)S(1)}, f32[2,316,512]{2,0,1:T(2,128)}, u32[]{:S(2)}) copy-start(f32[2,316,512]{2,0,1:T(2,128)} %param.14) | copy-start | bytes 3883012
  58.1 9.3 %copy-start.3 = (f32[8,4096]{1,0:T(8,128)S(1)}, f32[8,4096]{1,0:T(8,128)}, u32[]{:S(2)}) copy-start(f32[8,4096]{1,0:T(8,128)} %shift_ref.3) | copy-start | bytes 393220

commit v2 on v1

v2 whole, which is shorter than its diff:
```python
import functools
import math

import jax
import jax.numpy as jnp
from jax import lax
from jax.experimental import pallas as pl
from jax.experimental.pallas import tpu as pltpu
from jax.sharding import PartitionSpec as P

SINE = (1.0, -0.16666647791862488, 0.00833289884030819, -0.0001980085507966578, 2.5904087124217767e-06)
COSINE = (1.0, -0.5, 0.04166663438081741, -0.0013888360699638724, 2.476012559782248e-05, -2.6050881274386484e-07)
LANES = 128
ROWS = 8
AHEAD = 2
CHUNK_SECTORS = 2


def powers(square, factors):
    total = jnp.full_like(square, factors[-1])
    for factor in factors[-2::-1]:
        total = total * square + factor
    return total


def phase(angle):
    half = angle * 0.5
    square = half * half
    sine = half * powers(square, SINE)
    cosine = powers(square, COSINE)
    return 1.0 - 2.0 * sine * sine, 2.0 * sine * cosine


def leaf_up(leaf_hbm, table_hbm, shift_hbm, out_ref, leaf_ref, shift_ref, table_ref, small_sems, table_sems):
    chunks, _, width = table_ref.shape
    octants = shift_ref.shape[0]
    copies, _, rows, sector = out_ref.shape
    leaf_copy = pltpu.make_async_copy(leaf_hbm, leaf_ref, small_sems.at[0])
    shift_copy = pltpu.make_async_copy(shift_hbm, shift_ref, small_sems.at[1])

    def table_copy(chunk):
        source = table_hbm.at[:, pl.ds(chunk * width, width)]
        return pltpu.make_async_copy(source, table_ref.at[chunk], table_sems.at[chunk])

    leaf_copy.start()
    table_copy(0).start()
    shift_copy.start()
    for chunk in range(1, min(AHEAD, chunks)):
        table_copy(chunk).start()
    leaf_copy.wait()
    shift_copy.wait()
    leaves = leaf_ref.shape[0] // 2
    for chunk in range(chunks):
        table_copy(chunk).wait()
        if chunk + AHEAD < chunks:
            table_copy(chunk + AHEAD).start()
        values = jnp.dot(leaf_ref[...], table_ref[chunk], preferred_element_type=jnp.float32)
        real = values[:leaves].reshape(leaves // octants, octants, width)
        imag = values[leaves:].reshape(leaves // octants, octants, width)
        cos, sin = phase(shift_ref[:, chunk * width : (chunk + 1) * width])
        new_real = jnp.sum(real * cos[None] - imag * sin[None], axis=1)
        new_imag = jnp.sum(real * sin[None] + imag * cos[None], axis=1)
        block = jnp.concatenate([new_real, new_imag], axis=0).astype(out_ref.dtype)
        for part in range(width // sector):
            for copy in range(copies):
                out_ref[copy, chunk * (width // sector) + part] = block[:, part * sector : (part + 1) * sector]


def spread_rows(block, pattern_ref, first, part):
    pieces = block.shape[1] // LANES
    height = 2 * pieces
    for piece in range(pieces):
        lanes = block[:, piece * LANES : (piece + 1) * LANES]
        start = 2 * first * height + 2 * piece
        pattern_ref[pl.ds(start + part, ROWS, stride=2 * height), :] = lanes
        pattern_ref[pl.ds(start + height + 1 - part, ROWS, stride=2 * height), :] = lanes


def translate(source_ref, offset_ref, trans_ref, pattern_ref, same_ref, cross_ref, row_count, height):
    list_width = source_ref.shape[0] // row_count

    def one_row(row, carry):
        same = [jnp.zeros((height, LANES), jnp.float32) for _ in range(2)]
        cross = [jnp.zeros((height, LANES), jnp.float32) for _ in range(2)]
        for entry in range(list_width):
            at = row * list_width + entry
            offset = pl.multiple_of(offset_ref[at], height)
            source = pl.multiple_of(source_ref[at], height)
            factor = trans_ref[pl.ds(offset, height), :]
            same[entry % 2] += factor * pattern_ref[pl.ds(source, height), :]
            cross[entry % 2] += factor * pattern_ref[pl.ds(source + height, height), :]
        place = pl.ds(pl.multiple_of(row * height, height), height)
        same_ref[place, :] = same[0] + same[1]
        cross_ref[place, :] = cross[0] + cross[1]
        return carry

    lax.fori_loop(0, row_count, one_row, 0)


def gather_rows(same_ref, cross_ref, first, height):
    real, imag = [], []
    for piece in range(height // 2):
        even = pl.ds(first * height + 2 * piece, ROWS, stride=height)
        odd = pl.ds(first * height + 2 * piece + 1, ROWS, stride=height)
        real.append(same_ref[even, :] - same_ref[odd, :])
        imag.append(cross_ref[even, :] + cross_ref[odd, :])
    return jnp.concatenate(real, axis=1), jnp.concatenate(imag, axis=1)


def mid_translate(source_ref, offset_ref, mid_ref, trans_ref, out_ref, pattern_ref, same_ref, cross_ref):
    blocks, _, width = mid_ref.shape
    height = 2 * width // LANES
    for block in range(blocks):
        rows = mid_ref[block].astype(jnp.float32)
        spread_rows(rows[:ROWS], pattern_ref, block * ROWS, 0)
        spread_rows(rows[ROWS:], pattern_ref, block * ROWS, 1)
    row_count = out_ref.shape[1]
    translate(source_ref, offset_ref, trans_ref, pattern_ref, same_ref, cross_ref, row_count, height)
    for first in range(0, row_count, ROWS):
        real, imag = gather_rows(same_ref, cross_ref, first, height)
        out_ref[0, first : first + ROWS] = real
        out_ref[1, first : first + ROWS] = imag


def top_level(box_ref, source_ref, offset_ref, mid_ref, table_ref, shift_ref, trans_ref, out_ref, pattern_ref, same_ref, cross_ref):
    blocks, double, _ = mid_ref.shape
    octants = shift_ref.shape[0]
    width = out_ref.shape[2]
    height = 2 * width // LANES
    columns = pl.ds(pl.multiple_of(box_ref[0] * width, width), width)
    cos, sin = phase(shift_ref[:, columns])
    for first in range(0, blocks, ROWS):
        group = mid_ref[first : first + ROWS].reshape(ROWS * double, mid_ref.shape[2])
        values = jnp.dot(group, table_ref[0, :, columns], preferred_element_type=jnp.float32)
        values = values.reshape(ROWS, double, width)
        real, imag = values[:, :octants], values[:, octants:]
        new_real = jnp.sum(real * cos[None] - imag * sin[None], axis=1)
        new_imag = jnp.sum(real * sin[None] + imag * cos[None], axis=1)
        new_real = new_real.astype(jnp.bfloat16).astype(jnp.float32)
        new_imag = new_imag.astype(jnp.bfloat16).astype(jnp.float32)
        spread_rows(new_real, pattern_ref, first, 0)
        spread_rows(new_imag, pattern_ref, first, 1)
    translate(source_ref, offset_ref, trans_ref, pattern_ref, same_ref, cross_ref, blocks, height)
    groups, own, _ = out_ref.shape
    own = own // 2
    for group in range(groups):
        real, imag = [], []
        for first in range(0, own, ROWS):
            new_real, new_imag = gather_rows(same_ref, cross_ref, group * own + first, height)
            real.append(new_real)
            imag.append(new_imag)
        out_ref[group] = jnp.concatenate(real + imag, axis=0).astype(out_ref.dtype)


def children_of(parents, cos, sin):
    half = parents.shape[0] // 2
    octants, width = cos.shape
    parents = parents.astype(jnp.float32)
    real, imag = parents[:half, None, :], parents[half:, None, :]
    new_real = (real * cos[None] + imag * sin[None]).reshape(half * octants, width)
    new_imag = (imag * cos[None] - real * sin[None]).reshape(half * octants, width)
    return jnp.concatenate([new_real, new_imag], axis=0).astype(jnp.bfloat16)


ADJOINT = (((1,), (1,)), ((), ()))


def top_down(scale, top_ref, table_ref, shift_ref, far_ref, out_ref):
    slices, double, width = top_ref.shape
    total = None
    for part in range(slices):
        columns = slice(part * width, (part + 1) * width)
        cos, sin = phase(shift_ref[:, columns])
        children = children_of(top_ref[part], cos, sin)
        term = lax.dot_general(children, table_ref[0, :, columns], ADJOINT, preferred_element_type=jnp.float32)
        total = term if total is None else total + term
    half = total.shape[0] // 2
    real = far_ref[0] + scale * total[:half]
    imag = far_ref[1] + scale * total[half:]
    owners, rows, _ = out_ref.shape
    rows = rows // 2
    for owner in range(owners):
        place = slice(owner * rows, (owner + 1) * rows)
        out_ref[owner] = jnp.concatenate([real[place], imag[place]], axis=0).astype(out_ref.dtype)


def leaf_down(scale, mid_ref, table_ref, shift_ref, out_ref, total_ref):
    sectors, _, width = mid_ref.shape
    for part in range(sectors):
        columns = slice(part * width, (part + 1) * width)
        cos, sin = phase(shift_ref[:, columns])
        children = children_of(mid_ref[part], cos, sin)
        term = lax.dot_general(table_ref[:, columns], children, ADJOINT, preferred_element_type=jnp.float32)
        if part == 0:
            total_ref[...] = term
        else:
            total_ref[...] += term
    out_ref[...] = total_ref[...].T * scale


def params(mebibytes):
    return pltpu.CompilerParams(vmem_limit_bytes=mebibytes * 1024 * 1024)


def rows_of(trans):
    _, offsets, width = trans.shape
    pieces = width // LANES
    rows = jnp.transpose(trans.reshape(2, offsets, pieces, LANES), (1, 2, 0, 3))
    return rows.reshape(offsets * pieces * 2, LANES)


def on_device(
    leaf_out,
    interp_mid,
    shift_mid,
    trans_mid,
    list_mid,
    offset_mid,
    interp_top,
    shift_top,
    trans_top,
    list_top,
    offset_top,
):
    boxes = lax.axis_size("box")
    dirs = lax.axis_size("dir")
    box_index = lax.axis_index("box")
    octants = shift_mid.shape[0]
    leaves = leaf_out.shape[1]
    leaf_width, mid_width = interp_mid.shape
    own_mids = leaves // octants
    sector = trans_mid.shape[2]
    top_sector = interp_top.shape[2]
    top_width = trans_top.shape[3]
    devices = boxes * dirs
    mids = list_mid.shape[0]
    group_mids = mids // boxes
    tops = list_top.shape[0]
    group_tops = tops // boxes
    vmem = pl.BlockSpec(memory_space=pltpu.VMEM)
    smem = pl.BlockSpec(memory_space=pltpu.SMEM)
    hbm = pl.BlockSpec(memory_space=pl.ANY)
    top_height = 2 * top_width // LANES
    mid_height = 2 * sector // LANES

    chunk = sector * math.gcd(dirs, CHUNK_SECTORS)
    chunks = mid_width // chunk
    outgoing = pl.pallas_call(
        leaf_up,
        in_specs=[hbm, hbm, hbm],
        out_specs=vmem,
        out_shape=jax.ShapeDtypeStruct((boxes, dirs, 2 * own_mids, sector), jnp.bfloat16),
        scratch_shapes=[
            pltpu.VMEM((2 * leaves, leaf_width), jnp.bfloat16),
            pltpu.VMEM((octants, mid_width), jnp.float32),
            pltpu.VMEM((chunks, leaf_width, chunk), jnp.bfloat16),
            pltpu.SemaphoreType.DMA((2,)),
            pltpu.SemaphoreType.DMA((chunks,)),
        ],
        compiler_params=params(60),
        name="leaf_up",
    )(leaf_out.reshape(2 * leaves, leaf_width), interp_mid, shift_mid)
    outgoing = outgoing.reshape(devices, 2 * own_mids, sector)
    mid_all = lax.all_to_all(outgoing, ("box", "dir"), split_axis=0, concat_axis=0, tiled=True)

    box_scalar = box_index.astype(jnp.int32).reshape(1)
    top_list = (list_top * (2 * top_height)).reshape(-1)
    top_offsets = (offset_top * top_height).reshape(-1)
    own_list = lax.dynamic_slice_in_dim(list_mid, box_index * group_mids, group_mids, 0)
    own_offsets = lax.dynamic_slice_in_dim(offset_mid, box_index * group_mids, group_mids, 0)
    own_list = (own_list * (2 * mid_height)).reshape(-1)
    own_offsets = (own_offsets * mid_height).reshape(-1)
    rows_top = rows_of(trans_top.reshape(2, -1, top_width))
    rows_mid = rows_of(trans_mid)
    angles_top = shift_top.reshape(octants, top_sector)
    ready = (mid_all, top_list, top_offsets, own_list, own_offsets, rows_top, rows_mid, angles_top)
    mid_all, top_list, top_offsets, own_list, own_offsets, rows_top, rows_mid, angles_top = lax.optimization_barrier(ready)

    top_in = pl.pallas_call(
        top_level,
        in_specs=[smem, smem, smem, vmem, vmem, vmem, vmem],
        out_specs=vmem,
        out_shape=jax.ShapeDtypeStruct((boxes, 2 * group_tops, top_width), jnp.bfloat16),
        scratch_shapes=[
            pltpu.VMEM((2 * tops * top_height, LANES), jnp.float32),
            pltpu.VMEM((tops * top_height, LANES), jnp.float32),
            pltpu.VMEM((tops * top_height, LANES), jnp.float32),
        ],
        compiler_params=params(16),
        name="top_level",
    )(box_scalar, top_list, top_offsets, mid_all, interp_top, angles_top, rows_top)
    top_back = lax.all_to_all(top_in, "box", split_axis=0, concat_axis=0, tiled=True)

    mid_far = pl.pallas_call(
        mid_translate,
        in_specs=[smem, smem, vmem, vmem],
        out_specs=vmem,
        out_shape=jax.ShapeDtypeStruct((2, group_mids, sector), jnp.float32),
        scratch_shapes=[
            pltpu.VMEM((2 * mids * mid_height, LANES), jnp.float32),
            pltpu.VMEM((group_mids * mid_height, LANES), jnp.float32),
            pltpu.VMEM((group_mids * mid_height, LANES), jnp.float32),
        ],
        compiler_params=params(16),
        name="mid_translate",
    )(own_list, own_offsets, mid_all, rows_mid)

    incoming = pl.pallas_call(
        functools.partial(top_down, sector / top_sector),
        in_specs=[vmem] * 4,
        out_specs=vmem,
        out_shape=jax.ShapeDtypeStruct((dirs, 2 * own_mids, sector), jnp.bfloat16),
        compiler_params=params(16),
        name="top_down",
    )(top_back, interp_top, angles_top, mid_far)
    mid_back = lax.all_to_all(incoming, "dir", split_axis=0, concat_axis=0, tiled=True)

    leaf_in = pl.pallas_call(
        functools.partial(leaf_down, leaf_width / mid_width),
        in_specs=[vmem] * 3,
        out_specs=vmem,
        out_shape=jax.ShapeDtypeStruct((2 * leaves, leaf_width), jnp.float32),
        scratch_shapes=[pltpu.VMEM((leaf_width, 2 * leaves), jnp.float32)],
        compiler_params=params(20),
        name="leaf_down",
    )(mid_back, interp_mid, shift_mid)
    return leaf_in.reshape(2, leaves, leaf_width)


def solution(mesh):
    return jax.shard_map(
        on_device,
        mesh=mesh,
        in_specs=(
            P(None, ("box", "dir"), None),
            P(),
            P(),
            P(None, None, "dir"),
            P(),
            P(),
            P("dir", None, None),
            P(None, "dir", None),
            P(None, None, "dir", "box"),
            P(),
            P(),
        ),
        out_specs=P(None, ("box", "dir"), None),
        check_vma=False,
    )
```

time: 76.8 us -> 64 us (0.83)
  Pallas kernels: 36.9 us -> 24 us
  local copies, waits for them, and re-layouts: 5.8 us -> 7.33 us
    pallas_call x3, Pallas kernels: 24.7 us -> 14.6 us  [the longest x1 5.89 us: on_device(): pl.pallas_call(top_level, in_specs=[smem, smem, smem, vmem, vmem, vmem, v...]
    pallas_call x1, Pallas kernels: 11.3 us -> 8.54 us  [on_device(): pl.pallas_call(mid_translate, in_specs=[smem, smem, vmem, vmem], out_spec...]
    unnamed x19, local copies, waits for them, and re-layouts: 3.23 us -> 4.75 us
  transfers between devices with their start and end apart: 2 -> 2, of which waited for: 1 -> 1; matrix products, arithmetic and copies ran while one was open for 5% -> 4% of each run, Pallas kernels for 15% -> 13%
where the time goes in v2:
time: 64 us; the launch traced here: 63.5 us
  Pallas kernels  24 us (38%)
  waiting for transfers between devices  12.8 us (20%)
  starting transfers between devices  10.7 us (17%)
  blocking collectives  8.45 us (13%)
  local copies, waits for them, and re-layouts  7.33 us (11%)
    all_to_all x1, waiting for transfers between devices, on_device(): lax.all_to_all(outgoing, ('box', 'dir'), split_axis=0, concat_axis=0, til...  12.8 us
    pallas_call x1, Pallas kernels, on_device(): pl.pallas_call(mid_translate, in_specs=[smem, smem, vmem, vmem], out_spec...  8.54 us
    all_to_all x1, blocking collectives, on_device(): lax.all_to_all(incoming, 'dir', split_axis=0, concat_axis=0, tiled=True)  8.45 us
    all_to_all x1, starting transfers between devices, on_device(): lax.all_to_all(outgoing, ('box', 'dir'), split_axis=0, concat_axis=0, til...  7.45 us
    pallas_call x1, Pallas kernels, on_device(): pl.pallas_call(top_level, in_specs=[smem, smem, smem, vmem, vmem, vmem, v...  5.89 us
    pallas_call x1, Pallas kernels, on_device(): pl.pallas_call(leaf_up, in_specs=[hbm, hbm, hbm], out_specs=vmem, out_sha...  5.48 us
    unnamed x19, local copies, waits for them, and re-layouts  4.75 us
    all_to_all x1, starting transfers between devices, on_device(): lax.all_to_all(top_in, 'box', split_axis=0, concat_axis=0, tiled=True)  3.28 us
  transfers between devices with their start and end apart: 2, of which 1 were waited for; matrix products, arithmetic and copies ran while one was open for 4% of the time, Pallas kernels for 13%

profile of v2, /device:TPU:0, one launch (start us, length us, event | category | flops | bytes accessed | tf_op | source)
XLA Modules:
  0.0 63.5 jit_solution(17147856807774698514)
XLA Ops:
  0.0 5.5 %leaf_up.1 = bf16[4,8,16,512]{3,2,1,0:T(8,128)(2,1)} custom-call(bf16[128,1024]{1,0:T(8,128)(2,1)} %bitcast.22, bf16[1024,4096]{1,0:T(8,128)(2,1)} %table_ref.5, f32[8,4096]{1,0:T(8,128)} %shift_ref.1), custom_call_target="tpu_custom_call" | custom-call | tf_op jit(solution)/shard_map/leaf_up/pallas_call | solution.py:248
  5.5 0.0 copy-start.4
  5.5 7.5 %all-to-all-start = ((bf16[32,16,512]{2,1,0:T(8,128)(2,1)}), bf16[32,16,512]{2,1,0:T(8,128)(2,1)}, u32[]{:S(2)}, u32[]{:S(2)}) async-start(bf16[32,16,512]{2,1,0:T(8,128)(2,1)} %bitcast.20), calls=%async_computation | async-start | bytes 1048576 | tf_op jit(solution)/shard_map/all_to_all | solution.py:264
  13.0 0.1 reshape.39.source_ref
  13.1 0.1 reshape.40.offset_ref
  13.2 0.1 dynamic-slice_multiply_fusion
  13.2 0.1 copy.15
  13.3 0.1 reshape.42.offset_ref
  13.4 0.1 copy.14
  13.5 0.1 reshape.41.source_ref
  13.6 0.0 copy-start.1
  13.6 2.1 %copy.16 = f32[2,316,4,128]{3,0,2,1:T(2,128)S(1)} copy(f32[2,316,4,128]{3,2,1,0:T(4,128)} %bitcast.21) | data formatting | bytes 2588672 | tf_op jit(solution)/shard_map/reshape;reshape | solution.py:208
  15.7 12.8 %all-to-all-done.mid_ref = bf16[32,16,512]{2,1,0:T(8,128)(2,1)} async-done(((bf16[32,16,512]{2,1,0:T(8,128)(2,1)}), bf16[32,16,512]{2,1,0:T(8,128)(2,1)}, u32[]{:S(2)}, u32[]{:S(2)}) %all-to-all-start) | async-done | bytes 524320 | tf_op jit(solution)/shard_map/all_to_all | solution.py:264
  28.5 5.9 %top_level.1 = bf16[4,16,512]{2,1,0:T(8,128)(2,1)} custom-call(s32[1]{0:T(128)} %bitcast.box_ref, s32[2048]{0:T(1024)S(1)} %reshape.39.source_ref, s32[2048]{0:T(1024)S(1)} %reshape.40.offset_ref, bf16[32,16,512]{2,1,0:T(8,128)(2,1)} %all-to-all-done.mid_ref, bf16[1,512,2048]{2,1,0:T(8,128)(2,1)S(1)} %copy-done.1, f32[8,2048]{1,0:T(8,128)S(1)} %bitcast.18, ...), custom_call_target="tpu_custom_call" | custom-call | tf_op jit(solution)/shard_map/top_level/pallas_call | solution.py:279
  34.4 3.3 %all-to-all-start.1 = ((bf16[4,16,512]{2,1,0:T(8,128)(2,1)}), bf16[4,16,512]{2,1,0:T(8,128)(2,1)S(1)}, u32[]{:S(2)}, u32[]{:S(2)}) async-start(bf16[4,16,512]{2,1,0:T(8,128)(2,1)} %top_level.1), calls=%async_computation.1 | async-start | bytes 131072 | tf_op jit(solution)/shard_map/all_to_all | solution.py:292
  37.7 0.0 copy-start.2
  37.7 1.3 %copy-done.2 = f32[2,316,512]{2,0,1:T(2,128)S(1)} copy-done((f32[2,316,512]{2,0,1:T(2,128)S(1)}, f32[2,316,512]{2,0,1:T(2,128)}, u32[]{:S(2)}) %copy-start.2) | copy-done | bytes 1294360
  39.0 8.5 %mid_translate.1.far_ref = f32[2,64,512]{2,1,0:T(8,128)S(1)} custom-call(s32[4096]{0:T(1024)S(1)} %reshape.41.source_ref, s32[4096]{0:T(1024)S(1)} %reshape.42.offset_ref, bf16[32,16,512]{2,1,0:T(8,128)(2,1)} %all-to-all-done.mid_ref, f32[2528,128]{1,0:T(8,128)S(1)} %bitcast.17), custom_call_target="tpu_custom_call" | custom-call | tf_op jit(solution)/shard_map/mid_translate/pallas_call | solution.py:294
  47.5 0.0 copy-start.3
  47.5 0.0 all-to-all-done.1.top_ref
  47.6 0.8 %top_down.1 = bf16[8,16,512]{2,1,0:T(8,128)(2,1)S(1)} custom-call(bf16[4,16,512]{2,1,0:T(8,128)(2,1)S(1)} %all-to-all-done.1.top_ref, bf16[1,512,2048]{2,1,0:T(8,128)(2,1)S(1)} %copy-done.1, f32[8,2048]{1,0:T(8,128)S(1)} %bitcast.19, f32[2,64,512]{2,1,0:T(8,128)S(1)} %mid_translate.1.far_ref), custom_call_target="tpu_custom_call" | custom-call | tf_op jit(solution)/shard_map/top_down/pallas_call | solution.py:308
  48.4 8.5 %all_to_all.15.mid_ref = bf16[8,16,512]{2,1,0:T(8,128)(2,1)S(1)} all-to-all(bf16[8,16,512]{2,1,0:T(8,128)(2,1)S(1)} %top_down.1), channel_id=1, replica_groups=mesh['box'=4,'dir'=8] {'dir'}, dimensions={0} | all-to-all | bytes 262144 | tf_op jit(solution)/shard_map/all_to_all | solution.py:316
  56.9 3.4 %copy-done = bf16[1024,4096]{1,0:T(8,128)(2,1)S(1)} copy-done((bf16[1024,4096]{1,0:T(8,128)(2,1)S(1)}, bf16[1024,4096]{1,0:T(8,128)(2,1)}, u32[]{:S(2)}) %copy-start) | copy-done | bytes 8388632
  60.2 3.2 %leaf_down.1 = f32[128,1024]{1,0:T(8,128)} custom-call(bf16[8,16,512]{2,1,0:T(8,128)(2,1)S(1)} %all_to_all.15.mid_ref, bf16[1024,4096]{1,0:T(8,128)(2,1)S(1)} %copy-done, f32[8,4096]{1,0:T(8,128)S(1)} %copy-done.3), custom_call_target="tpu_custom_call" | custom-call | tf_op jit(solution)/shard_map/leaf_down/pallas_call | solution.py:318
  (15 shorter events, 0.1 us)
Async XLA Ops:
  0.0 13.0 %copy-start.5 = (s32[32,64]{1,0:T(8,128)S(1)}, s32[32,64]{1,0:T(8,128)}, u32[]{:S(2)}) copy-start(s32[32,64]{1,0:T(8,128)} %param.20) | copy-start | bytes 24580
  0.0 13.1 %copy-start.6 = (s32[32,64]{1,0:T(8,128)S(1)}, s32[32,64]{1,0:T(8,128)}, u32[]{:S(2)}) copy-start(s32[32,64]{1,0:T(8,128)} %param.21) | copy-start | bytes 24580
  0.0 13.1 %copy-start.7 = (s32[256,64]{0,1:T(8,128)S(1)}, s32[256,64]{0,1:T(8,128)}, u32[]{:S(2)}) copy-start(s32[256,64]{0,1:T(8,128)} %param.16) | copy-start | bytes 196612
  0.0 13.1 %copy-start.8 = (s32[256,64]{0,1:T(8,128)S(1)}, s32[256,64]{0,1:T(8,128)}, u32[]{:S(2)}) copy-start(s32[256,64]{0,1:T(8,128)} %param.15) | copy-start | bytes 196612
  5.5 8.1 %copy-start.4 = (f32[8,1,2048]{2,1,0:T(1,128)S(1)}, f32[8,1,2048]{2,1,0:T(1,128)}, u32[]{:S(2)}) copy-start(f32[8,1,2048]{2,1,0:T(1,128)} %param.18) | copy-start | bytes 196612
  5.5 23.0 %all-to-all-start = ((bf16[32,16,512]{2,1,0:T(8,128)(2,1)}), bf16[32,16,512]{2,1,0:T(8,128)(2,1)}, u32[]{:S(2)}, u32[]{:S(2)}) async-start(bf16[32,16,512]{2,1,0:T(8,128)(2,1)} %bitcast.20), calls=%async_computation | async-start | bytes 1048576 | tf_op jit(solution)/shard_map/all_to_all | solution.py:264
  13.6 14.9 %copy-start.1 = (bf16[1,512,2048]{2,1,0:T(8,128)(2,1)S(1)}, bf16[1,512,2048]{2,1,0:T(8,128)(2,1)}, u32[]{:S(2)}) copy-start(bf16[1,512,2048]{2,1,0:T(8,128)(2,1)} %table_ref.4) | copy-start | bytes 6291460
  34.4 13.2 %all-to-all-start.1 = ((bf16[4,16,512]{2,1,0:T(8,128)(2,1)}), bf16[4,16,512]{2,1,0:T(8,128)(2,1)S(1)}, u32[]{:S(2)}, u32[]{:S(2)}) async-start(bf16[4,16,512]{2,1,0:T(8,128)(2,1)} %top_level.1), calls=%async_computation.1 | async-start | bytes 131072 | tf_op jit(solution)/shard_map/all_to_all | solution.py:292
  37.7 1.3 %copy-start.2 = (f32[2,316,512]{2,0,1:T(2,128)S(1)}, f32[2,316,512]{2,0,1:T(2,128)}, u32[]{:S(2)}) copy-start(f32[2,316,512]{2,0,1:T(2,128)} %param.14) | copy-start | bytes 3883012
  47.5 9.3 %copy-start.3 = (f32[8,4096]{1,0:T(8,128)S(1)}, f32[8,4096]{1,0:T(8,128)}, u32[]{:S(2)}) copy-start(f32[8,4096]{1,0:T(8,128)} %shift_ref.1) | copy-start | bytes 393220
  56.9 3.4 %copy-start = (bf16[1024,4096]{1,0:T(8,128)(2,1)S(1)}, bf16[1024,4096]{1,0:T(8,128)(2,1)}, u32[]{:S(2)}) copy-start(bf16[1024,4096]{1,0:T(8,128)(2,1)} %table_ref.5) | copy-start | bytes 25165828

commit v3 on v2

v3 whole, which is shorter than its diff:
```python
import functools
import math

import jax
import jax.numpy as jnp
from jax import lax
from jax.experimental import pallas as pl
from jax.experimental.pallas import tpu as pltpu
from jax.sharding import PartitionSpec as P

SINE = (1.0, -0.16666647791862488, 0.00833289884030819, -0.0001980085507966578, 2.5904087124217767e-06)
COSINE = (1.0, -0.5, 0.04166663438081741, -0.0013888360699638724, 2.476012559782248e-05, -2.6050881274386484e-07)
HEAD_ROWS = 4
LANES = 128
ROWS = 8
AHEAD = 2
CHUNK_SECTORS = 2


def powers(square, factors):
    total = jnp.full_like(square, factors[-1])
    for factor in factors[-2::-1]:
        total = total * square + factor
    return total


def phase(angle):
    half = angle * 0.5
    square = half * half
    sine = half * powers(square, SINE)
    cosine = powers(square, COSINE)
    return 1.0 - 2.0 * sine * sine, 2.0 * sine * cosine


def leaf_up(leaf_hbm, table_hbm, shift_hbm, out_ref, leaf_ref, shift_ref, table_ref, small_sems, table_sems):
    chunks, _, width = table_ref.shape
    octants = shift_ref.shape[0]
    sector = out_ref.shape[2]
    leaf_copy = pltpu.make_async_copy(leaf_hbm, leaf_ref, small_sems.at[0])
    shift_copy = pltpu.make_async_copy(shift_hbm, shift_ref, small_sems.at[1])

    def table_copy(chunk):
        source = table_hbm.at[:, pl.ds(chunk * width, width)]
        return pltpu.make_async_copy(source, table_ref.at[chunk], table_sems.at[chunk])

    leaf_copy.start()
    table_copy(0).start()
    shift_copy.start()
    for chunk in range(1, min(AHEAD, chunks)):
        table_copy(chunk).start()
    leaf_copy.wait()
    shift_copy.wait()
    leaves = leaf_ref.shape[0] // 2
    for chunk in range(chunks):
        table_copy(chunk).wait()
        if chunk + AHEAD < chunks:
            table_copy(chunk + AHEAD).start()
        values = jnp.dot(leaf_ref[...], table_ref[chunk], preferred_element_type=jnp.float32)
        real = values[:leaves].reshape(leaves // octants, octants, width)
        imag = values[leaves:].reshape(leaves // octants, octants, width)
        cos, sin = phase(shift_ref[:, chunk * width : (chunk + 1) * width])
        new_real = jnp.sum(real * cos[None] - imag * sin[None], axis=1)
        new_imag = jnp.sum(real * sin[None] + imag * cos[None], axis=1)
        block = jnp.concatenate([new_real, new_imag], axis=0).astype(out_ref.dtype)
        for part in range(width // sector):
            out_ref[chunk * (width // sector) + part] = block[:, part * sector : (part + 1) * sector]


def spread_rows(block, pattern_ref, first, part):
    pieces = block.shape[1] // LANES
    height = 2 * pieces
    for piece in range(pieces):
        lanes = block[:, piece * LANES : (piece + 1) * LANES]
        start = 2 * first * height + 2 * piece
        pattern_ref[pl.ds(start + part, ROWS, stride=2 * height), :] = lanes
        pattern_ref[pl.ds(start + height + 1 - part, ROWS, stride=2 * height), :] = lanes


def index_copies(hbm_refs, index_refs, sems, head):
    entries = index_refs[0].shape[0]
    parts = (pl.ds(0, head), pl.ds(head, entries - head))
    return [
        [
            pltpu.make_async_copy(hbm_refs[which].at[part], index_refs[which].at[part], sems.at[2 * which + number])
            for which in range(2)
        ]
        for number, part in enumerate(parts)
    ]


def translate(index_refs, first_row, end_row, list_width, trans_ref, pattern_ref, same_ref, cross_ref, height):
    source_ref, offset_ref = index_refs

    def rows_at(step, carry):
        for row in (2 * step, 2 * step + 1):
            same = jnp.zeros((height, LANES), jnp.float32)
            cross = jnp.zeros((height, LANES), jnp.float32)
            for entry in range(list_width):
                source = pl.multiple_of(source_ref[row * list_width + entry], height)
                offset = pl.multiple_of(offset_ref[row * list_width + entry], height)
                factor = trans_ref[pl.ds(offset, height), :]
                same += factor * pattern_ref[pl.ds(source, height), :]
                cross += factor * pattern_ref[pl.ds(source + height, height), :]
            place = pl.ds(pl.multiple_of(row * height, height), height)
            same_ref[place, :] = same
            cross_ref[place, :] = cross
        return carry

    lax.fori_loop(first_row // 2, end_row // 2, rows_at, 0)


def gather_rows(same_ref, cross_ref, first, height):
    real, imag = [], []
    for piece in range(height // 2):
        even = pl.ds(first * height + 2 * piece, ROWS, stride=height)
        odd = pl.ds(first * height + 2 * piece + 1, ROWS, stride=height)
        real.append(same_ref[even, :] - same_ref[odd, :])
        imag.append(cross_ref[even, :] + cross_ref[odd, :])
    return jnp.concatenate(real, axis=1), jnp.concatenate(imag, axis=1)


def tables(shift_ref, table_hbm, cos_ref, sin_ref, table_ref, sem):
    table_copy = pltpu.make_async_copy(table_hbm, table_ref, sem)
    table_copy.start()
    cos_ref[...], sin_ref[...] = phase(shift_ref[:, 0, :])
    table_copy.wait()


def place_of(step):
    return lax.axis_index("box") ^ step


def top_up(mid_ref, table_ref, cos_ref, sin_ref, *out_refs):
    tops, double, sector = mid_ref.shape
    octants = cos_ref.shape[0]
    group = mid_ref[...].reshape(tops * double, sector)
    for step, out_ref in enumerate(out_refs):
        width = out_ref.shape[1]
        columns = pl.ds(pl.multiple_of(place_of(step) * width, width), width)
        values = jnp.dot(group, table_ref[0, :, columns], preferred_element_type=jnp.float32)
        values = values.reshape(tops, double, width)
        real, imag = values[:, :octants], values[:, octants:]
        cos, sin = cos_ref[:, columns], sin_ref[:, columns]
        new_real = jnp.sum(real * cos[None] - imag * sin[None], axis=1)
        new_imag = jnp.sum(real * sin[None] + imag * cos[None], axis=1)
        out_ref[...] = jnp.concatenate([new_real, new_imag], axis=0).astype(out_ref.dtype)


def top_translate(list_width, source_hbm, offset_hbm, trans_ref, *rest):
    count = (len(rest) - 6) // 2
    top_refs, out_refs = rest[:count], rest[count : 2 * count]
    pattern_ref, same_ref, cross_ref, *index_refs, sems = rest[2 * count :]
    head = HEAD_ROWS * list_width
    first_copies, later_copies = index_copies((source_hbm, offset_hbm), index_refs, sems, head)
    for copy in first_copies + later_copies:
        copy.start()
    own, width = top_refs[0].shape
    own = own // 2
    height = 2 * width // LANES
    for step, top_ref in enumerate(top_refs):
        rows = top_ref[...].astype(jnp.float32)
        for first in range(0, own, ROWS):
            base = place_of(step) * own + first
            spread_rows(rows[first : first + ROWS], pattern_ref, base, 0)
            spread_rows(rows[own + first : own + first + ROWS], pattern_ref, base, 1)
    for copy in first_copies:
        copy.wait()
    rest = (list_width, trans_ref, pattern_ref, same_ref, cross_ref, height)
    translate(index_refs, 0, HEAD_ROWS, *rest)
    for copy in later_copies:
        copy.wait()
    translate(index_refs, HEAD_ROWS, count * own, *rest)
    for step, out_ref in enumerate(out_refs):
        real, imag = [], []
        for first in range(0, own, ROWS):
            new_real, new_imag = gather_rows(same_ref, cross_ref, place_of(step) * own + first, height)
            real.append(new_real)
            imag.append(new_imag)
        out_ref[...] = jnp.concatenate(real + imag, axis=0).astype(out_ref.dtype)


def mid_translate(list_width, source_hbm, offset_hbm, trans_ref, *rest):
    group_refs = rest[:-7]
    out_ref, pattern_ref, same_ref, cross_ref, *index_refs, sems = rest[-7:]
    head = HEAD_ROWS * list_width
    first_copies, later_copies = index_copies((source_hbm, offset_hbm), index_refs, sems, head)
    for copy in first_copies + later_copies:
        copy.start()
    for step, group_ref in enumerate(group_refs):
        blocks, _, width = group_ref.shape
        height = 2 * width // LANES
        base = place_of(step) * (blocks * ROWS)
        for block in range(blocks):
            rows = group_ref[block].astype(jnp.float32)
            spread_rows(rows[:ROWS], pattern_ref, base + block * ROWS, 0)
            spread_rows(rows[ROWS:], pattern_ref, base + block * ROWS, 1)
    for copy in first_copies:
        copy.wait()
    rest = (list_width, trans_ref, pattern_ref, same_ref, cross_ref, height)
    translate(index_refs, 0, HEAD_ROWS, *rest)
    for copy in later_copies:
        copy.wait()
    translate(index_refs, HEAD_ROWS, out_ref.shape[1], *rest)
    for first in range(0, out_ref.shape[1], ROWS):
        real, imag = gather_rows(same_ref, cross_ref, first, height)
        out_ref[0, first : first + ROWS] = real
        out_ref[1, first : first + ROWS] = imag


def children_of(parents, cos, sin):
    half = parents.shape[0] // 2
    octants, width = cos.shape
    parents = parents.astype(jnp.float32)
    real, imag = parents[:half, None, :], parents[half:, None, :]
    new_real = (real * cos[None] + imag * sin[None]).reshape(half * octants, width)
    new_imag = (imag * cos[None] - real * sin[None]).reshape(half * octants, width)
    return jnp.concatenate([new_real, new_imag], axis=0).astype(jnp.bfloat16)


ADJOINT = (((1,), (1,)), ((), ()))


def top_down(scale, table_ref, cos_ref, sin_ref, far_ref, *rest):
    top_refs, out_ref = rest[:-1], rest[-1]
    total = None
    for step, top_ref in enumerate(top_refs):
        width = top_ref.shape[1]
        columns = pl.ds(pl.multiple_of(place_of(step) * width, width), width)
        children = children_of(top_ref[...], cos_ref[:, columns], sin_ref[:, columns])
        term = lax.dot_general(children, table_ref[0, :, columns], ADJOINT, preferred_element_type=jnp.float32)
        total = term if total is None else total + term
    half = total.shape[0] // 2
    real = far_ref[0] + scale * total[:half]
    imag = far_ref[1] + scale * total[half:]
    owners, rows, _ = out_ref.shape
    rows = rows // 2
    for owner in range(owners):
        place = slice(owner * rows, (owner + 1) * rows)
        out_ref[owner] = jnp.concatenate([real[place], imag[place]], axis=0).astype(out_ref.dtype)


def leaf_down(scale, mid_ref, table_ref, shift_ref, out_ref, total_ref):
    sectors, _, width = mid_ref.shape
    for part in range(sectors):
        columns = slice(part * width, (part + 1) * width)
        cos, sin = phase(shift_ref[:, columns])
        children = children_of(mid_ref[part], cos, sin)
        term = lax.dot_general(table_ref[:, columns], children, ADJOINT, preferred_element_type=jnp.float32)
        if part == 0:
            total_ref[...] = term
        else:
            total_ref[...] += term
    out_ref[...] = total_ref[...].T * scale


def cost(microseconds):
    return pl.CostEstimate(flops=int(microseconds * 1.15e9), bytes_accessed=0, transcendentals=0)


def params(mebibytes):
    return pltpu.CompilerParams(vmem_limit_bytes=mebibytes * 1024 * 1024)


def rows_of(trans):
    _, offsets, width = trans.shape
    pieces = width // LANES
    rows = jnp.transpose(trans.reshape(2, offsets, pieces, LANES), (1, 2, 0, 3))
    return rows.reshape(offsets * pieces * 2, LANES)


def swap(values, axis, step):
    size = lax.axis_size(axis)
    return lax.ppermute(values, axis, [(k, k ^ step) for k in range(size)])


def pass_on(values_ref, after_ref, out_ref):
    out_ref[...] = values_ref[...]


def follow(values, after):
    vmem = pl.BlockSpec(memory_space=pltpu.VMEM)
    return pl.pallas_call(
        pass_on,
        in_specs=[vmem, pl.BlockSpec(memory_space=pl.ANY)],
        out_specs=vmem,
        out_shape=jax.ShapeDtypeStruct(values.shape, values.dtype),
        compiler_params=params(16),
        cost_estimate=cost(0.1),
        name="pass_on",
    )(values, after)


def exchange(shares):
    received = list(shares)
    for step in reversed(range(1, len(shares))):
        received[step] = swap(shares[step], "box", step)
    return received


def on_device(
    leaf_out,
    interp_mid,
    shift_mid,
    trans_mid,
    list_mid,
    offset_mid,
    interp_top,
    shift_top,
    trans_top,
    list_top,
    offset_top,
):
    boxes = lax.axis_size("box")
    dirs = lax.axis_size("dir")
    box_index = lax.axis_index("box")
    octants = shift_mid.shape[0]
    leaves = leaf_out.shape[1]
    leaf_width, mid_width = interp_mid.shape
    own_mids = leaves // octants
    sector = trans_mid.shape[2]
    top_sector = interp_top.shape[2]
    top_width = trans_top.shape[3]
    mids = list_mid.shape[0]
    group_mids = mids // boxes
    tops = list_top.shape[0]
    group_tops = tops // boxes
    vmem = pl.BlockSpec(memory_space=pltpu.VMEM)
    smem = pl.BlockSpec(memory_space=pltpu.SMEM)
    hbm = pl.BlockSpec(memory_space=pl.ANY)
    top_height = 2 * top_width // LANES
    mid_height = 2 * sector // LANES

    chunk = sector * math.gcd(dirs, CHUNK_SECTORS)
    chunks = mid_width // chunk
    outgoing = pl.pallas_call(
        leaf_up,
        in_specs=[hbm, hbm, hbm],
        out_specs=vmem,
        out_shape=jax.ShapeDtypeStruct((dirs, 2 * own_mids, sector), jnp.bfloat16),
        scratch_shapes=[
            pltpu.VMEM((2 * leaves, leaf_width), jnp.bfloat16),
            pltpu.VMEM((octants, mid_width), jnp.float32),
            pltpu.VMEM((chunks, leaf_width, chunk), jnp.bfloat16),
            pltpu.SemaphoreType.DMA((2,)),
            pltpu.SemaphoreType.DMA((chunks,)),
        ],
        compiler_params=params(60),
        cost_estimate=cost(5),
        name="leaf_up",
    )(leaf_out.reshape(2 * leaves, leaf_width), interp_mid, shift_mid)
    mid_own = lax.all_to_all(outgoing, "dir", split_axis=0, concat_axis=0, tiled=True)

    list_width = list_mid.shape[1]
    top_index = [(list_top * (2 * top_height)).reshape(-1), (offset_top * top_height).reshape(-1)]
    own_list = lax.dynamic_slice_in_dim(list_mid, box_index * group_mids, group_mids, 0)
    own_offsets = lax.dynamic_slice_in_dim(offset_mid, box_index * group_mids, group_mids, 0)
    mid_index = [(own_list * (2 * mid_height)).reshape(-1), (own_offsets * mid_height).reshape(-1)]
    rows_top = rows_of(trans_top.reshape(2, -1, top_width))
    rows_mid = rows_of(trans_mid)
    table = jax.ShapeDtypeStruct((octants, top_sector), jnp.float32)
    cos_top, sin_top, table_top = pl.pallas_call(
        tables,
        in_specs=[vmem, hbm],
        out_specs=[vmem] * 3,
        out_shape=[table, table, jax.ShapeDtypeStruct(interp_top.shape, interp_top.dtype)],
        scratch_shapes=[pltpu.SemaphoreType.DMA],
        compiler_params=params(16),
        cost_estimate=cost(2),
        name="tables",
    )(shift_top, interp_top)
    ready = (mid_own, top_index, mid_index, rows_top, cos_top, sin_top, table_top)
    mid_own, top_index, mid_index, rows_top, cos_top, sin_top, table_top = lax.optimization_barrier(ready)

    share = jax.ShapeDtypeStruct((2 * dirs, top_width), jnp.bfloat16)
    top_out = pl.pallas_call(
        top_up,
        in_specs=[vmem] * 4,
        out_specs=[vmem] * boxes,
        out_shape=[share] * boxes,
        compiler_params=params(16),
        cost_estimate=cost(1),
        name="top_up",
    )(mid_own, table_top, cos_top, sin_top)
    top_all = exchange(top_out)

    groups = {0: follow(mid_own, top_out[0])}
    bits = [1 << k for k in reversed(range(boxes.bit_length() - 1))]
    for bit in bits:
        groups[bit] = swap(groups[0], "box", bit)

    top_in = pl.pallas_call(
        functools.partial(top_translate, list_width),
        in_specs=[hbm, hbm, vmem] + [vmem] * boxes,
        out_specs=[vmem] * boxes,
        out_shape=[share] * boxes,
        scratch_shapes=[
            pltpu.VMEM((2 * tops * top_height, LANES), jnp.float32),
            pltpu.VMEM((tops * top_height, LANES), jnp.float32),
            pltpu.VMEM((tops * top_height, LANES), jnp.float32),
            pltpu.SMEM(top_index[0].shape, jnp.int32),
            pltpu.SMEM(top_index[0].shape, jnp.int32),
            pltpu.SemaphoreType.DMA((4,)),
        ],
        compiler_params=params(16),
        cost_estimate=cost(15),
        name="top_translate",
    )(*top_index, rows_top, *top_all)
    top_back = exchange(top_in)

    for number, bit in enumerate(bits[1:], 1):
        for step in [step for step in groups if step and not step & (2 * bit - 1)]:
            values = follow(groups[step], top_in[0]) if number == 1 else groups[step]
            groups[step ^ bit] = swap(values, "box", bit)

    mid_far = pl.pallas_call(
        functools.partial(mid_translate, list_width),
        in_specs=[hbm, hbm, vmem] + [vmem] * boxes,
        out_specs=vmem,
        out_shape=jax.ShapeDtypeStruct((2, group_mids, sector), jnp.float32),
        scratch_shapes=[
            pltpu.VMEM((2 * mids * mid_height, LANES), jnp.float32),
            pltpu.VMEM((group_mids * mid_height, LANES), jnp.float32),
            pltpu.VMEM((group_mids * mid_height, LANES), jnp.float32),
            pltpu.SMEM(mid_index[0].shape, jnp.int32),
            pltpu.SMEM(mid_index[0].shape, jnp.int32),
            pltpu.SemaphoreType.DMA((4,)),
        ],
        compiler_params=params(16),
        cost_estimate=cost(1),
        name="mid_translate",
    )(*mid_index, rows_mid, *[groups[step] for step in range(boxes)])

    incoming = pl.pallas_call(
        functools.partial(top_down, sector / top_sector),
        in_specs=[vmem] * (4 + boxes),
        out_specs=vmem,
        out_shape=jax.ShapeDtypeStruct((dirs, 2 * own_mids, sector), jnp.bfloat16),
        compiler_params=params(16),
        cost_estimate=cost(1),
        name="top_down",
    )(table_top, cos_top, sin_top, mid_far, *top_back)
    mid_back = lax.all_to_all(incoming, "dir", split_axis=0, concat_axis=0, tiled=True)

    leaf_in = pl.pallas_call(
        functools.partial(leaf_down, leaf_width / mid_width),
        in_specs=[vmem] * 3,
        out_specs=vmem,
        out_shape=jax.ShapeDtypeStruct((2 * leaves, leaf_width), jnp.float32),
        scratch_shapes=[pltpu.VMEM((leaf_width, 2 * leaves), jnp.float32)],
        compiler_params=params(20),
        cost_estimate=cost(3),
        name="leaf_down",
    )(mid_back, interp_mid, shift_mid)
    return leaf_in.reshape(2, leaves, leaf_width)


def solution(mesh):
    return jax.shard_map(
        on_device,
        mesh=mesh,
        in_specs=(
            P(None, ("box", "dir"), None),
            P(),
            P(),
            P(None, None, "dir"),
            P(),
            P(),
            P("dir", None, None),
            P(None, "dir", None),
            P(None, None, "dir", "box"),
            P(),
            P(),
        ),
        out_specs=P(None, ("box", "dir"), None),
        check_vma=False,
    )
```

time: 64 us -> 56.9 us (0.89)
  waiting for transfers between devices: 12.8 us -> 2.82 us
  starting transfers between devices: 10.7 us -> 18.6 us
  Pallas kernels: 24 us -> 20.3 us
  local copies, waits for them, and re-layouts: 7.33 us -> 5.71 us
    ppermute x0 -> x9, starting transfers between devices: none -> 13.3 us  [swap(): return lax.ppermute(values, axis, [(k, k ^ step) for k in range(size)])]
    all_to_all x2 -> x1, waiting for transfers between devices: 12.8 us -> 1.06 us  [on_device(): lax.all_to_all(outgoing, 'dir', split_axis=0, concat_axis=0, tiled=True)]
    all_to_all x2 -> x1, starting transfers between devices: 10.7 us -> 5.32 us  [on_device(): lax.all_to_all(outgoing, 'dir', split_axis=0, concat_axis=0, tiled=True)]
    pallas_call x2 -> x6, Pallas kernels: 14.4 us -> 10.8 us  [the longest x1 6.43 us: on_device(): pl.pallas_call(functools.partial(mid_translate, list_width), in_specs=[hb...]
    ppermute x0 -> x9, waiting for transfers between devices: none -> 1.76 us  [swap(): return lax.ppermute(values, axis, [(k, k ^ step) for k in range(size)])]
    another operation x1, local copies, waits for them, and re-layouts: 2.13 us -> 0.67 us  [rows_of(): rows = jnp.transpose(trans.reshape(2, offsets, pieces, LANES), (1, 2, 0, 3))]
    unnamed x19 -> x28, local copies, waits for them, and re-layouts: 4.75 us -> 4.59 us
  transfers between devices with their start and end apart: 2 -> 10, of which waited for: 1 -> 3; matrix products, arithmetic and copies ran while one was open for 4% -> 2% of each run, Pallas kernels for 13% -> 18%
where the time goes in v3:
time: 56.9 us; the launch traced here: 56.5 us
  Pallas kernels  20.3 us (36%)
  starting transfers between devices  18.6 us (33%)
  blocking collectives  8.81 us (15%)
  local copies, waits for them, and re-layouts  5.71 us (10%)
  waiting for transfers between devices  2.82 us (5%)
    ppermute x9, starting transfers between devices, swap(): return lax.ppermute(values, axis, [(k, k ^ step) for k in range(size)])  13.3 us
    all_to_all x1, blocking collectives, on_device(): lax.all_to_all(incoming, 'dir', split_axis=0, concat_axis=0, tiled=True)  8.81 us
    pallas_call x1, Pallas kernels, on_device(): pl.pallas_call(functools.partial(mid_translate, list_width), in_specs=[hb...  6.43 us
    pallas_call x1, Pallas kernels, on_device(): pl.pallas_call(leaf_up, in_specs=[hbm, hbm, hbm], out_specs=vmem, out_sha...  5.41 us
    all_to_all x1, starting transfers between devices, on_device(): lax.all_to_all(outgoing, 'dir', split_axis=0, concat_axis=0, tiled=True)  5.32 us
    unnamed x28, local copies, waits for them, and re-layouts  4.59 us
    pallas_call x1, Pallas kernels, on_device(): pl.pallas_call(functools.partial(top_translate, list_width), in_specs=[hb...  3.46 us
    pallas_call x1, Pallas kernels, on_device(): pl.pallas_call(functools.partial(leaf_down, leaf_width / mid_width), in_s...  3.25 us
  transfers between devices with their start and end apart: 10, of which 3 were waited for; matrix products, arithmetic and copies ran while one was open for 2% of the time, Pallas kernels for 18%

profile of v3, /device:TPU:0, one launch (start us, length us, event | category | flops | bytes accessed | tf_op | source)
XLA Modules:
  0.0 56.5 jit_solution(2707431673405994499)
XLA Ops:
  0.0 5.4 %leaf_up.1 = bf16[8,16,512]{2,1,0:T(8,128)(2,1)} custom-call(bf16[128,1024]{1,0:T(8,128)(2,1)} %bitcast.16, bf16[1024,4096]{1,0:T(8,128)(2,1)} %table_ref.1, f32[8,4096]{1,0:T(8,128)} %shift_ref.3), custom_call_target="tpu_custom_call" | custom-call | flops 5750000128 | tf_op jit(solution)/shard_map/leaf_up/pallas_call | solution.py:335
  5.5 5.3 %all-to-all-start = ((bf16[8,16,512]{2,1,0:T(8,128)(2,1)}), bf16[8,16,512]{2,1,0:T(8,128)(2,1)S(1)}, u32[]{:S(2)}, u32[]{:S(2)}) async-start(bf16[8,16,512]{2,1,0:T(8,128)(2,1)} %leaf_up.1), calls=%async_computation | async-start | bytes 262144 | tf_op jit(solution)/shard_map/all_to_all | solution.py:351
  11.2 0.7 %copy.16 = f32[2,316,4,128]{3,0,2,1:T(2,128)S(1)} copy(f32[2,316,4,128]{3,2,1,0:T(4,128)S(1)} %bitcast.15) | data formatting | bytes 2588672 | tf_op jit(solution)/shard_map/reshape;reshape | solution.py:267
  12.1 1.6 %copy-done = bf16[1,512,2048]{2,1,0:T(8,128)(2,1)S(1)} copy-done((bf16[1,512,2048]{2,1,0:T(8,128)(2,1)S(1)}, bf16[1,512,2048]{2,1,0:T(8,128)(2,1)}, u32[]{:S(2)}) %copy-start) | copy-done | bytes 2097176
  13.7 0.2 tables.1
  13.9 1.3 %copy-done.4 = bf16[1,512,2048]{2,1,0:T(8,128)(2,1)} copy-done((bf16[1,512,2048]{2,1,0:T(8,128)(2,1)}, bf16[1,512,2048]{2,1,0:T(8,128)(2,1)S(1)}, u32[]{:S(2)}) %copy-start.4) | copy-done | bytes 2097176
  15.2 1.1 %all-to-all-done.mid_ref.values_ref = bf16[8,16,512]{2,1,0:T(8,128)(2,1)S(1)} async-done(((bf16[8,16,512]{2,1,0:T(8,128)(2,1)}), bf16[8,16,512]{2,1,0:T(8,128)(2,1)S(1)}, u32[]{:S(2)}, u32[]{:S(2)}) %all-to-all-start) | async-done | bytes 131104 | tf_op jit(solution)/shard_map/all_to_all | solution.py:351
  16.3 1.6 %copy-done.5 = bf16[1,512,2048]{2,1,0:T(8,128)(2,1)S(1)} copy-done((bf16[1,512,2048]{2,1,0:T(8,128)(2,1)S(1)}, bf16[1,512,2048]{2,1,0:T(8,128)(2,1)}, u32[]{:S(2)}) %copy-start.5) | copy-done | bytes 2097176
  17.9 0.6 %top_up.1 = (bf16[16,512]{1,0:T(8,128)(2,1)S(1)}, bf16[16,512]{1,0:T(8,128)(2,1)S(1)}, bf16[16,512]{1,0:T(8,128)(2,1)S(1)}, bf16[16,512]{1,0:T(8,128)(2,1)S(1)}) custom-call(bf16[8,16,512]{2,1,0:T(8,128)(2,1)S(1)} %all-to-all-done.mid_ref.values_ref, bf16[1,512,2048]{2,1,0:T(8,128)(2,1)S(1)} %copy-done.5, f32[8,2048]{1,0:T(8,128)S(1)} %get-tuple-element.29.cos_ref, ...), custom_call_target="tpu_custom_call" | custom-call | flops 1150000000 | tf_op jit(solution)/shard_map/top_up/pallas_call | solution.py:375
  18.6 1.6 %collective-permute-start.2 = (bf16[16,512]{1,0:T(8,128)(2,1)S(1)}, bf16[16,512]{1,0:T(8,128)(2,1)S(1)}, u32[]{:S(2)}, u32[]{:S(2)}) collective-permute-start(bf16[16,512]{1,0:T(8,128)(2,1)S(1)} %get-tuple-element.38), channel_id=1, source_target_pairs={{0,8},{8,0},{16,24},{24,16},{1,9},{9,1},{17,25},{25,17},{2,10},{10... | collective-permute-start | bytes 49160 | tf_op jit(solution)/shard_map/ppermute | solution.py:273
  20.2 2.6 %collective-permute-start.3 = (bf16[16,512]{1,0:T(8,128)(2,1)S(1)}, bf16[16,512]{1,0:T(8,128)(2,1)S(1)}, u32[]{:S(2)}, u32[]{:S(2)}) collective-permute-start(bf16[16,512]{1,0:T(8,128)(2,1)S(1)} %get-tuple-element.39), channel_id=1, source_target_pairs={{0,16},{8,24},{16,0},{24,8},{1,17},{9,25},{17,1},{25,9},{2,18},{10... | collective-permute-start | bytes 49160 | tf_op jit(solution)/shard_map/ppermute | solution.py:273
  22.8 0.2 collective-permute-start.4
  23.0 1.8 %collective-permute-start.1 = (bf16[8,16,512]{2,1,0:T(8,128)(2,1)S(1)}, bf16[8,16,512]{2,1,0:T(8,128)(2,1)S(1)}, u32[]{:S(2)}, u32[]{:S(2)}) collective-permute-start(bf16[8,16,512]{2,1,0:T(8,128)(2,1)S(1)} %pass_on.2.rest_0_), channel_id=1, source_target_pairs={{0,16},{8,24},{16,0},{24,8},{1,17},{9,25},{17,1},{25,9},{2,18},{10... | collective-permute-start | bytes 393224 | tf_op jit(solution)/shard_map/ppermute | solution.py:273
  24.8 2.5 %collective-permute-start = (bf16[8,16,512]{2,1,0:T(8,128)(2,1)S(1)}, bf16[8,16,512]{2,1,0:T(8,128)(2,1)S(1)}, u32[]{:S(2)}, u32[]{:S(2)}) collective-permute-start(bf16[8,16,512]{2,1,0:T(8,128)(2,1)S(1)} %pass_on.2.rest_0_), channel_id=1, source_target_pairs={{0,8},{8,0},{16,24},{24,16},{1,9},{9,1},{17,25},{25,17},{2,10},{10... | collective-permute-start | bytes 393224 | tf_op jit(solution)/shard_map/ppermute | solution.py:273
  27.3 1.3 %collective-permute-done.4.rest_3_ = bf16[16,512]{1,0:T(8,128)(2,1)S(1)} collective-permute-done((bf16[16,512]{1,0:T(8,128)(2,1)S(1)}, bf16[16,512]{1,0:T(8,128)(2,1)S(1)}, u32[]{:S(2)}, u32[]{:S(2)}) %collective-permute-start.4) | collective-permute-done | bytes 16416 | tf_op jit(solution)/shard_map/ppermute | solution.py:273
  28.6 3.5 %top_translate.1 = (bf16[16,512]{1,0:T(8,128)(2,1)S(1)}, bf16[16,512]{1,0:T(8,128)(2,1)S(1)}, bf16[16,512]{1,0:T(8,128)(2,1)S(1)}, bf16[16,512]{1,0:T(8,128)(2,1)S(1)}) custom-call(s32[2048]{0:T(1024)S(1)} %reshape.28.source_hbm, s32[2048]{0:T(1024)S(1)} %reshape.29.offset_hbm, f32[2528,128]{1,0:T(8,128)S(1)} %bitcast.11, ...), custom_call_target="tpu_custom_call" | custom-call | flops 17250000896 | tf_op jit(solution)/shard_map/top_translate/pallas_call | solution.py:391
  32.2 1.9 %collective-permute-start.6 = (bf16[16,512]{1,0:T(8,128)(2,1)S(1)}, bf16[16,512]{1,0:T(8,128)(2,1)S(1)}, u32[]{:S(2)}, u32[]{:S(2)}) collective-permute-start(bf16[16,512]{1,0:T(8,128)(2,1)S(1)} %get-tuple-element.42), channel_id=1, source_target_pairs={{0,8},{8,0},{16,24},{24,16},{1,9},{9,1},{17,25},{25,17},{2,10},{10... | collective-permute-start | bytes 49160 | tf_op jit(solution)/shard_map/ppermute | solution.py:273
  34.1 0.6 %collective-permute-start.7 = (bf16[16,512]{1,0:T(8,128)(2,1)S(1)}, bf16[16,512]{1,0:T(8,128)(2,1)S(1)}, u32[]{:S(2)}, u32[]{:S(2)}) collective-permute-start(bf16[16,512]{1,0:T(8,128)(2,1)S(1)} %get-tuple-element.43), channel_id=1, source_target_pairs={{0,16},{8,24},{16,0},{24,8},{1,17},{9,25},{17,1},{25,9},{2,18},{10... | collective-permute-start | bytes 49160 | tf_op jit(solution)/shard_map/ppermute | solution.py:273
  34.7 1.9 %collective-permute-start.8 = (bf16[16,512]{1,0:T(8,128)(2,1)S(1)}, bf16[16,512]{1,0:T(8,128)(2,1)S(1)}, u32[]{:S(2)}, u32[]{:S(2)}) collective-permute-start(bf16[16,512]{1,0:T(8,128)(2,1)S(1)} %get-tuple-element.44), channel_id=1, source_target_pairs={{0,24},{8,16},{16,8},{24,0},{1,25},{9,17},{17,9},{25,1},{2,26},{10... | collective-permute-start | bytes 49160 | tf_op jit(solution)/shard_map/ppermute | solution.py:273
  36.6 0.4 collective-permute-done.5.rest_3_
  37.1 6.4 %mid_translate.1.far_ref = f32[2,64,512]{2,1,0:T(8,128)S(1)} custom-call(s32[4096]{0:T(1024)S(1)} %reshape.30.source_hbm, s32[4096]{0:T(1024)S(1)} %reshape.31.offset_hbm, f32[2528,128]{1,0:T(8,128)S(1)} %bitcast.14, bf16[8,16,512]{2,1,0:T(8,128)(2,1)S(1)} %pass_on.2.rest_0_, bf16[8,16,512]{2,1,0:T(8,128)(2,1)S(1)} %collective-permute-done.rest_1_, ...), custom_call_target="tpu_custom_call" | custom-call | flops 1150000000 | tf_op jit(solution)/shard_map/mid_translate/pallas_call | solution.py:415
  43.6 0.8 %top_down.1 = bf16[8,16,512]{2,1,0:T(8,128)(2,1)S(1)} custom-call(bf16[1,512,2048]{2,1,0:T(8,128)(2,1)S(1)} %copy-done.6, f32[8,2048]{1,0:T(8,128)S(1)} %get-tuple-element.29.cos_ref, f32[8,2048]{1,0:T(8,128)S(1)} %get-tuple-element.30.sin_ref, f32[2,64,512]{2,1,0:T(8,128)S(1)} %mid_translate.1.far_ref, ...), custom_call_target="tpu_custom_call" | custom-call | flops 1150000000 | tf_op jit(solution)/shard_map/top_down/pallas_call | solution.py:433
  44.4 8.8 %all_to_all.10.mid_ref = bf16[8,16,512]{2,1,0:T(8,128)(2,1)S(1)} all-to-all(bf16[8,16,512]{2,1,0:T(8,128)(2,1)S(1)} %top_down.1), channel_id=1, replica_groups=mesh['box'=4,'dir'=8] {'dir'}, dimensions={0} | all-to-all | bytes 262144 | tf_op jit(solution)/shard_map/all_to_all | solution.py:442
  53.3 3.2 %leaf_down.1 = f32[128,1024]{1,0:T(8,128)} custom-call(bf16[8,16,512]{2,1,0:T(8,128)(2,1)S(1)} %all_to_all.10.mid_ref, bf16[1024,4096]{1,0:T(8,128)(2,1)S(1)} %bitcast.13, f32[8,4096]{1,0:T(8,128)S(1)} %copy-done.2), custom_call_target="tpu_custom_call" | custom-call | flops 3449999872 | tf_op jit(solution)/shard_map/leaf_down/pallas_call | solution.py:444
  (45 shorter events, 0.8 us)
Async XLA Ops:
  0.0 10.8 %copy-start.10 = (s32[256,64]{0,1:T(8,128)S(1)}, s32[256,64]{0,1:T(8,128)}, u32[]{:S(2)}) copy-start(s32[256,64]{0,1:T(8,128)} %param.16) | copy-start | bytes 196612
  0.0 10.8 %copy-start.11 = (s32[256,64]{0,1:T(8,128)S(1)}, s32[256,64]{0,1:T(8,128)}, u32[]{:S(2)}) copy-start(s32[256,64]{0,1:T(8,128)} %param.15) | copy-start | bytes 196612
  0.0 11.2 %copy-start.7 = (f32[2,316,1,512]{3,2,1,0:T(1,128)S(1)}, f32[2,316,1,512]{3,2,1,0:T(1,128)}, u32[]{:S(2)}) copy-start(f32[2,316,1,512]{3,2,1,0:T(1,128)} %param.19) | copy-start | bytes 3883012
  5.4 6.5 %copy-start.8 = (s32[32,64]{1,0:T(8,128)S(1)}, s32[32,64]{1,0:T(8,128)}, u32[]{:S(2)}) copy-start(s32[32,64]{1,0:T(8,128)} %param.20) | copy-start | bytes 24580
  5.4 6.5 %copy-start.9 = (s32[32,64]{1,0:T(8,128)S(1)}, s32[32,64]{1,0:T(8,128)}, u32[]{:S(2)}) copy-start(s32[32,64]{1,0:T(8,128)} %param.21) | copy-start | bytes 24580
  5.4 6.6 %copy-start.3 = (f32[8,1,2048]{2,1,0:T(1,128)S(1)}, f32[8,1,2048]{2,1,0:T(1,128)}, u32[]{:S(2)}) copy-start(f32[8,1,2048]{2,1,0:T(1,128)} %shift_ref.2) | copy-start | bytes 196612
  5.5 10.9 %all-to-all-start = ((bf16[8,16,512]{2,1,0:T(8,128)(2,1)}), bf16[8,16,512]{2,1,0:T(8,128)(2,1)S(1)}, u32[]{:S(2)}, u32[]{:S(2)}) async-start(bf16[8,16,512]{2,1,0:T(8,128)(2,1)} %leaf_up.1), calls=%async_computation | async-start | bytes 262144 | tf_op jit(solution)/shard_map/all_to_all | solution.py:351
  12.1 1.6 %copy-start = (bf16[1,512,2048]{2,1,0:T(8,128)(2,1)S(1)}, bf16[1,512,2048]{2,1,0:T(8,128)(2,1)}, u32[]{:S(2)}) copy-start(bf16[1,512,2048]{2,1,0:T(8,128)(2,1)} %table_hbm.3) | copy-start | bytes 6291460
  13.9 1.4 %copy-start.4 = (bf16[1,512,2048]{2,1,0:T(8,128)(2,1)}, bf16[1,512,2048]{2,1,0:T(8,128)(2,1)S(1)}, u32[]{:S(2)}) copy-start(bf16[1,512,2048]{2,1,0:T(8,128)(2,1)S(1)} %get-tuple-element.28.table_ref) | copy-start | bytes 6291460
  16.3 1.6 %copy-start.5 = (bf16[1,512,2048]{2,1,0:T(8,128)(2,1)S(1)}, bf16[1,512,2048]{2,1,0:T(8,128)(2,1)}, u32[]{:S(2)}) copy-start(bf16[1,512,2048]{2,1,0:T(8,128)(2,1)} %copy-done.4) | copy-start | bytes 6291460
  17.9 35.4 %slice-start = ((s8[8388608]{0:T(1024)(128)(4,1)}), s8[4194304]{0:T(1024)(128)(4,1)S(1)}, s32[]{:S(2)}) async-start(s8[8388608]{0:T(1024)(128)(4,1)} %bitcast.12), calls=%async_computation.2 | async-start | bytes 8388608
  18.6 8.7 %collective-permute-start.2 = (bf16[16,512]{1,0:T(8,128)(2,1)S(1)}, bf16[16,512]{1,0:T(8,128)(2,1)S(1)}, u32[]{:S(2)}, u32[]{:S(2)}) collective-permute-start(bf16[16,512]{1,0:T(8,128)(2,1)S(1)} %get-tuple-element.38), channel_id=1, source_target_pairs={{0,8},{8,0},{16,24},{24,16},{1,9},{9,1},{17,25},{25,17},{2,10},{10... | collective-permute-start | bytes 49160 | tf_op jit(solution)/shard_map/ppermute | solution.py:273
  20.2 7.1 %collective-permute-start.3 = (bf16[16,512]{1,0:T(8,128)(2,1)S(1)}, bf16[16,512]{1,0:T(8,128)(2,1)S(1)}, u32[]{:S(2)}, u32[]{:S(2)}) collective-permute-start(bf16[16,512]{1,0:T(8,128)(2,1)S(1)} %get-tuple-element.39), channel_id=1, source_target_pairs={{0,16},{8,24},{16,0},{24,8},{1,17},{9,25},{17,1},{25,9},{2,18},{10... | collective-permute-start | bytes 49160 | tf_op jit(solution)/shard_map/ppermute | solution.py:273
  22.8 5.8 %collective-permute-start.4 = (bf16[16,512]{1,0:T(8,128)(2,1)S(1)}, bf16[16,512]{1,0:T(8,128)(2,1)S(1)}, u32[]{:S(2)}, u32[]{:S(2)}) collective-permute-start(bf16[16,512]{1,0:T(8,128)(2,1)S(1)} %get-tuple-element.40), channel_id=1, source_target_pairs={{0,24},{8,16},{16,8},{24,0},{1,25},{9,17},{17,9},{25,1},{2,26},{10... | collective-permute-start | bytes 49160 | tf_op jit(solution)/shard_map/ppermute | solution.py:273
  23.0 14.1 %copy-start.1 = (f32[2,316,512]{2,0,1:T(2,128)S(1)}, f32[2,316,512]{2,0,1:T(2,128)}, u32[]{:S(2)}) copy-start(f32[2,316,512]{2,0,1:T(2,128)} %param.14) | copy-start | bytes 3883012
  23.0 30.2 %slice-start.1 = ((s8[8388608]{0:T(1024)(128)(4,1)}), s8[4194304]{0:T(1024)(128)(4,1)S(1)}, s32[]{:S(2)}) async-start(s8[8388608]{0:T(1024)(128)(4,1)} %bitcast.12), calls=%async_computation.3 | async-start | bytes 8388608
  23.0 9.0 %collective-permute-start.1 = (bf16[8,16,512]{2,1,0:T(8,128)(2,1)S(1)}, bf16[8,16,512]{2,1,0:T(8,128)(2,1)S(1)}, u32[]{:S(2)}, u32[]{:S(2)}) collective-permute-start(bf16[8,16,512]{2,1,0:T(8,128)(2,1)S(1)} %pass_on.2.rest_0_), channel_id=1, source_target_pairs={{0,16},{8,24},{16,0},{24,8},{1,17},{9,25},{17,1},{25,9},{2,18},{10... | collective-permute-start | bytes 393224 | tf_op jit(solution)/shard_map/ppermute | solution.py:273
  24.8 11.8 %collective-permute-start = (bf16[8,16,512]{2,1,0:T(8,128)(2,1)S(1)}, bf16[8,16,512]{2,1,0:T(8,128)(2,1)S(1)}, u32[]{:S(2)}, u32[]{:S(2)}) collective-permute-start(bf16[8,16,512]{2,1,0:T(8,128)(2,1)S(1)} %pass_on.2.rest_0_), channel_id=1, source_target_pairs={{0,8},{8,0},{16,24},{24,16},{1,9},{9,1},{17,25},{25,17},{2,10},{10... | collective-permute-start | bytes 393224 | tf_op jit(solution)/shard_map/ppermute | solution.py:273
  32.1 5.0 %collective-permute-start.5 = (bf16[8,16,512]{2,1,0:T(8,128)(2,1)S(1)}, bf16[8,16,512]{2,1,0:T(8,128)(2,1)S(1)}, u32[]{:S(2)}, u32[]{:S(2)}) collective-permute-start(bf16[8,16,512]{2,1,0:T(8,128)(2,1)S(1)} %pass_on.3), channel_id=1, source_target_pairs={{0,8},{8,0},{16,24},{24,16},{1,9},{9,1},{17,25},{25,17},{2,10},{10... | collective-permute-start | bytes 393224 | tf_op jit(solution)/shard_map/ppermute | solution.py:273
  32.2 11.3 %collective-permute-start.6 = (bf16[16,512]{1,0:T(8,128)(2,1)S(1)}, bf16[16,512]{1,0:T(8,128)(2,1)S(1)}, u32[]{:S(2)}, u32[]{:S(2)}) collective-permute-start(bf16[16,512]{1,0:T(8,128)(2,1)S(1)} %get-tuple-element.42), channel_id=1, source_target_pairs={{0,8},{8,0},{16,24},{24,16},{1,9},{9,1},{17,25},{25,17},{2,10},{10... | collective-permute-start | bytes 49160 | tf_op jit(solution)/shard_map/ppermute | solution.py:273
  34.1 9.4 %collective-permute-start.7 = (bf16[16,512]{1,0:T(8,128)(2,1)S(1)}, bf16[16,512]{1,0:T(8,128)(2,1)S(1)}, u32[]{:S(2)}, u32[]{:S(2)}) collective-permute-start(bf16[16,512]{1,0:T(8,128)(2,1)S(1)} %get-tuple-element.43), channel_id=1, source_target_pairs={{0,16},{8,24},{16,0},{24,8},{1,17},{9,25},{17,1},{25,9},{2,18},{10... | collective-permute-start | bytes 49160 | tf_op jit(solution)/shard_map/ppermute | solution.py:273
  34.7 8.8 %collective-permute-start.8 = (bf16[16,512]{1,0:T(8,128)(2,1)S(1)}, bf16[16,512]{1,0:T(8,128)(2,1)S(1)}, u32[]{:S(2)}, u32[]{:S(2)}) collective-permute-start(bf16[16,512]{1,0:T(8,128)(2,1)S(1)} %get-tuple-element.44), channel_id=1, source_target_pairs={{0,24},{8,16},{16,8},{24,0},{1,25},{9,17},{17,9},{25,1},{2,26},{10... | collective-permute-start | bytes 49160 | tf_op jit(solution)/shard_map/ppermute | solution.py:273
  37.1 6.5 %copy-start.6 = (bf16[1,512,2048]{2,1,0:T(8,128)(2,1)S(1)}, bf16[1,512,2048]{2,1,0:T(8,128)(2,1)}, u32[]{:S(2)}) copy-start(bf16[1,512,2048]{2,1,0:T(8,128)(2,1)} %copy-done.4) | copy-start | bytes 6291460
  43.5 9.7 %copy-start.2 = (f32[8,4096]{1,0:T(8,128)S(1)}, f32[8,4096]{1,0:T(8,128)}, u32[]{:S(2)}) copy-start(f32[8,4096]{1,0:T(8,128)} %shift_ref.3) | copy-start | bytes 393220

commit v4 on v3

--- a/solution.py
+++ b/solution.py
@@ -11,6 +11,7 @@
 SINE = (1.0, -0.16666647791862488, 0.00833289884030819, -0.0001980085507966578, 2.5904087124217767e-06)
 COSINE = (1.0, -0.5, 0.04166663438081741, -0.0013888360699638724, 2.476012559782248e-05, -2.6050881274386484e-07)
 HEAD_ROWS = 4
+UNROLL = 4
 LANES = 128
 ROWS = 8
 AHEAD = 2
@@ -92,7 +93,7 @@
     source_ref, offset_ref = index_refs
 
     def rows_at(step, carry):
-        for row in (2 * step, 2 * step + 1):
+        for row in [UNROLL * step + k for k in range(UNROLL)]:
             same = jnp.zeros((height, LANES), jnp.float32)
             cross = jnp.zeros((height, LANES), jnp.float32)
             for entry in range(list_width):
@@ -106,7 +107,7 @@
             cross_ref[place, :] = cross
         return carry
 
-    lax.fori_loop(first_row // 2, end_row // 2, rows_at, 0)
+    lax.fori_loop(first_row // UNROLL, end_row // UNROLL, rows_at, 0)
 
 
 def gather_rows(same_ref, cross_ref, first, height):
@@ -119,11 +120,8 @@
     return jnp.concatenate(real, axis=1), jnp.concatenate(imag, axis=1)
 
 
-def tables(shift_ref, table_hbm, cos_ref, sin_ref, table_ref, sem):
-    table_copy = pltpu.make_async_copy(table_hbm, table_ref, sem)
-    table_copy.start()
+def tables(shift_ref, cos_ref, sin_ref):
     cos_ref[...], sin_ref[...] = phase(shift_ref[:, 0, :])
-    table_copy.wait()
 
 
 def place_of(step):
@@ -146,14 +144,17 @@
         out_ref[...] = jnp.concatenate([new_real, new_imag], axis=0).astype(out_ref.dtype)
 
 
-def top_translate(list_width, source_hbm, offset_hbm, trans_ref, *rest):
-    count = (len(rest) - 6) // 2
+def top_translate(list_width, source_hbm, offset_hbm, plane_ref, *rest):
+    count = (len(rest) - 7) // 2
     top_refs, out_refs = rest[:count], rest[count : 2 * count]
-    pattern_ref, same_ref, cross_ref, *index_refs, sems = rest[2 * count :]
+    trans_ref, pattern_ref, same_ref, cross_ref, *index_refs, sems = rest[2 * count :]
     head = HEAD_ROWS * list_width
     first_copies, later_copies = index_copies((source_hbm, offset_hbm), index_refs, sems, head)
     for copy in first_copies + later_copies:
         copy.start()
+    plane = plane_ref.shape[0] // 2
+    for part in range(2):
+        trans_ref[pl.ds(part, plane, stride=2), :] = plane_ref[part * plane : (part + 1) * plane, :]
     own, width = top_refs[0].shape
     own = own // 2
     height = 2 * width // LANES
@@ -355,21 +356,20 @@
     own_list = lax.dynamic_slice_in_dim(list_mid, box_index * group_mids, group_mids, 0)
     own_offsets = lax.dynamic_slice_in_dim(offset_mid, box_index * group_mids, group_mids, 0)
     mid_index = [(own_list * (2 * mid_height)).reshape(-1), (own_offsets * mid_height).reshape(-1)]
-    rows_top = rows_of(trans_top.reshape(2, -1, top_width))
+    rows_top = trans_top.reshape(-1, LANES)
     rows_mid = rows_of(trans_mid)
     table = jax.ShapeDtypeStruct((octants, top_sector), jnp.float32)
-    cos_top, sin_top, table_top = pl.pallas_call(
+    cos_top, sin_top = pl.pallas_call(
         tables,
-        in_specs=[vmem, hbm],
-        out_specs=[vmem] * 3,
-        out_shape=[table, table, jax.ShapeDtypeStruct(interp_top.shape, interp_top.dtype)],
-        scratch_shapes=[pltpu.SemaphoreType.DMA],
+        in_specs=[vmem],
+        out_specs=[vmem] * 2,
+        out_shape=[table, table],
         compiler_params=params(16),
         cost_estimate=cost(2),
         name="tables",
-    )(shift_top, interp_top)
-    ready = (mid_own, top_index, mid_index, rows_top, cos_top, sin_top, table_top)
-    mid_own, top_index, mid_index, rows_top, cos_top, sin_top, table_top = lax.optimization_barrier(ready)
+    )(shift_top)
+    ready = (mid_own, top_index, mid_index, cos_top, sin_top)
+    mid_own, top_index, mid_index, cos_top, sin_top = lax.optimization_barrier(ready)
 
     share = jax.ShapeDtypeStruct((2 * dirs, top_width), jnp.bfloat16)
     top_out = pl.pallas_call(
@@ -378,9 +378,9 @@
         out_specs=[vmem] * boxes,
         out_shape=[share] * boxes,
         compiler_params=params(16),
-        cost_estimate=cost(1),
+        cost_estimate=cost(4),
         name="top_up",
-    )(mid_own, table_top, cos_top, sin_top)
+    )(mid_own, interp_top, cos_top, sin_top)
     top_all = exchange(top_out)
 
     groups = {0: follow(mid_own, top_out[0])}
@@ -394,6 +394,7 @@
         out_specs=[vmem] * boxes,
         out_shape=[share] * boxes,
         scratch_shapes=[
+            pltpu.VMEM(rows_top.shape, jnp.float32),
             pltpu.VMEM((2 * tops * top_height, LANES), jnp.float32),
             pltpu.VMEM((tops * top_height, LANES), jnp.float32),
             pltpu.VMEM((tops * top_height, LANES), jnp.float32),
@@ -438,7 +439,7 @@
         compiler_params=params(16),
         cost_estimate=cost(1),
         name="top_down",
-    )(table_top, cos_top, sin_top, mid_far, *top_back)
+    )(interp_top, cos_top, sin_top, mid_far, *top_back)
     mid_back = lax.all_to_all(incoming, "dir", split_axis=0, concat_axis=0, tiled=True)
 
     leaf_in = pl.pallas_call(

time: 56.9 us -> 53.9 us (0.947)
  local copies, waits for them, and re-layouts: 5.71 us -> 0.5 us
  waiting for transfers between devices: 2.82 us -> 6.63 us
  blocking collectives: 8.81 us -> 7.92 us
    unnamed x28 -> x22, local copies, waits for them, and re-layouts: 4.59 us -> 0.04 us
    all_to_all x1, waiting for transfers between devices: 1.06 us -> 4.85 us  [on_device(): lax.all_to_all(outgoing, 'dir', split_axis=0, concat_axis=0, tiled=True)]
    all_to_all x1, blocking collectives: 8.81 us -> 7.92 us  [on_device(): lax.all_to_all(incoming, 'dir', split_axis=0, concat_axis=0, tiled=True)]
    another operation x1 -> x0, local copies, waits for them, and re-layouts: 0.67 us -> none  [rows_of(): rows = jnp.transpose(trans.reshape(2, offsets, pieces, LANES), (1, 2, 0, 3))]
  transfers between devices with their start and end apart: 10 -> 10, of which waited for: 3 -> 3; matrix products, arithmetic and copies ran while one was open for 2% -> 1% of each run, Pallas kernels for 18% -> 18%
where the time goes in v4:
time: 53.9 us; the launch traced here: 53.7 us
  Pallas kernels  19.9 us (37%)
  starting transfers between devices  18.5 us (34%)
  blocking collectives  7.92 us (15%)
  waiting for transfers between devices  6.63 us (12%)
    ppermute x9, starting transfers between devices, swap(): return lax.ppermute(values, axis, [(k, k ^ step) for k in range(size)])  13.3 us
    all_to_all x1, blocking collectives, on_device(): lax.all_to_all(incoming, 'dir', split_axis=0, concat_axis=0, tiled=True)  7.92 us
    pallas_call x1, Pallas kernels, on_device(): pl.pallas_call(functools.partial(mid_translate, list_width), in_specs=[hb...  6.34 us
    pallas_call x1, Pallas kernels, on_device(): pl.pallas_call(leaf_up, in_specs=[hbm, hbm, hbm], out_specs=vmem, out_sha...  5.35 us
    all_to_all x1, starting transfers between devices, on_device(): lax.all_to_all(outgoing, 'dir', split_axis=0, concat_axis=0, tiled=True)  5.21 us
    all_to_all x1, waiting for transfers between devices, on_device(): lax.all_to_all(outgoing, 'dir', split_axis=0, concat_axis=0, tiled=True)  4.85 us
    pallas_call x1, Pallas kernels, on_device(): pl.pallas_call(functools.partial(top_translate, list_width), in_specs=[hb...  3.35 us
    pallas_call x1, Pallas kernels, on_device(): pl.pallas_call(functools.partial(leaf_down, leaf_width / mid_width), in_s...  3.25 us
  transfers between devices with their start and end apart: 10, of which 3 were waited for; matrix products, arithmetic and copies ran while one was open for 1% of the time, Pallas kernels for 18%

profile of v4, /device:TPU:0, one launch (start us, length us, event | category | flops | bytes accessed | tf_op | source)
XLA Modules:
  0.0 53.7 jit_solution(6212935427415181188)
XLA Ops:
  0.0 5.3 %leaf_up.1 = bf16[8,16,512]{2,1,0:T(8,128)(2,1)} custom-call(bf16[128,1024]{1,0:T(8,128)(2,1)} %bitcast.12, bf16[1024,4096]{1,0:T(8,128)(2,1)} %table_ref.5, f32[8,4096]{1,0:T(8,128)} %shift_ref.3), custom_call_target="tpu_custom_call" | custom-call | flops 5750000128 | tf_op jit(solution)/shard_map/leaf_up/pallas_call | solution.py:336
  5.4 5.2 %all-to-all-start = ((bf16[8,16,512]{2,1,0:T(8,128)(2,1)}), bf16[8,16,512]{2,1,0:T(8,128)(2,1)S(1)}, u32[]{:S(2)}, u32[]{:S(2)}) async-start(bf16[8,16,512]{2,1,0:T(8,128)(2,1)} %leaf_up.1), calls=%async_computation | async-start | bytes 262144 | tf_op jit(solution)/shard_map/all_to_all | solution.py:352
  10.8 0.1 dynamic-slice_multiply_fusion
  10.9 0.1 reshape.31.offset_hbm
  11.1 0.1 reshape.30.source_hbm
  11.2 0.1 tables.1
  11.3 4.9 %all-to-all-done.mid_ref.values_ref = bf16[8,16,512]{2,1,0:T(8,128)(2,1)S(1)} async-done(((bf16[8,16,512]{2,1,0:T(8,128)(2,1)}), bf16[8,16,512]{2,1,0:T(8,128)(2,1)S(1)}, u32[]{:S(2)}, u32[]{:S(2)}) %all-to-all-start) | async-done | bytes 131104 | tf_op jit(solution)/shard_map/all_to_all | solution.py:352
  16.1 0.6 %top_up.1 = (bf16[16,512]{1,0:T(8,128)(2,1)S(1)}, bf16[16,512]{1,0:T(8,128)(2,1)S(1)}, bf16[16,512]{1,0:T(8,128)(2,1)S(1)}, bf16[16,512]{1,0:T(8,128)(2,1)S(1)}) custom-call(bf16[8,16,512]{2,1,0:T(8,128)(2,1)S(1)} %all-to-all-done.mid_ref.values_ref, bf16[1,512,2048]{2,1,0:T(8,128)(2,1)S(1)} %copy-done, f32[8,2048]{1,0:T(8,128)S(1)} %get-tuple-element.24.cos_ref, ...), custom_call_target="tpu_custom_call" | custom-call | flops 4600000000 | tf_op jit(solution)/shard_map/top_up/pallas_call | solution.py:375
  16.8 1.6 %collective-permute-start.2 = (bf16[16,512]{1,0:T(8,128)(2,1)S(1)}, bf16[16,512]{1,0:T(8,128)(2,1)S(1)}, u32[]{:S(2)}, u32[]{:S(2)}) collective-permute-start(bf16[16,512]{1,0:T(8,128)(2,1)S(1)} %get-tuple-element.32), channel_id=1, source_target_pairs={{0,8},{8,0},{16,24},{24,16},{1,9},{9,1},{17,25},{25,17},{2,10},{10... | collective-permute-start | bytes 49160 | tf_op jit(solution)/shard_map/ppermute | solution.py:274
  18.4 2.6 %collective-permute-start.3 = (bf16[16,512]{1,0:T(8,128)(2,1)S(1)}, bf16[16,512]{1,0:T(8,128)(2,1)S(1)}, u32[]{:S(2)}, u32[]{:S(2)}) collective-permute-start(bf16[16,512]{1,0:T(8,128)(2,1)S(1)} %get-tuple-element.33), channel_id=1, source_target_pairs={{0,16},{8,24},{16,0},{24,8},{1,17},{9,25},{17,1},{25,9},{2,18},{10... | collective-permute-start | bytes 49160 | tf_op jit(solution)/shard_map/ppermute | solution.py:274
  21.0 0.2 collective-permute-start.4
  21.2 1.7 %collective-permute-start.1 = (bf16[8,16,512]{2,1,0:T(8,128)(2,1)S(1)}, bf16[8,16,512]{2,1,0:T(8,128)(2,1)S(1)}, u32[]{:S(2)}, u32[]{:S(2)}) collective-permute-start(bf16[8,16,512]{2,1,0:T(8,128)(2,1)S(1)} %pass_on.2.rest_0_), channel_id=1, source_target_pairs={{0,16},{8,24},{16,0},{24,8},{1,17},{9,25},{17,1},{25,9},{2,18},{10... | collective-permute-start | bytes 393224 | tf_op jit(solution)/shard_map/ppermute | solution.py:274
  23.0 2.5 %collective-permute-start = (bf16[8,16,512]{2,1,0:T(8,128)(2,1)S(1)}, bf16[8,16,512]{2,1,0:T(8,128)(2,1)S(1)}, u32[]{:S(2)}, u32[]{:S(2)}) collective-permute-start(bf16[8,16,512]{2,1,0:T(8,128)(2,1)S(1)} %pass_on.2.rest_0_), channel_id=1, source_target_pairs={{0,8},{8,0},{16,24},{24,16},{1,9},{9,1},{17,25},{25,17},{2,10},{10... | collective-permute-start | bytes 393224 | tf_op jit(solution)/shard_map/ppermute | solution.py:274
  25.5 1.3 %collective-permute-done.4.rest_3_ = bf16[16,512]{1,0:T(8,128)(2,1)S(1)} collective-permute-done((bf16[16,512]{1,0:T(8,128)(2,1)S(1)}, bf16[16,512]{1,0:T(8,128)(2,1)S(1)}, u32[]{:S(2)}, u32[]{:S(2)}) %collective-permute-start.4) | collective-permute-done | bytes 16416 | tf_op jit(solution)/shard_map/ppermute | solution.py:274
  26.8 3.4 %top_translate.1 = (bf16[16,512]{1,0:T(8,128)(2,1)S(1)}, bf16[16,512]{1,0:T(8,128)(2,1)S(1)}, bf16[16,512]{1,0:T(8,128)(2,1)S(1)}, bf16[16,512]{1,0:T(8,128)(2,1)S(1)}) custom-call(s32[2048]{0:T(1024)S(1)} %reshape.28.source_hbm, s32[2048]{0:T(1024)S(1)} %reshape.29.offset_hbm, f32[2528,128]{1,0:T(8,128)S(1)} %bitcast.10, ...), custom_call_target="tpu_custom_call" | custom-call | flops 17250000896 | tf_op jit(solution)/shard_map/top_translate/pallas_call | solution.py:391
  30.2 0.2 collective-permute-start.5
  30.4 1.9 %collective-permute-start.6 = (bf16[16,512]{1,0:T(8,128)(2,1)S(1)}, bf16[16,512]{1,0:T(8,128)(2,1)S(1)}, u32[]{:S(2)}, u32[]{:S(2)}) collective-permute-start(bf16[16,512]{1,0:T(8,128)(2,1)S(1)} %get-tuple-element.36), channel_id=1, source_target_pairs={{0,8},{8,0},{16,24},{24,16},{1,9},{9,1},{17,25},{25,17},{2,10},{10... | collective-permute-start | bytes 49160 | tf_op jit(solution)/shard_map/ppermute | solution.py:274
  32.3 0.7 %collective-permute-start.7 = (bf16[16,512]{1,0:T(8,128)(2,1)S(1)}, bf16[16,512]{1,0:T(8,128)(2,1)S(1)}, u32[]{:S(2)}, u32[]{:S(2)}) collective-permute-start(bf16[16,512]{1,0:T(8,128)(2,1)S(1)} %get-tuple-element.37), channel_id=1, source_target_pairs={{0,16},{8,24},{16,0},{24,8},{1,17},{9,25},{17,1},{25,9},{2,18},{10... | collective-permute-start | bytes 49160 | tf_op jit(solution)/shard_map/ppermute | solution.py:274
  32.9 1.8 %collective-permute-start.8 = (bf16[16,512]{1,0:T(8,128)(2,1)S(1)}, bf16[16,512]{1,0:T(8,128)(2,1)S(1)}, u32[]{:S(2)}, u32[]{:S(2)}) collective-permute-start(bf16[16,512]{1,0:T(8,128)(2,1)S(1)} %get-tuple-element.38), channel_id=1, source_target_pairs={{0,24},{8,16},{16,8},{24,0},{1,25},{9,17},{17,9},{25,1},{2,26},{10... | collective-permute-start | bytes 49160 | tf_op jit(solution)/shard_map/ppermute | solution.py:274
  34.8 0.5 collective-permute-done.5.rest_3_
  35.2 6.3 %mid_translate.1.far_ref = f32[2,64,512]{2,1,0:T(8,128)S(1)} custom-call(s32[4096]{0:T(1024)S(1)} %reshape.30.source_hbm, s32[4096]{0:T(1024)S(1)} %reshape.31.offset_hbm, f32[2528,128]{1,0:T(8,128)S(1)} %bitcast.11, bf16[8,16,512]{2,1,0:T(8,128)(2,1)S(1)} %pass_on.2.rest_0_, bf16[8,16,512]{2,1,0:T(8,128)(2,1)S(1)} %collective-permute-done.rest_1_, ...), custom_call_target="tpu_custom_call" | custom-call | flops 1150000000 | tf_op jit(solution)/shard_map/mid_translate/pallas_call | solution.py:416
  41.6 0.9 %top_down.1 = bf16[8,16,512]{2,1,0:T(8,128)(2,1)S(1)} custom-call(bf16[1,512,2048]{2,1,0:T(8,128)(2,1)S(1)} %copy-done, f32[8,2048]{1,0:T(8,128)S(1)} %get-tuple-element.24.cos_ref, f32[8,2048]{1,0:T(8,128)S(1)} %get-tuple-element.25.sin_ref, f32[2,64,512]{2,1,0:T(8,128)S(1)} %mid_translate.1.far_ref, ...), custom_call_target="tpu_custom_call" | custom-call | flops 1150000000 | tf_op jit(solution)/shard_map/top_down/pallas_call | solution.py:434
  42.5 7.9 %all_to_all.10.mid_ref = bf16[8,16,512]{2,1,0:T(8,128)(2,1)S(1)} all-to-all(bf16[8,16,512]{2,1,0:T(8,128)(2,1)S(1)} %top_down.1), channel_id=1, replica_groups=mesh['box'=4,'dir'=8] {'dir'}, dimensions={0} | all-to-all | bytes 262144 | tf_op jit(solution)/shard_map/all_to_all | solution.py:443
  50.4 3.2 %leaf_down.1 = f32[128,1024]{1,0:T(8,128)} custom-call(bf16[8,16,512]{2,1,0:T(8,128)(2,1)S(1)} %all_to_all.10.mid_ref, bf16[1024,4096]{1,0:T(8,128)(2,1)S(1)} %bitcast.9, f32[8,4096]{1,0:T(8,128)S(1)} %copy-done.3), custom_call_target="tpu_custom_call" | custom-call | flops 3449999872 | tf_op jit(solution)/shard_map/leaf_down/pallas_call | solution.py:445
  (38 shorter events, 0.4 us)
Async XLA Ops:
  0.0 10.6 %copy-start.5 = (s32[32,64]{1,0:T(8,128)S(1)}, s32[32,64]{1,0:T(8,128)}, u32[]{:S(2)}) copy-start(s32[32,64]{1,0:T(8,128)} %param.20) | copy-start | bytes 24580
  0.0 10.7 %copy-start.6 = (s32[32,64]{1,0:T(8,128)S(1)}, s32[32,64]{1,0:T(8,128)}, u32[]{:S(2)}) copy-start(s32[32,64]{1,0:T(8,128)} %param.21) | copy-start | bytes 24580
  0.0 10.7 %copy-start.7 = (s32[256,64]{0,1:T(8,128)S(1)}, s32[256,64]{0,1:T(8,128)}, u32[]{:S(2)}) copy-start(s32[256,64]{0,1:T(8,128)} %param.16) | copy-start | bytes 196612
  0.0 10.7 %copy-start.8 = (s32[256,64]{0,1:T(8,128)S(1)}, s32[256,64]{0,1:T(8,128)}, u32[]{:S(2)}) copy-start(s32[256,64]{0,1:T(8,128)} %param.15) | copy-start | bytes 196612
  0.0 11.1 %copy-start.4 = (f32[8,1,2048]{2,1,0:T(1,128)S(1)}, f32[8,1,2048]{2,1,0:T(1,128)}, u32[]{:S(2)}) copy-start(f32[8,1,2048]{2,1,0:T(1,128)} %shift_ref.2) | copy-start | bytes 196612
  5.4 10.7 %all-to-all-start = ((bf16[8,16,512]{2,1,0:T(8,128)(2,1)}), bf16[8,16,512]{2,1,0:T(8,128)(2,1)S(1)}, u32[]{:S(2)}, u32[]{:S(2)}) async-start(bf16[8,16,512]{2,1,0:T(8,128)(2,1)} %leaf_up.1), calls=%async_computation | async-start | bytes 262144 | tf_op jit(solution)/shard_map/all_to_all | solution.py:352
  11.2 5.0 %copy-start = (bf16[1,512,2048]{2,1,0:T(8,128)(2,1)S(1)}, bf16[1,512,2048]{2,1,0:T(8,128)(2,1)}, u32[]{:S(2)}) copy-start(bf16[1,512,2048]{2,1,0:T(8,128)(2,1)} %table_ref.4) | copy-start | bytes 6291460
  16.1 10.7 %copy-start.1 = (f32[2,316,1,512]{3,2,1,0:T(1,128)S(1)}, f32[2,316,1,512]{3,2,1,0:T(1,128)}, u32[]{:S(2)}) copy-start(f32[2,316,1,512]{3,2,1,0:T(1,128)} %param.19) | copy-start | bytes 3883012
  16.1 34.3 %slice-start = ((s8[8388608]{0:T(1024)(128)(4,1)}), s8[4194304]{0:T(1024)(128)(4,1)S(1)}, s32[]{:S(2)}) async-start(s8[8388608]{0:T(1024)(128)(4,1)} %bitcast.8), calls=%async_computation.2 | async-start | bytes 8388608
  16.8 8.7 %collective-permute-start.2 = (bf16[16,512]{1,0:T(8,128)(2,1)S(1)}, bf16[16,512]{1,0:T(8,128)(2,1)S(1)}, u32[]{:S(2)}, u32[]{:S(2)}) collective-permute-start(bf16[16,512]{1,0:T(8,128)(2,1)S(1)} %get-tuple-element.32), channel_id=1, source_target_pairs={{0,8},{8,0},{16,24},{24,16},{1,9},{9,1},{17,25},{25,17},{2,10},{10... | collective-permute-start | bytes 49160 | tf_op jit(solution)/shard_map/ppermute | solution.py:274
  18.4 7.1 %collective-permute-start.3 = (bf16[16,512]{1,0:T(8,128)(2,1)S(1)}, bf16[16,512]{1,0:T(8,128)(2,1)S(1)}, u32[]{:S(2)}, u32[]{:S(2)}) collective-permute-start(bf16[16,512]{1,0:T(8,128)(2,1)S(1)} %get-tuple-element.33), channel_id=1, source_target_pairs={{0,16},{8,24},{16,0},{24,8},{1,17},{9,25},{17,1},{25,9},{2,18},{10... | collective-permute-start | bytes 49160 | tf_op jit(solution)/shard_map/ppermute | solution.py:274
  21.0 5.8 %collective-permute-start.4 = (bf16[16,512]{1,0:T(8,128)(2,1)S(1)}, bf16[16,512]{1,0:T(8,128)(2,1)S(1)}, u32[]{:S(2)}, u32[]{:S(2)}) collective-permute-start(bf16[16,512]{1,0:T(8,128)(2,1)S(1)} %get-tuple-element.34), channel_id=1, source_target_pairs={{0,24},{8,16},{16,8},{24,0},{1,25},{9,17},{17,9},{25,1},{2,26},{10... | collective-permute-start | bytes 49160 | tf_op jit(solution)/shard_map/ppermute | solution.py:274
  21.2 8.9 %collective-permute-start.1 = (bf16[8,16,512]{2,1,0:T(8,128)(2,1)S(1)}, bf16[8,16,512]{2,1,0:T(8,128)(2,1)S(1)}, u32[]{:S(2)}, u32[]{:S(2)}) collective-permute-start(bf16[8,16,512]{2,1,0:T(8,128)(2,1)S(1)} %pass_on.2.rest_0_), channel_id=1, source_target_pairs={{0,16},{8,24},{16,0},{24,8},{1,17},{9,25},{17,1},{25,9},{2,18},{10... | collective-permute-start | bytes 393224 | tf_op jit(solution)/shard_map/ppermute | solution.py:274
  23.0 11.8 %collective-permute-start = (bf16[8,16,512]{2,1,0:T(8,128)(2,1)S(1)}, bf16[8,16,512]{2,1,0:T(8,128)(2,1)S(1)}, u32[]{:S(2)}, u32[]{:S(2)}) collective-permute-start(bf16[8,16,512]{2,1,0:T(8,128)(2,1)S(1)} %pass_on.2.rest_0_), channel_id=1, source_target_pairs={{0,8},{8,0},{16,24},{24,16},{1,9},{9,1},{17,25},{25,17},{2,10},{10... | collective-permute-start | bytes 393224 | tf_op jit(solution)/shard_map/ppermute | solution.py:274
  26.8 8.4 %copy-start.2 = (f32[2,316,512]{2,0,1:T(2,128)S(1)}, f32[2,316,512]{2,0,1:T(2,128)}, u32[]{:S(2)}) copy-start(f32[2,316,512]{2,0,1:T(2,128)} %param.14) | copy-start | bytes 3883012
  26.8 23.6 %slice-start.1 = ((s8[8388608]{0:T(1024)(128)(4,1)}), s8[4194304]{0:T(1024)(128)(4,1)S(1)}, s32[]{:S(2)}) async-start(s8[8388608]{0:T(1024)(128)(4,1)} %bitcast.8), calls=%async_computation.3 | async-start | bytes 8388608
  30.2 5.0 %collective-permute-start.5 = (bf16[8,16,512]{2,1,0:T(8,128)(2,1)S(1)}, bf16[8,16,512]{2,1,0:T(8,128)(2,1)S(1)}, u32[]{:S(2)}, u32[]{:S(2)}) collective-permute-start(bf16[8,16,512]{2,1,0:T(8,128)(2,1)S(1)} %pass_on.3), channel_id=1, source_target_pairs={{0,8},{8,0},{16,24},{24,16},{1,9},{9,1},{17,25},{25,17},{2,10},{10... | collective-permute-start | bytes 393224 | tf_op jit(solution)/shard_map/ppermute | solution.py:274
  30.4 11.2 %collective-permute-start.6 = (bf16[16,512]{1,0:T(8,128)(2,1)S(1)}, bf16[16,512]{1,0:T(8,128)(2,1)S(1)}, u32[]{:S(2)}, u32[]{:S(2)}) collective-permute-start(bf16[16,512]{1,0:T(8,128)(2,1)S(1)} %get-tuple-element.36), channel_id=1, source_target_pairs={{0,8},{8,0},{16,24},{24,16},{1,9},{9,1},{17,25},{25,17},{2,10},{10... | collective-permute-start | bytes 49160 | tf_op jit(solution)/shard_map/ppermute | solution.py:274
  32.3 9.3 %collective-permute-start.7 = (bf16[16,512]{1,0:T(8,128)(2,1)S(1)}, bf16[16,512]{1,0:T(8,128)(2,1)S(1)}, u32[]{:S(2)}, u32[]{:S(2)}) collective-permute-start(bf16[16,512]{1,0:T(8,128)(2,1)S(1)} %get-tuple-element.37), channel_id=1, source_target_pairs={{0,16},{8,24},{16,0},{24,8},{1,17},{9,25},{17,1},{25,9},{2,18},{10... | collective-permute-start | bytes 49160 | tf_op jit(solution)/shard_map/ppermute | solution.py:274
  32.9 8.7 %collective-permute-start.8 = (bf16[16,512]{1,0:T(8,128)(2,1)S(1)}, bf16[16,512]{1,0:T(8,128)(2,1)S(1)}, u32[]{:S(2)}, u32[]{:S(2)}) collective-permute-start(bf16[16,512]{1,0:T(8,128)(2,1)S(1)} %get-tuple-element.38), channel_id=1, source_target_pairs={{0,24},{8,16},{16,8},{24,0},{1,25},{9,17},{17,9},{25,1},{2,26},{10... | collective-permute-start | bytes 49160 | tf_op jit(solution)/shard_map/ppermute | solution.py:274
  41.6 8.8 %copy-start.3 = (f32[8,4096]{1,0:T(8,128)S(1)}, f32[8,4096]{1,0:T(8,128)}, u32[]{:S(2)}) copy-start(f32[8,4096]{1,0:T(8,128)} %shift_ref.3) | copy-start | bytes 393220

commit v5 on v4

--- a/solution.py
+++ b/solution.py
@@ -14,7 +14,7 @@
 UNROLL = 4
 LANES = 128
 ROWS = 8
-AHEAD = 2
+AHEAD = 3
 CHUNK_SECTORS = 2
 
 
@@ -293,7 +293,7 @@
 
 def exchange(shares):
     received = list(shares)
-    for step in reversed(range(1, len(shares))):
+    for step in range(1, len(shares)):
         received[step] = swap(shares[step], "box", step)
     return received
 
@@ -394,10 +394,10 @@
         out_specs=[vmem] * boxes,
         out_shape=[share] * boxes,
         scratch_shapes=[
-            pltpu.VMEM(rows_top.shape, jnp.float32),
-            pltpu.VMEM((2 * tops * top_height, LANES), jnp.float32),
-            pltpu.VMEM((tops * top_height, LANES), jnp.float32),
-            pltpu.VMEM((tops * top_height, LANES), jnp.float32),
+            pltpu.VMEM((rows_top.shape[0] + ROWS, LANES), jnp.float32),
+            pltpu.VMEM((2 * (tops + 1) * top_height, LANES), jnp.float32),
+            pltpu.VMEM(((tops + 1) * top_height, LANES), jnp.float32),
+            pltpu.VMEM(((tops + 1) * top_height, LANES), jnp.float32),
             pltpu.SMEM(top_index[0].shape, jnp.int32),
             pltpu.SMEM(top_index[0].shape, jnp.int32),
             pltpu.SemaphoreType.DMA((4,)),
@@ -419,9 +419,9 @@
         out_specs=vmem,
         out_shape=jax.ShapeDtypeStruct((2, group_mids, sector), jnp.float32),
         scratch_shapes=[
-            pltpu.VMEM((2 * mids * mid_height, LANES), jnp.float32),
-            pltpu.VMEM((group_mids * mid_height, LANES), jnp.float32),
-            pltpu.VMEM((group_mids * mid_height, LANES), jnp.float32),
+            pltpu.VMEM((2 * (mids + 1) * mid_height, LANES), jnp.float32),
+            pltpu.VMEM(((group_mids + 1) * mid_height, LANES), jnp.float32),
+            pltpu.VMEM(((group_mids + 1) * mid_height, LANES), jnp.float32),
             pltpu.SMEM(mid_index[0].shape, jnp.int32),
             pltpu.SMEM(mid_index[0].shape, jnp.int32),
             pltpu.SemaphoreType.DMA((4,)),

time: 53.9 us -> 53.9 us (level)
  no operation moved by 1% of the time
where the time goes in v5:
time: 53.9 us; the launch traced here: 53.6 us
  Pallas kernels  19.8 us (37%)
  starting transfers between devices  18.5 us (34%)
  blocking collectives  7.92 us (15%)
  waiting for transfers between devices  6.61 us (12%)
    ppermute x9, starting transfers between devices, swap(): return lax.ppermute(values, axis, [(k, k ^ step) for k in range(size)])  13.3 us
    all_to_all x1, blocking collectives, on_device(): lax.all_to_all(incoming, 'dir', split_axis=0, concat_axis=0, tiled=True)  7.92 us
    pallas_call x1, Pallas kernels, on_device(): pl.pallas_call(functools.partial(mid_translate, list_width), in_specs=[hb...  6.34 us
    pallas_call x1, Pallas kernels, on_device(): pl.pallas_call(leaf_up, in_specs=[hbm, hbm, hbm], out_specs=vmem, out_sha...  5.29 us
    all_to_all x1, starting transfers between devices, on_device(): lax.all_to_all(outgoing, 'dir', split_axis=0, concat_axis=0, tiled=True)  5.22 us
    all_to_all x1, waiting for transfers between devices, on_device(): lax.all_to_all(outgoing, 'dir', split_axis=0, concat_axis=0, tiled=True)  4.85 us
    pallas_call x1, Pallas kernels, on_device(): pl.pallas_call(functools.partial(top_translate, list_width), in_specs=[hb...  3.34 us
    pallas_call x1, Pallas kernels, on_device(): pl.pallas_call(functools.partial(leaf_down, leaf_width / mid_width), in_s...  3.25 us
  transfers between devices with their start and end apart: 10, of which 3 were waited for; matrix products, arithmetic and copies ran while one was open for 1% of the time, Pallas kernels for 18%

profile of v5, /device:TPU:0, one launch (start us, length us, event | category | flops | bytes accessed | tf_op | source)
XLA Modules:
  0.0 53.6 jit_solution(9765196820773772885)
XLA Ops:
  0.0 5.3 %leaf_up.1 = bf16[8,16,512]{2,1,0:T(8,128)(2,1)} custom-call(bf16[128,1024]{1,0:T(8,128)(2,1)} %bitcast.12, bf16[1024,4096]{1,0:T(8,128)(2,1)} %table_ref.5, f32[8,4096]{1,0:T(8,128)} %shift_ref.3), custom_call_target="tpu_custom_call" | custom-call | flops 5750000128 | tf_op jit(solution)/shard_map/leaf_up/pallas_call | solution.py:336
  5.3 5.2 %all-to-all-start = ((bf16[8,16,512]{2,1,0:T(8,128)(2,1)}), bf16[8,16,512]{2,1,0:T(8,128)(2,1)S(1)}, u32[]{:S(2)}, u32[]{:S(2)}) async-start(bf16[8,16,512]{2,1,0:T(8,128)(2,1)} %leaf_up.1), calls=%async_computation | async-start | bytes 262144 | tf_op jit(solution)/shard_map/all_to_all | solution.py:352
  10.7 0.1 dynamic-slice_multiply_fusion
  10.9 0.1 reshape.31.offset_hbm
  11.0 0.1 reshape.30.source_hbm
  11.1 0.1 tables.1
  11.2 4.9 %all-to-all-done.mid_ref.values_ref = bf16[8,16,512]{2,1,0:T(8,128)(2,1)S(1)} async-done(((bf16[8,16,512]{2,1,0:T(8,128)(2,1)}), bf16[8,16,512]{2,1,0:T(8,128)(2,1)S(1)}, u32[]{:S(2)}, u32[]{:S(2)}) %all-to-all-start) | async-done | bytes 131104 | tf_op jit(solution)/shard_map/all_to_all | solution.py:352
  16.1 0.6 %top_up.1 = (bf16[16,512]{1,0:T(8,128)(2,1)S(1)}, bf16[16,512]{1,0:T(8,128)(2,1)S(1)}, bf16[16,512]{1,0:T(8,128)(2,1)S(1)}, bf16[16,512]{1,0:T(8,128)(2,1)S(1)}) custom-call(bf16[8,16,512]{2,1,0:T(8,128)(2,1)S(1)} %all-to-all-done.mid_ref.values_ref, bf16[1,512,2048]{2,1,0:T(8,128)(2,1)S(1)} %copy-done, f32[8,2048]{1,0:T(8,128)S(1)} %get-tuple-element.24.cos_ref, ...), custom_call_target="tpu_custom_call" | custom-call | flops 4600000000 | tf_op jit(solution)/shard_map/top_up/pallas_call | solution.py:375
  16.7 1.6 %collective-permute-start.2 = (bf16[16,512]{1,0:T(8,128)(2,1)S(1)}, bf16[16,512]{1,0:T(8,128)(2,1)S(1)}, u32[]{:S(2)}, u32[]{:S(2)}) collective-permute-start(bf16[16,512]{1,0:T(8,128)(2,1)S(1)} %get-tuple-element.32), channel_id=1, source_target_pairs={{0,8},{8,0},{16,24},{24,16},{1,9},{9,1},{17,25},{25,17},{2,10},{10... | collective-permute-start | bytes 49160 | tf_op jit(solution)/shard_map/ppermute | solution.py:274
  18.4 2.6 %collective-permute-start.3 = (bf16[16,512]{1,0:T(8,128)(2,1)S(1)}, bf16[16,512]{1,0:T(8,128)(2,1)S(1)}, u32[]{:S(2)}, u32[]{:S(2)}) collective-permute-start(bf16[16,512]{1,0:T(8,128)(2,1)S(1)} %get-tuple-element.33), channel_id=1, source_target_pairs={{0,16},{8,24},{16,0},{24,8},{1,17},{9,25},{17,1},{25,9},{2,18},{10... | collective-permute-start | bytes 49160 | tf_op jit(solution)/shard_map/ppermute | solution.py:274
  20.9 0.2 collective-permute-start.4
  21.2 1.7 %collective-permute-start.1 = (bf16[8,16,512]{2,1,0:T(8,128)(2,1)S(1)}, bf16[8,16,512]{2,1,0:T(8,128)(2,1)S(1)}, u32[]{:S(2)}, u32[]{:S(2)}) collective-permute-start(bf16[8,16,512]{2,1,0:T(8,128)(2,1)S(1)} %pass_on.2.rest_0_), channel_id=1, source_target_pairs={{0,16},{8,24},{16,0},{24,8},{1,17},{9,25},{17,1},{25,9},{2,18},{10... | collective-permute-start | bytes 393224 | tf_op jit(solution)/shard_map/ppermute | solution.py:274
  22.9 2.5 %collective-permute-start = (bf16[8,16,512]{2,1,0:T(8,128)(2,1)S(1)}, bf16[8,16,512]{2,1,0:T(8,128)(2,1)S(1)}, u32[]{:S(2)}, u32[]{:S(2)}) collective-permute-start(bf16[8,16,512]{2,1,0:T(8,128)(2,1)S(1)} %pass_on.2.rest_0_), channel_id=1, source_target_pairs={{0,8},{8,0},{16,24},{24,16},{1,9},{9,1},{17,25},{25,17},{2,10},{10... | collective-permute-start | bytes 393224 | tf_op jit(solution)/shard_map/ppermute | solution.py:274
  25.4 1.3 %collective-permute-done.4.rest_3_ = bf16[16,512]{1,0:T(8,128)(2,1)S(1)} collective-permute-done((bf16[16,512]{1,0:T(8,128)(2,1)S(1)}, bf16[16,512]{1,0:T(8,128)(2,1)S(1)}, u32[]{:S(2)}, u32[]{:S(2)}) %collective-permute-start.4) | collective-permute-done | bytes 16416 | tf_op jit(solution)/shard_map/ppermute | solution.py:274
  26.7 3.3 %top_translate.1 = (bf16[16,512]{1,0:T(8,128)(2,1)S(1)}, bf16[16,512]{1,0:T(8,128)(2,1)S(1)}, bf16[16,512]{1,0:T(8,128)(2,1)S(1)}, bf16[16,512]{1,0:T(8,128)(2,1)S(1)}) custom-call(s32[2048]{0:T(1024)S(1)} %reshape.28.source_hbm, s32[2048]{0:T(1024)S(1)} %reshape.29.offset_hbm, f32[2528,128]{1,0:T(8,128)S(1)} %bitcast.10, ...), custom_call_target="tpu_custom_call" | custom-call | flops 17250000896 | tf_op jit(solution)/shard_map/top_translate/pallas_call | solution.py:391
  30.1 0.2 collective-permute-start.5
  30.3 1.9 %collective-permute-start.6 = (bf16[16,512]{1,0:T(8,128)(2,1)S(1)}, bf16[16,512]{1,0:T(8,128)(2,1)S(1)}, u32[]{:S(2)}, u32[]{:S(2)}) collective-permute-start(bf16[16,512]{1,0:T(8,128)(2,1)S(1)} %get-tuple-element.36), channel_id=1, source_target_pairs={{0,8},{8,0},{16,24},{24,16},{1,9},{9,1},{17,25},{25,17},{2,10},{10... | collective-permute-start | bytes 49160 | tf_op jit(solution)/shard_map/ppermute | solution.py:274
  32.2 0.7 %collective-permute-start.7 = (bf16[16,512]{1,0:T(8,128)(2,1)S(1)}, bf16[16,512]{1,0:T(8,128)(2,1)S(1)}, u32[]{:S(2)}, u32[]{:S(2)}) collective-permute-start(bf16[16,512]{1,0:T(8,128)(2,1)S(1)} %get-tuple-element.37), channel_id=1, source_target_pairs={{0,16},{8,24},{16,0},{24,8},{1,17},{9,25},{17,1},{25,9},{2,18},{10... | collective-permute-start | bytes 49160 | tf_op jit(solution)/shard_map/ppermute | solution.py:274
  32.9 1.8 %collective-permute-start.8 = (bf16[16,512]{1,0:T(8,128)(2,1)S(1)}, bf16[16,512]{1,0:T(8,128)(2,1)S(1)}, u32[]{:S(2)}, u32[]{:S(2)}) collective-permute-start(bf16[16,512]{1,0:T(8,128)(2,1)S(1)} %get-tuple-element.38), channel_id=1, source_target_pairs={{0,24},{8,16},{16,8},{24,0},{1,25},{9,17},{17,9},{25,1},{2,26},{10... | collective-permute-start | bytes 49160 | tf_op jit(solution)/shard_map/ppermute | solution.py:274
  34.7 0.4 collective-permute-done.5.rest_3_
  35.1 6.3 %mid_translate.1.far_ref = f32[2,64,512]{2,1,0:T(8,128)S(1)} custom-call(s32[4096]{0:T(1024)S(1)} %reshape.30.source_hbm, s32[4096]{0:T(1024)S(1)} %reshape.31.offset_hbm, f32[2528,128]{1,0:T(8,128)S(1)} %bitcast.11, bf16[8,16,512]{2,1,0:T(8,128)(2,1)S(1)} %pass_on.2.rest_0_, bf16[8,16,512]{2,1,0:T(8,128)(2,1)S(1)} %collective-permute-done.rest_1_, ...), custom_call_target="tpu_custom_call" | custom-call | flops 1150000000 | tf_op jit(solution)/shard_map/mid_translate/pallas_call | solution.py:416
  41.5 0.9 %top_down.1 = bf16[8,16,512]{2,1,0:T(8,128)(2,1)S(1)} custom-call(bf16[1,512,2048]{2,1,0:T(8,128)(2,1)S(1)} %copy-done, f32[8,2048]{1,0:T(8,128)S(1)} %get-tuple-element.24.cos_ref, f32[8,2048]{1,0:T(8,128)S(1)} %get-tuple-element.25.sin_ref, f32[2,64,512]{2,1,0:T(8,128)S(1)} %mid_translate.1.far_ref, ...), custom_call_target="tpu_custom_call" | custom-call | flops 1150000000 | tf_op jit(solution)/shard_map/top_down/pallas_call | solution.py:434
  42.4 7.9 %all_to_all.10.mid_ref = bf16[8,16,512]{2,1,0:T(8,128)(2,1)S(1)} all-to-all(bf16[8,16,512]{2,1,0:T(8,128)(2,1)S(1)} %top_down.1), channel_id=1, replica_groups=mesh['box'=4,'dir'=8] {'dir'}, dimensions={0} | all-to-all | bytes 262144 | tf_op jit(solution)/shard_map/all_to_all | solution.py:443
  50.3 3.2 %leaf_down.1 = f32[128,1024]{1,0:T(8,128)} custom-call(bf16[8,16,512]{2,1,0:T(8,128)(2,1)S(1)} %all_to_all.10.mid_ref, bf16[1024,4096]{1,0:T(8,128)(2,1)S(1)} %bitcast.9, f32[8,4096]{1,0:T(8,128)S(1)} %copy-done.3), custom_call_target="tpu_custom_call" | custom-call | flops 3449999872 | tf_op jit(solution)/shard_map/leaf_down/pallas_call | solution.py:445
  (38 shorter events, 0.4 us)
Async XLA Ops:
  0.0 10.5 %copy-start.5 = (s32[32,64]{1,0:T(8,128)S(1)}, s32[32,64]{1,0:T(8,128)}, u32[]{:S(2)}) copy-start(s32[32,64]{1,0:T(8,128)} %param.20) | copy-start | bytes 24580
  0.0 10.6 %copy-start.6 = (s32[32,64]{1,0:T(8,128)S(1)}, s32[32,64]{1,0:T(8,128)}, u32[]{:S(2)}) copy-start(s32[32,64]{1,0:T(8,128)} %param.21) | copy-start | bytes 24580
  0.0 10.7 %copy-start.7 = (s32[256,64]{0,1:T(8,128)S(1)}, s32[256,64]{0,1:T(8,128)}, u32[]{:S(2)}) copy-start(s32[256,64]{0,1:T(8,128)} %param.16) | copy-start | bytes 196612
  0.0 10.7 %copy-start.8 = (s32[256,64]{0,1:T(8,128)S(1)}, s32[256,64]{0,1:T(8,128)}, u32[]{:S(2)}) copy-start(s32[256,64]{0,1:T(8,128)} %param.15) | copy-start | bytes 196612
  0.0 11.1 %copy-start.4 = (f32[8,1,2048]{2,1,0:T(1,128)S(1)}, f32[8,1,2048]{2,1,0:T(1,128)}, u32[]{:S(2)}) copy-start(f32[8,1,2048]{2,1,0:T(1,128)} %shift_ref.2) | copy-start | bytes 196612
  5.3 10.8 %all-to-all-start = ((bf16[8,16,512]{2,1,0:T(8,128)(2,1)}), bf16[8,16,512]{2,1,0:T(8,128)(2,1)S(1)}, u32[]{:S(2)}, u32[]{:S(2)}) async-start(bf16[8,16,512]{2,1,0:T(8,128)(2,1)} %leaf_up.1), calls=%async_computation | async-start | bytes 262144 | tf_op jit(solution)/shard_map/all_to_all | solution.py:352
  11.1 5.0 %copy-start = (bf16[1,512,2048]{2,1,0:T(8,128)(2,1)S(1)}, bf16[1,512,2048]{2,1,0:T(8,128)(2,1)}, u32[]{:S(2)}) copy-start(bf16[1,512,2048]{2,1,0:T(8,128)(2,1)} %table_ref.4) | copy-start | bytes 6291460
  16.1 10.7 %copy-start.1 = (f32[2,316,1,512]{3,2,1,0:T(1,128)S(1)}, f32[2,316,1,512]{3,2,1,0:T(1,128)}, u32[]{:S(2)}) copy-start(f32[2,316,1,512]{3,2,1,0:T(1,128)} %param.19) | copy-start | bytes 3883012
  16.1 34.3 %slice-start = ((s8[8388608]{0:T(1024)(128)(4,1)}), s8[4194304]{0:T(1024)(128)(4,1)S(1)}, s32[]{:S(2)}) async-start(s8[8388608]{0:T(1024)(128)(4,1)} %bitcast.8), calls=%async_computation.2 | async-start | bytes 8388608
  16.7 8.7 %collective-permute-start.2 = (bf16[16,512]{1,0:T(8,128)(2,1)S(1)}, bf16[16,512]{1,0:T(8,128)(2,1)S(1)}, u32[]{:S(2)}, u32[]{:S(2)}) collective-permute-start(bf16[16,512]{1,0:T(8,128)(2,1)S(1)} %get-tuple-element.32), channel_id=1, source_target_pairs={{0,8},{8,0},{16,24},{24,16},{1,9},{9,1},{17,25},{25,17},{2,10},{10... | collective-permute-start | bytes 49160 | tf_op jit(solution)/shard_map/ppermute | solution.py:274
  18.4 7.1 %collective-permute-start.3 = (bf16[16,512]{1,0:T(8,128)(2,1)S(1)}, bf16[16,512]{1,0:T(8,128)(2,1)S(1)}, u32[]{:S(2)}, u32[]{:S(2)}) collective-permute-start(bf16[16,512]{1,0:T(8,128)(2,1)S(1)} %get-tuple-element.33), channel_id=1, source_target_pairs={{0,16},{8,24},{16,0},{24,8},{1,17},{9,25},{17,1},{25,9},{2,18},{10... | collective-permute-start | bytes 49160 | tf_op jit(solution)/shard_map/ppermute | solution.py:274
  20.9 5.8 %collective-permute-start.4 = (bf16[16,512]{1,0:T(8,128)(2,1)S(1)}, bf16[16,512]{1,0:T(8,128)(2,1)S(1)}, u32[]{:S(2)}, u32[]{:S(2)}) collective-permute-start(bf16[16,512]{1,0:T(8,128)(2,1)S(1)} %get-tuple-element.34), channel_id=1, source_target_pairs={{0,24},{8,16},{16,8},{24,0},{1,25},{9,17},{17,9},{25,1},{2,26},{10... | collective-permute-start | bytes 49160 | tf_op jit(solution)/shard_map/ppermute | solution.py:274
  21.2 8.9 %collective-permute-start.1 = (bf16[8,16,512]{2,1,0:T(8,128)(2,1)S(1)}, bf16[8,16,512]{2,1,0:T(8,128)(2,1)S(1)}, u32[]{:S(2)}, u32[]{:S(2)}) collective-permute-start(bf16[8,16,512]{2,1,0:T(8,128)(2,1)S(1)} %pass_on.2.rest_0_), channel_id=1, source_target_pairs={{0,16},{8,24},{16,0},{24,8},{1,17},{9,25},{17,1},{25,9},{2,18},{10... | collective-permute-start | bytes 393224 | tf_op jit(solution)/shard_map/ppermute | solution.py:274
  22.9 11.8 %collective-permute-start = (bf16[8,16,512]{2,1,0:T(8,128)(2,1)S(1)}, bf16[8,16,512]{2,1,0:T(8,128)(2,1)S(1)}, u32[]{:S(2)}, u32[]{:S(2)}) collective-permute-start(bf16[8,16,512]{2,1,0:T(8,128)(2,1)S(1)} %pass_on.2.rest_0_), channel_id=1, source_target_pairs={{0,8},{8,0},{16,24},{24,16},{1,9},{9,1},{17,25},{25,17},{2,10},{10... | collective-permute-start | bytes 393224 | tf_op jit(solution)/shard_map/ppermute | solution.py:274
  26.7 8.4 %copy-start.2 = (f32[2,316,512]{2,0,1:T(2,128)S(1)}, f32[2,316,512]{2,0,1:T(2,128)}, u32[]{:S(2)}) copy-start(f32[2,316,512]{2,0,1:T(2,128)} %param.14) | copy-start | bytes 3883012
  26.7 23.6 %slice-start.1 = ((s8[8388608]{0:T(1024)(128)(4,1)}), s8[4194304]{0:T(1024)(128)(4,1)S(1)}, s32[]{:S(2)}) async-start(s8[8388608]{0:T(1024)(128)(4,1)} %bitcast.8), calls=%async_computation.3 | async-start | bytes 8388608
  30.1 5.0 %collective-permute-start.5 = (bf16[8,16,512]{2,1,0:T(8,128)(2,1)S(1)}, bf16[8,16,512]{2,1,0:T(8,128)(2,1)S(1)}, u32[]{:S(2)}, u32[]{:S(2)}) collective-permute-start(bf16[8,16,512]{2,1,0:T(8,128)(2,1)S(1)} %pass_on.3), channel_id=1, source_target_pairs={{0,8},{8,0},{16,24},{24,16},{1,9},{9,1},{17,25},{25,17},{2,10},{10... | collective-permute-start | bytes 393224 | tf_op jit(solution)/shard_map/ppermute | solution.py:274
  30.3 11.2 %collective-permute-start.6 = (bf16[16,512]{1,0:T(8,128)(2,1)S(1)}, bf16[16,512]{1,0:T(8,128)(2,1)S(1)}, u32[]{:S(2)}, u32[]{:S(2)}) collective-permute-start(bf16[16,512]{1,0:T(8,128)(2,1)S(1)} %get-tuple-element.36), channel_id=1, source_target_pairs={{0,8},{8,0},{16,24},{24,16},{1,9},{9,1},{17,25},{25,17},{2,10},{10... | collective-permute-start | bytes 49160 | tf_op jit(solution)/shard_map/ppermute | solution.py:274
  32.2 9.3 %collective-permute-start.7 = (bf16[16,512]{1,0:T(8,128)(2,1)S(1)}, bf16[16,512]{1,0:T(8,128)(2,1)S(1)}, u32[]{:S(2)}, u32[]{:S(2)}) collective-permute-start(bf16[16,512]{1,0:T(8,128)(2,1)S(1)} %get-tuple-element.37), channel_id=1, source_target_pairs={{0,16},{8,24},{16,0},{24,8},{1,17},{9,25},{17,1},{25,9},{2,18},{10... | collective-permute-start | bytes 49160 | tf_op jit(solution)/shard_map/ppermute | solution.py:274
  32.9 8.7 %collective-permute-start.8 = (bf16[16,512]{1,0:T(8,128)(2,1)S(1)}, bf16[16,512]{1,0:T(8,128)(2,1)S(1)}, u32[]{:S(2)}, u32[]{:S(2)}) collective-permute-start(bf16[16,512]{1,0:T(8,128)(2,1)S(1)} %get-tuple-element.38), channel_id=1, source_target_pairs={{0,24},{8,16},{16,8},{24,0},{1,25},{9,17},{17,9},{25,1},{2,26},{10... | collective-permute-start | bytes 49160 | tf_op jit(solution)/shard_map/ppermute | solution.py:274
  41.5 8.8 %copy-start.3 = (f32[8,4096]{1,0:T(8,128)S(1)}, f32[8,4096]{1,0:T(8,128)}, u32[]{:S(2)}) copy-start(f32[8,4096]{1,0:T(8,128)} %shift_ref.3) | copy-start | bytes 393220

commit v6 on v5

--- a/solution.py
+++ b/solution.py
@@ -15,6 +15,7 @@
 LANES = 128
 ROWS = 8
 AHEAD = 3
+DOWN_BLOCKS = 4
 CHUNK_SECTORS = 2
 
 
@@ -240,18 +241,23 @@
         out_ref[owner] = jnp.concatenate([real[place], imag[place]], axis=0).astype(out_ref.dtype)
 
 
-def leaf_down(scale, mid_ref, table_ref, shift_ref, out_ref, total_ref):
+def leaf_down(scale, mid_ref, table_ref, shift_ref, out_hbm, children_ref, total_ref, sems):
     sectors, _, width = mid_ref.shape
     for part in range(sectors):
         columns = slice(part * width, (part + 1) * width)
         cos, sin = phase(shift_ref[:, columns])
-        children = children_of(mid_ref[part], cos, sin)
-        term = lax.dot_general(table_ref[:, columns], children, ADJOINT, preferred_element_type=jnp.float32)
-        if part == 0:
-            total_ref[...] = term
-        else:
-            total_ref[...] += term
-    out_ref[...] = total_ref[...].T * scale
+        children_ref[:, columns] = children_of(mid_ref[part], cos, sin)
+    blocks, _, size = total_ref.shape
+    copies = []
+    for block in range(blocks):
+        place = slice(block * size, (block + 1) * size)
+        term = lax.dot_general(table_ref[place, :], children_ref[...], ADJOINT, preferred_element_type=jnp.float32)
+        total_ref[block] = term.T * scale
+        target = out_hbm.at[:, pl.ds(block * size, size)]
+        copies.append(pltpu.make_async_copy(total_ref.at[block], target, sems.at[block]))
+        copies[block].start()
+    for copy in copies:
+        copy.wait()
 
 
 def cost(microseconds):
@@ -445,9 +451,13 @@
     leaf_in = pl.pallas_call(
         functools.partial(leaf_down, leaf_width / mid_width),
         in_specs=[vmem] * 3,
-        out_specs=vmem,
+        out_specs=hbm,
         out_shape=jax.ShapeDtypeStruct((2 * leaves, leaf_width), jnp.float32),
-        scratch_shapes=[pltpu.VMEM((leaf_width, 2 * leaves), jnp.float32)],
+        scratch_shapes=[
+            pltpu.VMEM((2 * leaves, mid_width), jnp.bfloat16),
+            pltpu.VMEM((DOWN_BLOCKS, 2 * leaves, leaf_width // DOWN_BLOCKS), jnp.float32),
+            pltpu.SemaphoreType.DMA((DOWN_BLOCKS,)),
+        ],
         compiler_params=params(20),
         cost_estimate=cost(3),
         name="leaf_down",

time: 53.9 us -> 53.8 us (level)
  no operation moved by 1% of the time
where the time goes in v6:
time: 53.8 us; the launch traced here: 53.5 us
  Pallas kernels  19.8 us (37%)
  starting transfers between devices  18.5 us (34%)
  blocking collectives  7.92 us (15%)
  waiting for transfers between devices  6.61 us (12%)
    ppermute x9, starting transfers between devices, swap(): return lax.ppermute(values, axis, [(k, k ^ step) for k in range(size)])  13.3 us
    all_to_all x1, blocking collectives, on_device(): lax.all_to_all(incoming, 'dir', split_axis=0, concat_axis=0, tiled=True)  7.92 us
    pallas_call x1, Pallas kernels, on_device(): pl.pallas_call(functools.partial(mid_translate, list_width), in_specs=[hb...  6.34 us
    pallas_call x1, Pallas kernels, on_device(): pl.pallas_call(leaf_up, in_specs=[hbm, hbm, hbm], out_specs=vmem, out_sha...  5.29 us
    all_to_all x1, starting transfers between devices, on_device(): lax.all_to_all(outgoing, 'dir', split_axis=0, concat_axis=0, tiled=True)  5.22 us
    all_to_all x1, waiting for transfers between devices, on_device(): lax.all_to_all(outgoing, 'dir', split_axis=0, concat_axis=0, tiled=True)  4.85 us
    pallas_call x1, Pallas kernels, on_device(): pl.pallas_call(functools.partial(top_translate, list_width), in_specs=[hb...  3.35 us
    pallas_call x1, Pallas kernels, on_device(): pl.pallas_call(functools.partial(leaf_down, leaf_width / mid_width), in_s...  3.17 us
  transfers between devices with their start and end apart: 10, of which 3 were waited for; matrix products, arithmetic and copies ran while one was open for 1% of the time, Pallas kernels for 18%

profile of v6, /device:TPU:0, one launch (start us, length us, event | category | flops | bytes accessed | tf_op | source)
XLA Modules:
  0.0 53.5 jit_solution(314545716546376786)
XLA Ops:
  0.0 5.3 %leaf_up.1 = bf16[8,16,512]{2,1,0:T(8,128)(2,1)} custom-call(bf16[128,1024]{1,0:T(8,128)(2,1)} %bitcast.12, bf16[1024,4096]{1,0:T(8,128)(2,1)} %table_ref.5, f32[8,4096]{1,0:T(8,128)} %shift_ref.3), custom_call_target="tpu_custom_call" | custom-call | flops 5750000128 | tf_op jit(solution)/shard_map/leaf_up/pallas_call | solution.py:342
  5.3 5.2 %all-to-all-start = ((bf16[8,16,512]{2,1,0:T(8,128)(2,1)}), bf16[8,16,512]{2,1,0:T(8,128)(2,1)S(1)}, u32[]{:S(2)}, u32[]{:S(2)}) async-start(bf16[8,16,512]{2,1,0:T(8,128)(2,1)} %leaf_up.1), calls=%async_computation | async-start | bytes 262144 | tf_op jit(solution)/shard_map/all_to_all | solution.py:358
  10.7 0.1 dynamic-slice_multiply_fusion
  10.9 0.1 reshape.31.offset_hbm
  11.0 0.1 reshape.30.source_hbm
  11.1 0.1 tables.1
  11.2 4.9 %all-to-all-done.mid_ref.values_ref = bf16[8,16,512]{2,1,0:T(8,128)(2,1)S(1)} async-done(((bf16[8,16,512]{2,1,0:T(8,128)(2,1)}), bf16[8,16,512]{2,1,0:T(8,128)(2,1)S(1)}, u32[]{:S(2)}, u32[]{:S(2)}) %all-to-all-start) | async-done | bytes 131104 | tf_op jit(solution)/shard_map/all_to_all | solution.py:358
  16.1 0.6 %top_up.1 = (bf16[16,512]{1,0:T(8,128)(2,1)S(1)}, bf16[16,512]{1,0:T(8,128)(2,1)S(1)}, bf16[16,512]{1,0:T(8,128)(2,1)S(1)}, bf16[16,512]{1,0:T(8,128)(2,1)S(1)}) custom-call(bf16[8,16,512]{2,1,0:T(8,128)(2,1)S(1)} %all-to-all-done.mid_ref.values_ref, bf16[1,512,2048]{2,1,0:T(8,128)(2,1)S(1)} %copy-done, f32[8,2048]{1,0:T(8,128)S(1)} %get-tuple-element.24.cos_ref, ...), custom_call_target="tpu_custom_call" | custom-call | flops 4600000000 | tf_op jit(solution)/shard_map/top_up/pallas_call | solution.py:381
  16.7 1.6 %collective-permute-start.2 = (bf16[16,512]{1,0:T(8,128)(2,1)S(1)}, bf16[16,512]{1,0:T(8,128)(2,1)S(1)}, u32[]{:S(2)}, u32[]{:S(2)}) collective-permute-start(bf16[16,512]{1,0:T(8,128)(2,1)S(1)} %get-tuple-element.32), channel_id=1, source_target_pairs={{0,8},{8,0},{16,24},{24,16},{1,9},{9,1},{17,25},{25,17},{2,10},{10... | collective-permute-start | bytes 49160 | tf_op jit(solution)/shard_map/ppermute | solution.py:280
  18.4 2.6 %collective-permute-start.3 = (bf16[16,512]{1,0:T(8,128)(2,1)S(1)}, bf16[16,512]{1,0:T(8,128)(2,1)S(1)}, u32[]{:S(2)}, u32[]{:S(2)}) collective-permute-start(bf16[16,512]{1,0:T(8,128)(2,1)S(1)} %get-tuple-element.33), channel_id=1, source_target_pairs={{0,16},{8,24},{16,0},{24,8},{1,17},{9,25},{17,1},{25,9},{2,18},{10... | collective-permute-start | bytes 49160 | tf_op jit(solution)/shard_map/ppermute | solution.py:280
  20.9 0.2 collective-permute-start.4
  21.2 1.7 %collective-permute-start.1 = (bf16[8,16,512]{2,1,0:T(8,128)(2,1)S(1)}, bf16[8,16,512]{2,1,0:T(8,128)(2,1)S(1)}, u32[]{:S(2)}, u32[]{:S(2)}) collective-permute-start(bf16[8,16,512]{2,1,0:T(8,128)(2,1)S(1)} %pass_on.2.rest_0_), channel_id=1, source_target_pairs={{0,16},{8,24},{16,0},{24,8},{1,17},{9,25},{17,1},{25,9},{2,18},{10... | collective-permute-start | bytes 393224 | tf_op jit(solution)/shard_map/ppermute | solution.py:280
  22.9 2.5 %collective-permute-start = (bf16[8,16,512]{2,1,0:T(8,128)(2,1)S(1)}, bf16[8,16,512]{2,1,0:T(8,128)(2,1)S(1)}, u32[]{:S(2)}, u32[]{:S(2)}) collective-permute-start(bf16[8,16,512]{2,1,0:T(8,128)(2,1)S(1)} %pass_on.2.rest_0_), channel_id=1, source_target_pairs={{0,8},{8,0},{16,24},{24,16},{1,9},{9,1},{17,25},{25,17},{2,10},{10... | collective-permute-start | bytes 393224 | tf_op jit(solution)/shard_map/ppermute | solution.py:280
  25.4 1.3 %collective-permute-done.4.rest_3_ = bf16[16,512]{1,0:T(8,128)(2,1)S(1)} collective-permute-done((bf16[16,512]{1,0:T(8,128)(2,1)S(1)}, bf16[16,512]{1,0:T(8,128)(2,1)S(1)}, u32[]{:S(2)}, u32[]{:S(2)}) %collective-permute-start.4) | collective-permute-done | bytes 16416 | tf_op jit(solution)/shard_map/ppermute | solution.py:280
  26.7 3.3 %top_translate.1 = (bf16[16,512]{1,0:T(8,128)(2,1)S(1)}, bf16[16,512]{1,0:T(8,128)(2,1)S(1)}, bf16[16,512]{1,0:T(8,128)(2,1)S(1)}, bf16[16,512]{1,0:T(8,128)(2,1)S(1)}) custom-call(s32[2048]{0:T(1024)S(1)} %reshape.28.source_hbm, s32[2048]{0:T(1024)S(1)} %reshape.29.offset_hbm, f32[2528,128]{1,0:T(8,128)S(1)} %bitcast.10, ...), custom_call_target="tpu_custom_call" | custom-call | flops 17250000896 | tf_op jit(solution)/shard_map/top_translate/pallas_call | solution.py:397
  30.1 0.2 collective-permute-start.5
  30.3 1.9 %collective-permute-start.6 = (bf16[16,512]{1,0:T(8,128)(2,1)S(1)}, bf16[16,512]{1,0:T(8,128)(2,1)S(1)}, u32[]{:S(2)}, u32[]{:S(2)}) collective-permute-start(bf16[16,512]{1,0:T(8,128)(2,1)S(1)} %get-tuple-element.36), channel_id=1, source_target_pairs={{0,8},{8,0},{16,24},{24,16},{1,9},{9,1},{17,25},{25,17},{2,10},{10... | collective-permute-start | bytes 49160 | tf_op jit(solution)/shard_map/ppermute | solution.py:280
  32.2 0.7 %collective-permute-start.7 = (bf16[16,512]{1,0:T(8,128)(2,1)S(1)}, bf16[16,512]{1,0:T(8,128)(2,1)S(1)}, u32[]{:S(2)}, u32[]{:S(2)}) collective-permute-start(bf16[16,512]{1,0:T(8,128)(2,1)S(1)} %get-tuple-element.37), channel_id=1, source_target_pairs={{0,16},{8,24},{16,0},{24,8},{1,17},{9,25},{17,1},{25,9},{2,18},{10... | collective-permute-start | bytes 49160 | tf_op jit(solution)/shard_map/ppermute | solution.py:280
  32.9 1.8 %collective-permute-start.8 = (bf16[16,512]{1,0:T(8,128)(2,1)S(1)}, bf16[16,512]{1,0:T(8,128)(2,1)S(1)}, u32[]{:S(2)}, u32[]{:S(2)}) collective-permute-start(bf16[16,512]{1,0:T(8,128)(2,1)S(1)} %get-tuple-element.38), channel_id=1, source_target_pairs={{0,24},{8,16},{16,8},{24,0},{1,25},{9,17},{17,9},{25,1},{2,26},{10... | collective-permute-start | bytes 49160 | tf_op jit(solution)/shard_map/ppermute | solution.py:280
  34.7 0.4 collective-permute-done.5.rest_3_
  35.1 6.3 %mid_translate.1.far_ref = f32[2,64,512]{2,1,0:T(8,128)S(1)} custom-call(s32[4096]{0:T(1024)S(1)} %reshape.30.source_hbm, s32[4096]{0:T(1024)S(1)} %reshape.31.offset_hbm, f32[2528,128]{1,0:T(8,128)S(1)} %bitcast.11, bf16[8,16,512]{2,1,0:T(8,128)(2,1)S(1)} %pass_on.2.rest_0_, bf16[8,16,512]{2,1,0:T(8,128)(2,1)S(1)} %collective-permute-done.rest_1_, ...), custom_call_target="tpu_custom_call" | custom-call | flops 1150000000 | tf_op jit(solution)/shard_map/mid_translate/pallas_call | solution.py:422
  41.5 0.9 %top_down.1 = bf16[8,16,512]{2,1,0:T(8,128)(2,1)S(1)} custom-call(bf16[1,512,2048]{2,1,0:T(8,128)(2,1)S(1)} %copy-done, f32[8,2048]{1,0:T(8,128)S(1)} %get-tuple-element.24.cos_ref, f32[8,2048]{1,0:T(8,128)S(1)} %get-tuple-element.25.sin_ref, f32[2,64,512]{2,1,0:T(8,128)S(1)} %mid_translate.1.far_ref, ...), custom_call_target="tpu_custom_call" | custom-call | flops 1150000000 | tf_op jit(solution)/shard_map/top_down/pallas_call | solution.py:440
  42.4 7.9 %all_to_all.10.mid_ref = bf16[8,16,512]{2,1,0:T(8,128)(2,1)S(1)} all-to-all(bf16[8,16,512]{2,1,0:T(8,128)(2,1)S(1)} %top_down.1), channel_id=1, replica_groups=mesh['box'=4,'dir'=8] {'dir'}, dimensions={0} | all-to-all | bytes 262144 | tf_op jit(solution)/shard_map/all_to_all | solution.py:449
  50.3 3.2 %leaf_down.1 = f32[128,1024]{1,0:T(8,128)} custom-call(bf16[8,16,512]{2,1,0:T(8,128)(2,1)S(1)} %all_to_all.10.mid_ref, bf16[1024,4096]{1,0:T(8,128)(2,1)S(1)} %bitcast.9, f32[8,4096]{1,0:T(8,128)S(1)} %copy-done.3), custom_call_target="tpu_custom_call" | custom-call | flops 3449999872 | tf_op jit(solution)/shard_map/leaf_down/pallas_call | solution.py:451
  (38 shorter events, 0.4 us)
Async XLA Ops:
  0.0 10.5 %copy-start.5 = (s32[32,64]{1,0:T(8,128)S(1)}, s32[32,64]{1,0:T(8,128)}, u32[]{:S(2)}) copy-start(s32[32,64]{1,0:T(8,128)} %param.20) | copy-start | bytes 24580
  0.0 10.6 %copy-start.6 = (s32[32,64]{1,0:T(8,128)S(1)}, s32[32,64]{1,0:T(8,128)}, u32[]{:S(2)}) copy-start(s32[32,64]{1,0:T(8,128)} %param.21) | copy-start | bytes 24580
  0.0 10.7 %copy-start.7 = (s32[256,64]{0,1:T(8,128)S(1)}, s32[256,64]{0,1:T(8,128)}, u32[]{:S(2)}) copy-start(s32[256,64]{0,1:T(8,128)} %param.16) | copy-start | bytes 196612
  0.0 10.7 %copy-start.8 = (s32[256,64]{0,1:T(8,128)S(1)}, s32[256,64]{0,1:T(8,128)}, u32[]{:S(2)}) copy-start(s32[256,64]{0,1:T(8,128)} %param.15) | copy-start | bytes 196612
  0.0 11.1 %copy-start.4 = (f32[8,1,2048]{2,1,0:T(1,128)S(1)}, f32[8,1,2048]{2,1,0:T(1,128)}, u32[]{:S(2)}) copy-start(f32[8,1,2048]{2,1,0:T(1,128)} %shift_ref.2) | copy-start | bytes 196612
  5.3 10.8 %all-to-all-start = ((bf16[8,16,512]{2,1,0:T(8,128)(2,1)}), bf16[8,16,512]{2,1,0:T(8,128)(2,1)S(1)}, u32[]{:S(2)}, u32[]{:S(2)}) async-start(bf16[8,16,512]{2,1,0:T(8,128)(2,1)} %leaf_up.1), calls=%async_computation | async-start | bytes 262144 | tf_op jit(solution)/shard_map/all_to_all | solution.py:358
  11.1 5.0 %copy-start = (bf16[1,512,2048]{2,1,0:T(8,128)(2,1)S(1)}, bf16[1,512,2048]{2,1,0:T(8,128)(2,1)}, u32[]{:S(2)}) copy-start(bf16[1,512,2048]{2,1,0:T(8,128)(2,1)} %table_ref.4) | copy-start | bytes 6291460
  16.1 10.7 %copy-start.1 = (f32[2,316,1,512]{3,2,1,0:T(1,128)S(1)}, f32[2,316,1,512]{3,2,1,0:T(1,128)}, u32[]{:S(2)}) copy-start(f32[2,316,1,512]{3,2,1,0:T(1,128)} %param.19) | copy-start | bytes 3883012
  16.1 34.3 %slice-start = ((s8[8388608]{0:T(1024)(128)(4,1)}), s8[4194304]{0:T(1024)(128)(4,1)S(1)}, s32[]{:S(2)}) async-start(s8[8388608]{0:T(1024)(128)(4,1)} %bitcast.8), calls=%async_computation.2 | async-start | bytes 8388608
  16.7 8.7 %collective-permute-start.2 = (bf16[16,512]{1,0:T(8,128)(2,1)S(1)}, bf16[16,512]{1,0:T(8,128)(2,1)S(1)}, u32[]{:S(2)}, u32[]{:S(2)}) collective-permute-start(bf16[16,512]{1,0:T(8,128)(2,1)S(1)} %get-tuple-element.32), channel_id=1, source_target_pairs={{0,8},{8,0},{16,24},{24,16},{1,9},{9,1},{17,25},{25,17},{2,10},{10... | collective-permute-start | bytes 49160 | tf_op jit(solution)/shard_map/ppermute | solution.py:280
  18.4 7.1 %collective-permute-start.3 = (bf16[16,512]{1,0:T(8,128)(2,1)S(1)}, bf16[16,512]{1,0:T(8,128)(2,1)S(1)}, u32[]{:S(2)}, u32[]{:S(2)}) collective-permute-start(bf16[16,512]{1,0:T(8,128)(2,1)S(1)} %get-tuple-element.33), channel_id=1, source_target_pairs={{0,16},{8,24},{16,0},{24,8},{1,17},{9,25},{17,1},{25,9},{2,18},{10... | collective-permute-start | bytes 49160 | tf_op jit(solution)/shard_map/ppermute | solution.py:280
  20.9 5.8 %collective-permute-start.4 = (bf16[16,512]{1,0:T(8,128)(2,1)S(1)}, bf16[16,512]{1,0:T(8,128)(2,1)S(1)}, u32[]{:S(2)}, u32[]{:S(2)}) collective-permute-start(bf16[16,512]{1,0:T(8,128)(2,1)S(1)} %get-tuple-element.34), channel_id=1, source_target_pairs={{0,24},{8,16},{16,8},{24,0},{1,25},{9,17},{17,9},{25,1},{2,26},{10... | collective-permute-start | bytes 49160 | tf_op jit(solution)/shard_map/ppermute | solution.py:280
  21.2 8.9 %collective-permute-start.1 = (bf16[8,16,512]{2,1,0:T(8,128)(2,1)S(1)}, bf16[8,16,512]{2,1,0:T(8,128)(2,1)S(1)}, u32[]{:S(2)}, u32[]{:S(2)}) collective-permute-start(bf16[8,16,512]{2,1,0:T(8,128)(2,1)S(1)} %pass_on.2.rest_0_), channel_id=1, source_target_pairs={{0,16},{8,24},{16,0},{24,8},{1,17},{9,25},{17,1},{25,9},{2,18},{10... | collective-permute-start | bytes 393224 | tf_op jit(solution)/shard_map/ppermute | solution.py:280
  22.9 11.8 %collective-permute-start = (bf16[8,16,512]{2,1,0:T(8,128)(2,1)S(1)}, bf16[8,16,512]{2,1,0:T(8,128)(2,1)S(1)}, u32[]{:S(2)}, u32[]{:S(2)}) collective-permute-start(bf16[8,16,512]{2,1,0:T(8,128)(2,1)S(1)} %pass_on.2.rest_0_), channel_id=1, source_target_pairs={{0,8},{8,0},{16,24},{24,16},{1,9},{9,1},{17,25},{25,17},{2,10},{10... | collective-permute-start | bytes 393224 | tf_op jit(solution)/shard_map/ppermute | solution.py:280
  26.7 8.4 %copy-start.2 = (f32[2,316,512]{2,0,1:T(2,128)S(1)}, f32[2,316,512]{2,0,1:T(2,128)}, u32[]{:S(2)}) copy-start(f32[2,316,512]{2,0,1:T(2,128)} %param.14) | copy-start | bytes 3883012
  26.7 23.6 %slice-start.1 = ((s8[8388608]{0:T(1024)(128)(4,1)}), s8[4194304]{0:T(1024)(128)(4,1)S(1)}, s32[]{:S(2)}) async-start(s8[8388608]{0:T(1024)(128)(4,1)} %bitcast.8), calls=%async_computation.3 | async-start | bytes 8388608
  30.1 5.0 %collective-permute-start.5 = (bf16[8,16,512]{2,1,0:T(8,128)(2,1)S(1)}, bf16[8,16,512]{2,1,0:T(8,128)(2,1)S(1)}, u32[]{:S(2)}, u32[]{:S(2)}) collective-permute-start(bf16[8,16,512]{2,1,0:T(8,128)(2,1)S(1)} %pass_on.3), channel_id=1, source_target_pairs={{0,8},{8,0},{16,24},{24,16},{1,9},{9,1},{17,25},{25,17},{2,10},{10... | collective-permute-start | bytes 393224 | tf_op jit(solution)/shard_map/ppermute | solution.py:280
  30.3 11.2 %collective-permute-start.6 = (bf16[16,512]{1,0:T(8,128)(2,1)S(1)}, bf16[16,512]{1,0:T(8,128)(2,1)S(1)}, u32[]{:S(2)}, u32[]{:S(2)}) collective-permute-start(bf16[16,512]{1,0:T(8,128)(2,1)S(1)} %get-tuple-element.36), channel_id=1, source_target_pairs={{0,8},{8,0},{16,24},{24,16},{1,9},{9,1},{17,25},{25,17},{2,10},{10... | collective-permute-start | bytes 49160 | tf_op jit(solution)/shard_map/ppermute | solution.py:280
  32.2 9.3 %collective-permute-start.7 = (bf16[16,512]{1,0:T(8,128)(2,1)S(1)}, bf16[16,512]{1,0:T(8,128)(2,1)S(1)}, u32[]{:S(2)}, u32[]{:S(2)}) collective-permute-start(bf16[16,512]{1,0:T(8,128)(2,1)S(1)} %get-tuple-element.37), channel_id=1, source_target_pairs={{0,16},{8,24},{16,0},{24,8},{1,17},{9,25},{17,1},{25,9},{2,18},{10... | collective-permute-start | bytes 49160 | tf_op jit(solution)/shard_map/ppermute | solution.py:280
  32.9 8.7 %collective-permute-start.8 = (bf16[16,512]{1,0:T(8,128)(2,1)S(1)}, bf16[16,512]{1,0:T(8,128)(2,1)S(1)}, u32[]{:S(2)}, u32[]{:S(2)}) collective-permute-start(bf16[16,512]{1,0:T(8,128)(2,1)S(1)} %get-tuple-element.38), channel_id=1, source_target_pairs={{0,24},{8,16},{16,8},{24,0},{1,25},{9,17},{17,9},{25,1},{2,26},{10... | collective-permute-start | bytes 49160 | tf_op jit(solution)/shard_map/ppermute | solution.py:280
  41.5 8.8 %copy-start.3 = (f32[8,4096]{1,0:T(8,128)S(1)}, f32[8,4096]{1,0:T(8,128)}, u32[]{:S(2)}) copy-start(f32[8,4096]{1,0:T(8,128)} %shift_ref.3) | copy-start | bytes 393220
